TPU v7x, 32 devices: a whole 2x2x4 slice. The times are simulated.
32 devices in a mesh: grp: 4 (over y, x), seq: 8 (over z, core).
Axes of the slice: x: 2, y: 2, z: 4, core: 2. Of those that a mesh axis runs over, the one named last changes fastest.
Arguments:
- hidden: bfloat16 [4, 1024, 2048], P('grp', 'seq'), may hold values from -6 to 6
- modality: int32 [4, 1024], P('grp', 'seq'), may hold values from 0 to 2, as said below
- starts: int32 [4], P('grp'), may hold values from 32 to 992, as said below
- norm_gain: bfloat16 [2048], P(('grp', 'seq')), may hold values from 0.099609375 to 1.8984375
- in_weight: bfloat16 [2048, 3, 8192], P(('grp', 'seq')), may hold values from -0.125 to 0.125
- conv_weight: bfloat16 [4096, 4], P(('grp', 'seq')), may hold values from -3 to 3
- conv_bias: bfloat16 [4096], P(('grp', 'seq')), may hold values from -3 to 3
- xproj_weight: bfloat16 [4096, 3, 160], P(('grp', 'seq')), may hold values from -0.09375 to 0.09375
- dtproj_weight: bfloat16 [128, 3, 4096], P(('grp', 'seq')), may hold values from -0.5 to 0.5
- step_bias: bfloat16 [4096, 3], P(('grp', 'seq')), may hold values from -11 to -2
- decay_log: bfloat16 [4096, 16], P(('grp', 'seq')), may hold values from 0 to 2.765625
- skip_weight: bfloat16 [4096], P(('grp', 'seq')), may hold values from -4 to 4
- out_weight: bfloat16 [4096, 3, 2048], P(('grp', 'seq')), may hold values from -0.1875 to 0.1875
- cotangent: bfloat16 [4, 1024, 2048], P('grp', 'seq'), may hold values from -6 to 6
Outputs:
- output: bfloat16 [4, 1024, 2048], P('grp', 'seq')
- grad_hidden: float32 [4, 1024, 2048], P('grp', 'seq')
- grad_norm_gain: float32 [2048], P(('grp', 'seq'))
- grad_in_weight: float32 [2048, 3, 8192], P(('grp', 'seq'))
- grad_conv_weight: float32 [4096, 4], P(('grp', 'seq'))
- grad_conv_bias: float32 [4096], P(('grp', 'seq'))
- grad_xproj_weight: float32 [4096, 3, 160], P(('grp', 'seq'))
- grad_dtproj_weight: float32 [128, 3, 4096], P(('grp', 'seq'))
- grad_step_bias: float32 [4096, 3], P(('grp', 'seq'))
- grad_decay_log: float32 [4096, 16], P(('grp', 'seq'))
- grad_skip_weight: float32 [4096], P(('grp', 'seq'))
- grad_out_weight: float32 [4096, 3, 2048], P(('grp', 'seq'))
Inputs may be any that keep to these rules, and one draw needn't show every extreme that they name: Token modality ids; within a group they change only at multiples of 16 positions; every draw has a group that mixes modalities, and some groups may hold modality 0 only. `starts`: A group's first sequence begins at 0 and its second at this position; one of the two has 32 to 64 tokens.
All inputs are finite; a program needn't handle non-finite values.
Results may differ from a plain program's by a relative error of at most 0.011.
Values may be sent and summed in bfloat16 or wider, within the bound.
No kernel may reach another device: no remote copies, remote signals or barrier semaphores. Data moves between devices by JAX's collectives and lax.ppermute only.
A program may use at most 1.1875 GiB of HBM per device.

v0:
```python
import math

import jax
import jax.numpy as jnp
from jax import lax
from jax.sharding import PartitionSpec as P

EPS = 1e-05


def from_behind(x, axis, by):
    length = lax.axis_size(axis)
    pairs = [(i, i + by) for i in range(length) if 0 <= i + by < length]
    return lax.ppermute(x, axis, pairs)


def prefix(x, axis, join, neutral):
    place = lax.axis_index(axis)
    gathered = jax.tree.map(
        lambda a, kind: lax.all_gather(a.astype(kind), axis), x, (jnp.bfloat16, jnp.bfloat16)
    )
    state = jax.tree.map(lambda a, e: jnp.zeros_like(a) + jnp.asarray(e, a.dtype), x, neutral)

    def one(lap, state):
        return join(
            state,
            jax.tree.map(
                lambda a, own: lax.dynamic_index_in_dim(a, lap, 0, False).astype(own.dtype),
                gathered,
                x,
            ),
        )

    return lax.fori_loop(0, place, one, state)


def prefix_2(value, axis, join, neutral):
    count, mine = (lax.axis_size(axis), lax.axis_index(axis))
    pieces = jax.tree.map(lambda part: lax.all_gather(part, axis), value)
    pieces = jax.tree.map(lambda part: part[::-1], pieces)
    mine = count - 1 - mine
    so_far = jax.tree.map(
        lambda part, zero: jnp.full_like(part, 0) + jnp.asarray(zero, part.dtype), value, neutral
    )

    def lap(position, so_far):
        longer = join(so_far, jax.tree.map(lambda part: part[position], pieces))
        return jax.tree.map(lambda new, old: jnp.where(position < mine, new, old), longer, so_far)

    return lax.fori_loop(0, count - 1, lap, so_far)


def as_sent(x):

    def short(part):
        return part.astype(jnp.bfloat16) if part.dtype == jnp.float32 else part

    return jax.tree.map(short, x)


def silu_slope(values):
    sigmoid_part = jax.nn.sigmoid(values)
    return sigmoid_part * (1.0 + values * (1.0 - sigmoid_part))


def mode_split(values, low_masks):
    return values[:, None, :] * low_masks[:, :, None]


def shape_blocks(values, block_len):
    return values.reshape((values.shape[0] // block_len, block_len) + values.shape[1:])


def local_states(decay_rate, step_size, in_select, activated, keep_mask):

    def one_token(token_state, token_items):
        step_row, select_row, act_row, keep_row = token_items
        new_state = (
            keep_row * jnp.exp(step_row[:, None] * decay_rate) * token_state
            + (step_row * act_row)[:, None] * select_row[None, :]
        )
        return (new_state, token_state)

    zero_state = jnp.zeros(decay_rate.shape, jnp.float32)
    return lax.scan(one_token, zero_state, (step_size, in_select, activated, keep_mask))


def local_grads(decay_rate, step_size, out_select, keep_mask, grad_read):

    def one_token(grad_state, token_items):
        step_row, read_row, keep_row, grad_row = token_items
        grad_here = grad_state + grad_row[:, None] * read_row[None, :]
        return (keep_row * jnp.exp(step_row[:, None] * decay_rate) * grad_here, grad_here)

    zero_state = jnp.zeros(decay_rate.shape, jnp.float32)
    return lax.scan(
        one_token, zero_state, (step_size, out_select, keep_mask, grad_read), reverse=True
    )


def read_blocks(entry_state, decay_rate, items, block_len):

    def read_one_block(block_items):
        (
            prior_block,
            step_block,
            insel_block,
            outsel_block,
            act_block,
            keep_block,
            sum_block,
            clear_block,
        ) = block_items
        fade_block = keep_block[:, None, None] * jnp.exp(step_block[:, :, None] * decay_rate[None])
        states_full = (
            fade_block * prior_block
            + (step_block * act_block)[:, :, None] * insel_block[:, None, :]
        )
        states_full = (
            states_full
            + clear_block[:, None, None]
            * jnp.exp(sum_block[:, :, None] * decay_rate[None])
            * entry_state[None]
        )
        return jnp.sum(states_full * outsel_block[:, None, :], axis=2)

    result = lax.map(read_one_block, tuple((shape_blocks(values, block_len) for values in items)))
    return result.reshape(-1, result.shape[-1])


def back_blocks(entry_state, exit_grad, decay_rate, items, block_len):

    def back_one_block(rate_sum, block_items):
        (
            prior_block,
            step_block,
            insel_block,
            outsel_block,
            act_block,
            keep_block,
            gread_block,
            glocal_block,
            excl_block,
            cexcl_block,
            after_block,
            cafter_block,
        ) = block_items
        fade_block = keep_block[:, None, None] * jnp.exp(step_block[:, :, None] * decay_rate[None])
        prior_full = (
            prior_block
            + cexcl_block[:, None, None]
            * jnp.exp(excl_block[:, :, None] * decay_rate[None])
            * entry_state[None]
        )
        states_full = (
            fade_block * prior_full + (step_block * act_block)[:, :, None] * insel_block[:, None, :]
        )
        grad_full = (
            glocal_block
            + cafter_block[:, None, None]
            * jnp.exp(after_block[:, :, None] * decay_rate[None])
            * exit_grad[None]
        )
        grad_outsel = jnp.sum(gread_block[:, :, None] * states_full, axis=1)
        weighted = jnp.sum(grad_full * insel_block[:, None, :], axis=2)
        decay_part = grad_full * fade_block * prior_full
        grad_step_row = act_block * weighted + jnp.sum(decay_part * decay_rate[None], axis=2)
        grad_act_row = step_block * weighted
        grad_insel = jnp.sum(grad_full * (step_block * act_block)[:, :, None], axis=1)
        rate_sum = rate_sum + jnp.sum(decay_part * step_block[:, :, None], axis=0)
        return (rate_sum, (grad_step_row, grad_act_row, grad_insel, grad_outsel))

    zero_state = jnp.zeros(decay_rate.shape, jnp.float32)
    grad_rate, (grad_steps, grad_acts, grad_insels, grad_outsels) = lax.scan(
        back_one_block, zero_state, tuple((shape_blocks(values, block_len) for values in items))
    )
    return (
        grad_steps.reshape(-1, grad_steps.shape[-1]),
        grad_acts.reshape(-1, grad_acts.shape[-1]),
        grad_insels.reshape(-1, grad_insels.shape[-1]),
        grad_outsels.reshape(-1, grad_outsels.shape[-1]),
        grad_rate,
    )


def on_device(
    hidden,
    modality,
    starts,
    norm_gain,
    in_weight,
    conv_weight,
    conv_bias,
    xproj_weight,
    dtproj_weight,
    step_bias,
    decay_log,
    skip_weight,
    out_weight,
    cotangent,
):
    gathered = (
        lax.all_gather(norm_gain, ("grp", "seq"), axis=0, tiled=True),
        lax.all_gather(in_weight, ("grp", "seq"), axis=0, tiled=True),
        lax.all_gather(conv_weight, ("grp", "seq"), axis=0, tiled=True),
        lax.all_gather(conv_bias, ("grp", "seq"), axis=0, tiled=True),
        lax.all_gather(xproj_weight, ("grp", "seq"), axis=0, tiled=True),
        lax.all_gather(dtproj_weight, ("grp", "seq"), axis=0, tiled=True),
        lax.all_gather(step_bias, ("grp", "seq"), axis=0, tiled=True),
        lax.all_gather(decay_log, ("grp", "seq"), axis=0, tiled=True),
        lax.all_gather(skip_weight, ("grp", "seq"), axis=0, tiled=True),
        lax.all_gather(out_weight, ("grp", "seq"), axis=0, tiled=True),
    )
    (
        gain_whole,
        in_whole,
        convw_whole,
        convb_whole,
        xproj_whole,
        delta_projection_full,
        bias_whole,
        decay_whole,
        skip_whole,
        out_whole,
    ) = gathered
    tokens = hidden[0].astype(jnp.float32)
    mode_ids = modality[0]
    row_total = tokens.shape[0]
    inner_width = convw_whole.shape[0]
    rank_width = delta_projection_full.shape[0]
    states = decay_whole.shape[1]
    mode_count = in_whole.shape[1]
    block_len = math.gcd(row_total, 16)
    seq_index = lax.axis_index("seq")
    position = seq_index * row_total + jnp.arange(row_total, dtype=jnp.int32)
    second_start = starts[0]
    seq_begin = jnp.where(position >= second_start, second_start, 0)
    keep_mask = 1.0 - ((position == 0) | (position == second_start)).astype(jnp.float32)
    mode_masks = (mode_ids[:, None] == jnp.arange(mode_count, dtype=jnp.int32)[None, :]).astype(
        jnp.float32
    )
    low_masks = mode_masks.astype(jnp.bfloat16)
    decay_rate = -jnp.exp(decay_whole.astype(jnp.float32))
    gain_value = gain_whole.astype(jnp.float32)
    convw_value = convw_whole.astype(jnp.float32)
    convb_value = convb_whole.astype(jnp.float32)
    bias_value = bias_whole.astype(jnp.float32)
    skip_value = skip_whole.astype(jnp.float32)
    zero_state = jnp.zeros(decay_rate.shape, jnp.float32)
    one_state = jnp.ones(decay_rate.shape, jnp.float32)
    norm_scale = lax.rsqrt(jnp.mean(tokens * tokens, axis=1, keepdims=True) + EPS)
    normed = (tokens * norm_scale * gain_value).astype(jnp.bfloat16)
    normed_modes = mode_split(normed, low_masks)
    projected = jnp.einsum(
        "lmd,dmk->lk", normed_modes, in_whole, preferred_element_type=jnp.float32
    )
    conv_in = projected[:, :inner_width]
    gate_in = projected[:, inner_width:]
    left_rim = from_behind(conv_in[-3:], "seq", 1)
    extended = jnp.concatenate([left_rim, conv_in], axis=0)
    tap_masks = [
        (position - 3 + tap_index >= seq_begin).astype(jnp.float32)[:, None]
        for tap_index in range(4)
    ]
    pre_act = convb_value + sum(
        (
            convw_value[:, tap_index]
            * extended[tap_index : tap_index + row_total]
            * tap_masks[tap_index]
            for tap_index in range(4)
        )
    )
    activated = jax.nn.silu(pre_act)
    act_modes = mode_split(activated.astype(jnp.bfloat16), low_masks)
    xproj_out = jnp.einsum(
        "lmc,cmk->lk", act_modes, xproj_whole, preferred_element_type=jnp.float32
    )
    rank_per_modality = mode_split(xproj_out[:, :rank_width].astype(jnp.bfloat16), low_masks)
    in_select = xproj_out[:, rank_width : rank_width + states]
    out_select = xproj_out[:, rank_width + states :]
    step_pre = jnp.einsum(
        "uds,sdp->up", rank_per_modality, delta_projection_full, preferred_element_type=jnp.float32
    ) + jnp.dot(mode_masks, bias_value.T, precision=lax.Precision.HIGHEST)
    step_size = jax.nn.softplus(step_pre)
    sum_incl = jnp.cumsum(step_size, axis=0)
    zero_row = jnp.zeros((1, inner_width), jnp.float32)
    sum_excl = jnp.concatenate([zero_row, sum_incl[:-1]], axis=0)
    sum_rev = jnp.cumsum(step_size[::-1], axis=0)[::-1]
    sum_after = jnp.concatenate([sum_rev[1:], zero_row], axis=0)
    clear_incl = jnp.cumprod(keep_mask)
    one_entry = jnp.ones((1,), jnp.float32)
    clear_excl = jnp.concatenate([one_entry, clear_incl[:-1]], axis=0)
    clear_rev = jnp.cumprod(keep_mask[::-1])[::-1]
    clear_after = jnp.concatenate([clear_rev[1:], one_entry], axis=0)
    local_state, prior_local = local_states(decay_rate, step_size, in_select, activated, keep_mask)
    cumulative_decay = jnp.exp(decay_rate * jnp.sum(step_size, axis=0)[:, None]) * jnp.prod(
        keep_mask
    )

    def link(earlier, later_part):
        return (earlier[0] * later_part[0], later_part[0] * earlier[1] + later_part[1])

    _, entry_state = prefix((cumulative_decay, local_state), "seq", link, (one_state, zero_state))
    readout_value = read_blocks(
        entry_state,
        decay_rate,
        (prior_local, step_size, in_select, out_select, activated, keep_mask, sum_incl, clear_incl),
        block_len,
    )
    readout_value = readout_value + skip_value * activated
    gate_act = jax.nn.silu(gate_in)
    gated_modes = mode_split((readout_value * gate_act).astype(jnp.bfloat16), low_masks)
    branch_out = jnp.einsum(
        "lmc,cmd->ld", gated_modes, out_whole, preferred_element_type=jnp.float32
    )
    output = (tokens + branch_out).astype(jnp.bfloat16)[None]
    back_weights = (
        lax.all_gather(norm_gain, ("grp", "seq"), axis=0, tiled=True),
        lax.all_gather(in_weight, ("grp", "seq"), axis=0, tiled=True),
        lax.all_gather(conv_weight, ("grp", "seq"), axis=0, tiled=True),
        lax.all_gather(conv_bias, ("grp", "seq"), axis=0, tiled=True),
        lax.all_gather(xproj_weight, ("grp", "seq"), axis=0, tiled=True),
        lax.all_gather(dtproj_weight, ("grp", "seq"), axis=0, tiled=True),
        lax.all_gather(step_bias, ("grp", "seq"), axis=0, tiled=True),
        lax.all_gather(decay_log, ("grp", "seq"), axis=0, tiled=True),
        lax.all_gather(skip_weight, ("grp", "seq"), axis=0, tiled=True),
        lax.all_gather(out_weight, ("grp", "seq"), axis=0, tiled=True),
    )
    back_in = back_weights[1]
    back_xproj = back_weights[4]
    back_dtproj = back_weights[5]
    back_out = back_weights[9]
    grad_out = cotangent[0].astype(jnp.float32)
    grad_modes = mode_split(cotangent[0], low_masks)
    grad_out_weight = jnp.einsum(
        "lmc,ld->cmd", gated_modes, cotangent[0], preferred_element_type=jnp.float32
    )
    grad_gated = jnp.einsum("lmd,cmd->lc", grad_modes, back_out, preferred_element_type=jnp.float32)
    grad_read = grad_gated * gate_act
    grad_gate = grad_gated * readout_value * silu_slope(gate_in)
    grad_skip = jnp.sum(grad_read * activated, axis=0)
    carried, grad_local = local_grads(decay_rate, step_size, out_select, keep_mask, grad_read)

    def link_back(earlier, later_part):
        return (later_part[0] * earlier[0], later_part[1] + later_part[0] * earlier[1])

    _, exit_grad = prefix_2((cumulative_decay, carried), "seq", link_back, (one_state, zero_state))
    grad_steps, state_act, grad_insel, grad_outsel, grad_rate = back_blocks(
        entry_state,
        exit_grad,
        decay_rate,
        (
            prior_local,
            step_size,
            in_select,
            out_select,
            activated,
            keep_mask,
            grad_read,
            grad_local,
            sum_excl,
            clear_excl,
            sum_after,
            clear_after,
        ),
        block_len,
    )
    grad_act = state_act + skip_value * grad_read
    grad_pre = grad_steps * jax.nn.sigmoid(step_pre)
    grad_step_bias = jnp.dot(grad_pre.T, mode_masks, precision=lax.Precision.HIGHEST)
    reduced_rank_input = grad_pre.astype(jnp.bfloat16)
    gradient_delta_projection = jnp.einsum(
        "xna,xi->ani", rank_per_modality, reduced_rank_input, preferred_element_type=jnp.float32
    )
    grad_rank = jnp.einsum(
        "lmc,rmc->lr",
        mode_split(reduced_rank_input, low_masks),
        back_dtproj,
        preferred_element_type=jnp.float32,
    )
    xproj_grad = jnp.concatenate([grad_rank, grad_insel, grad_outsel], axis=1).astype(jnp.bfloat16)
    grad_xproj = jnp.einsum(
        "lmc,lk->cmk", act_modes, xproj_grad, preferred_element_type=jnp.float32
    )
    grad_act = grad_act + jnp.einsum(
        "lmk,cmk->lc",
        mode_split(xproj_grad, low_masks),
        back_xproj,
        preferred_element_type=jnp.float32,
    )
    grad_pre_act = grad_act * silu_slope(pre_act)
    grad_conv_bias = jnp.sum(grad_pre_act, axis=0)
    grad_conv_weight = jnp.stack(
        [
            jnp.sum(
                grad_pre_act * extended[tap_index : tap_index + row_total] * tap_masks[tap_index],
                axis=0,
            )
            for tap_index in range(4)
        ],
        axis=1,
    )
    grad_extended = sum(
        (
            jnp.pad(
                grad_pre_act * convw_value[:, tap_index] * tap_masks[tap_index],
                ((tap_index, 3 - tap_index), (0, 0)),
            )
            for tap_index in range(4)
        )
    )
    from_right = from_behind(as_sent(grad_extended[:3]), "seq", -1)
    grad_conv_in = grad_extended[3:] + jnp.pad(from_right, ((row_total - 3, 0), (0, 0)))
    proj_grad = jnp.concatenate([grad_conv_in, grad_gate], axis=1).astype(jnp.bfloat16)
    grad_normed = jnp.einsum(
        "lmk,dmk->ld", mode_split(proj_grad, low_masks), back_in, preferred_element_type=jnp.float32
    )
    unit_tokens = tokens * norm_scale
    grad_norm_gain = jnp.sum(grad_normed * unit_tokens, axis=0)
    scaled_grad = grad_normed * gain_value
    grad_hidden = grad_out + norm_scale * (
        scaled_grad - unit_tokens * jnp.mean(scaled_grad * unit_tokens, axis=1, keepdims=True)
    )
    grad_decay_log = grad_rate * decay_rate
    grad_in_weight = lax.psum_scatter(
        jnp.einsum("lmd,lk->dmk", normed_modes, proj_grad, preferred_element_type=jnp.float32),
        ("grp", "seq"),
        scatter_dimension=0,
        tiled=True,
    )
    summed = (
        lax.psum_scatter(grad_norm_gain, ("grp", "seq"), scatter_dimension=0, tiled=True),
        lax.psum_scatter(grad_conv_weight, ("grp", "seq"), scatter_dimension=0, tiled=True),
        lax.psum_scatter(grad_conv_bias, ("grp", "seq"), scatter_dimension=0, tiled=True),
        lax.psum_scatter(grad_xproj, ("grp", "seq"), scatter_dimension=0, tiled=True),
        lax.psum_scatter(
            gradient_delta_projection, ("grp", "seq"), scatter_dimension=0, tiled=True
        ),
        lax.psum_scatter(grad_step_bias, ("grp", "seq"), scatter_dimension=0, tiled=True),
        lax.psum_scatter(grad_decay_log, ("grp", "seq"), scatter_dimension=0, tiled=True),
        lax.psum_scatter(grad_skip, ("grp", "seq"), scatter_dimension=0, tiled=True),
        lax.psum_scatter(grad_out_weight, ("grp", "seq"), scatter_dimension=0, tiled=True),
    )
    return (
        output,
        grad_hidden[None],
        summed[0],
        grad_in_weight,
        summed[1],
        summed[2],
        summed[3],
        summed[4],
        summed[5],
        summed[6],
        summed[7],
        summed[8],
    )


def solution(mesh):
    return jax.shard_map(
        on_device,
        mesh=mesh,
        in_specs=(
            P("grp", "seq", None),
            P("grp", "seq"),
            P("grp"),
            P(("grp", "seq")),
            P(("grp", "seq"), None, None),
            P(("grp", "seq"), None),
            P(("grp", "seq")),
            P(("grp", "seq"), None, None),
            P(("grp", "seq"), None, None),
            P(("grp", "seq"), None),
            P(("grp", "seq"), None),
            P(("grp", "seq")),
            P(("grp", "seq"), None, None),
            P("grp", "seq", None),
        ),
        out_specs=(
            P("grp", "seq", None),
            P("grp", "seq", None),
            P(("grp", "seq")),
            P(("grp", "seq"), None, None),
            P(("grp", "seq"), None),
            P(("grp", "seq")),
            P(("grp", "seq"), None, None),
            P(("grp", "seq"), None, None),
            P(("grp", "seq"), None),
            P(("grp", "seq"), None),
            P(("grp", "seq")),
            P(("grp", "seq"), None, None),
        ),
        check_vma=False,
    )
```

profile of v0, /device:TPU:0, one launch (start us, length us, event | category | flops | bytes accessed | tf_op | source)
XLA Modules:
  0.0 7583.4 jit_solution(18280783043783875769)
XLA Ops:
  12.2 46.2 all-reduce.7
  58.4 39.2 all-gather.4
  97.6 37.0 all_gather.59
  134.6 45.5 all_gather.64
  180.4 351.7 %all-gather.15.cloned.1.call-done = bf16[2048,3,8192]{2,0,1:T(8,128)(2,1)} async-done(((bf16[64,3,8192]{2,0,1:T(8,128)(2,1)}), bf16[2048,3,8192]{2,0,1:T(8,128)(2,1)}) %all-gather.15.cloned.1.call-update) | async-done | bytes 100663312 | tf_op jit(solution)/shard_map/all_gather | solution.py:204
  532.1 37.3 convolution_bitcast_fusion.2
  572.5 40.4 all_gather.65
  616.2 194.1 %all-gather.21.cloned.1.call-done = bf16[4096,3,2048]{2,0,1:T(8,128)(2,1)} async-done(((bf16[128,3,2048]{2,0,1:T(8,128)(2,1)}), bf16[4096,3,2048]{2,0,1:T(8,128)(2,1)}) %all-gather.21.cloned.1.call-update) | async-done | bytes 50331664 | tf_op jit(solution)/shard_map/all_gather | solution.py:212
  810.3 29.7 multiply_reduce_fusion.5
  843.5 32.1 all-gather.17.cloned.1.call-done
  879.4 59.9 all-gather.19.cloned.1.call-done
  949.6 11.2 broadcast.205.clone
  960.8 387.6 %while.87 = (s32[]{:T(128)}, f32[4096,16]{0,1:T(8,128)S(1)}, f32[128,4096,16]{1,2,0:T(8,128)}, f32[128]{0:T(128)S(1)}, f32[128,4096]{1,0:T(8,128)S(1)}, /*index=...) while((s32[]{:T(128)}, f32[4096,16]{0,1:T(8,128)S(1)}, ...), condition=%wide.region_2.3_spmd.clone, body=%wide.region_1.2_spmd.clone.sunk | while | flops 462851 | bytes 1458516 | solution.py:85
  1349.3 39.5 all-gather.5
  1392.1 11.3 broadcast.205.clone.1
  1403.4 395.3 %while.88 = (s32[]{:T(128)}, f32[4096,16]{0,1:T(8,128)S(1)}, f32[128,4096,16]{1,2,0:T(8,128)}, f32[128]{0:T(128)S(1)}, f32[128,4096]{1,0:T(8,128)S(1)}, /*index=...) while((s32[]{:T(128)}, f32[4096,16]{0,1:T(8,128)S(1)}, ...), condition=%wide.region_13.14_spmd.clone, body=%wide.region_12.13_spmd.clone.sunk | while | flops 589828 | bytes 1425832 | solution.py:96
  1798.7 10.5 rev.15
  1817.0 16.8 slice.96
  1844.8 67.5 while.86
  1922.7 16.7 rev.16
  1939.4 21.5 while.89
  1964.1 121.9 %while.90 = (s32[]{:T(128)}, f32[4096,16]{0,1:T(8,128)S(1)}, f32[8,16,4096]{2,1,0:T(8,128)}, f32[8,16,4096]{2,1,0:T(8,128)}, bf16[8,16,16]{2,1,0:T(8,128)(2,1)S(...) while((s32[]{:T(128)}, f32[4096,16]{0,1:T(8,128)S(1)}, ...), condition=%wide.region_24.25_spmd.clone, body=%wide.region_18.24_spmd.clone.sunk | while | flops 26410496 | bytes 16536383 | solution.py:174
  2135.1 65.3 convolution_bitcast_fusion
  2200.4 280.4 %copy.96 = f32[2048,3,8192]{2,1,0:T(4,128)} copy(f32[2048,3,8192]{0,2,1:T(8,128)} %convolution_bitcast_fusion) | data formatting | bytes 402653184 | tf_op jit(solution)/shard_map/lmd,lk->dmk/transpose | solution.py:426
  2488.9 37.3 convolution_bitcast_fusion.1
  2527.2 18.9 fusion.41
  2546.9 42.8 fusion.88
  2589.7 45.7 all-reduce.13
  2644.6 3610.0 %all-reduce.17.cloned.1.call-done = f32[2048,3,8192]{2,1,0:T(4,128)} async-done(((f32[2048,3,8192]{2,1,0:T(4,128)}), f32[2048,3,8192]{2,1,0:T(4,128)}) %all-reduce.17.cloned.1.call-update) | async-done | bytes 201326608
  6273.7 117.0 %reduce-scatter.12.cloned.1.call-done = f32[128,16]{0,1:T(8,128)} async-done(((f32[4096,16]{0,1:T(8,128)}), f32[128,16]{0,1:T(8,128)}) %reduce-scatter.12.cloned.1.call-update) | async-done | bytes 8208 | tf_op jit(solution)/shard_map/reduce_scatter | solution.py:440
  6390.7 125.8 %reduce-scatter.10.cloned.1.call-done = f32[128,3,160]{0,2,1:T(8,128)} async-done(((f32[4096,3,160]{0,2,1:T(8,128)}), f32[128,3,160]{0,2,1:T(8,128)}) %reduce-scatter.10.cloned.1.call-update) | async-done | bytes 245776 | tf_op jit(solution)/shard_map/reduce_scatter | solution.py:435
  6516.4 1060.0 %reduce-scatter.14.cloned.1.call-done = f32[128,3,2048]{2,0,1:T(8,128)} async-done(((f32[4096,3,2048]{2,0,1:T(8,128)}), f32[128,3,2048]{2,0,1:T(8,128)}) %reduce-scatter.14.cloned.1.call-update) | async-done | bytes 3145744 | tf_op jit(solution)/shard_map/reduce_scatter | solution.py:442
  (1833 shorter events, 1137.0 us)
Async XLA Ops:
  7.2 524.9 %all-gather.15.cloned.1.call-start = ((), (), s32[]{:S(2)}) async-start(), calls=%async_computation.5 | async-start | bytes 103809024 | tf_op jit(solution)/shard_map/all_gather | solution.py:204
  8.0 802.3 %all-gather.21.cloned.1.call-start = ((), (), s32[]{:S(2)}) async-start(), calls=%async_computation.8 | async-start | bytes 51904512 | tf_op jit(solution)/shard_map/all_gather | solution.py:212
  8.7 866.8 %all-gather.17.cloned.1.call-start = ((), (), s32[]{:S(2)}) async-start(), calls=%async_computation.6 | async-start | bytes 4055040 | tf_op jit(solution)/shard_map/all_gather | solution.py:207
  9.5 929.9 %all-gather.19.cloned.1.call-start = ((), (), s32[]{:S(2)}) async-start(), calls=%async_computation.7 | async-start | bytes 4325376 | tf_op jit(solution)/shard_map/all_gather | solution.py:208
  10.3 1828.3 %all-gather.23.cloned.1.call-start = ((), (), s32[]{:S(2)}) async-start(), calls=%async_computation.12 | async-start | bytes 1179648 | tf_op jit(solution)/shard_map/all_gather | solution.py:20
  11.2 558.2 %copy-start.47 = (f32[128]{0:T(128)}, f32[128]{0:T(128)S(1)}, u32[]{:S(2)}) copy-start(f32[128]{0:T(128)S(1)} %add_rsqrt_fusion) | copy-start | bytes 1540
  11.3 2123.8 %copy-start.22 = (bf16[128,3]{0,1:T(4,128)(2,1)}, bf16[128,3]{0,1:T(4,128)(2,1)S(1)}, u32[]{:S(2)}) copy-start(bf16[128,3]{0,1:T(4,128)(2,1)S(1)} %convert_convert_fusion) | copy-start | bytes 2308
  11.9 798.3 %copy-start.52 = (f32[128]{0:T(128)}, f32[128]{0:T(128)S(1)}, u32[]{:S(2)}) copy-start(f32[128]{0:T(128)S(1)} %get-tuple-element.1061) | copy-start | bytes 1540
  11.9 798.3 %copy-start.54 = (f32[128]{0:T(128)}, f32[128]{0:T(128)S(1)}, u32[]{:S(2)}) copy-start(f32[128]{0:T(128)S(1)} %get-tuple-element.1062) | copy-start | bytes 1540
  11.9 798.3 %copy-start.56 = (f32[128]{0:T(128)}, f32[128]{0:T(128)S(1)}, u32[]{:S(2)}) copy-start(f32[128]{0:T(128)S(1)} %get-tuple-element.1059) | copy-start | bytes 1540
  12.0 798.3 %copy-start.58 = (f32[128]{0:T(128)}, f32[128]{0:T(128)S(1)}, u32[]{:S(2)}) copy-start(f32[128]{0:T(128)S(1)} %get-tuple-element.1060) | copy-start | bytes 1540
  58.4 511.0 %copy-start.28 = (f32[2048]{0:T(1024)}, f32[2048]{0:T(1024)S(1)}, u32[]{:S(2)}) copy-start(f32[2048]{0:T(1024)S(1)} %convert_element_type.155) | copy-start | bytes 24580
  180.1 630.2 %copy-start.33 = (f32[4096,1]{0,1:T(1,128)}, f32[4096,1]{0,1:T(1,128)S(1)}, u32[]{:S(2)}) copy-start(f32[4096,1]{0,1:T(1,128)S(1)} %get-tuple-element.1052) | copy-start | bytes 49156
  180.1 630.2 %copy-start.35 = (f32[4096,1]{0,1:T(1,128)}, f32[4096,1]{0,1:T(1,128)S(1)}, u32[]{:S(2)}) copy-start(f32[4096,1]{0,1:T(1,128)S(1)} %get-tuple-element.1053) | copy-start | bytes 49156
  180.1 630.2 %copy-start.37 = (f32[4096,1]{0,1:T(1,128)}, f32[4096,1]{0,1:T(1,128)S(1)}, u32[]{:S(2)}) copy-start(f32[4096,1]{0,1:T(1,128)S(1)} %get-tuple-element.1054) | copy-start | bytes 49156
  180.3 389.1 %copy-start.1 = (bf16[128,2048]{1,0:T(8,128)(2,1)}, bf16[128,2048]{1,0:T(8,128)(2,1)S(1)}, u32[]{:S(2)}) copy-start(bf16[128,2048]{1,0:T(8,128)(2,1)S(1)} %fusion.82) | copy-start | bytes 1572868
  180.4 392.2 %copy-start.49 = (bf16[128,16]{0,1:T(8,128)(2,1)S(1)}, bf16[128,16]{0,1:T(8,128)(2,1)}, u32[]{:S(2)}) copy-start(bf16[128,16]{0,1:T(8,128)(2,1)} %param.36) | copy-start | bytes 12292
  570.3 239.9 %collective-permute-start = (f32[3,4096]{1,0:T(4,128)S(1)}, f32[3,4096]{1,0:T(4,128)S(1)}, u32[]{:S(2)}, u32[]{:S(2)}) collective-permute-start(f32[3,4096]{1,0:T(4,128)S(1)} %slice.103), channel_id=1, source_target_pairs={{0,1},{1,2},{2,3},{3,4},{4,5},{5,6},{6,7},{8,9},{9,10},{10,11},{11... | collective-permute-start | bytes 147464 | tf_op jit(solution)/shard_map/ppermute | solution.py:14
  612.9 335.1 %copy-start.24 = (bf16[4096,16]{0,1:T(8,128)(2,1)}, bf16[4096,16]{0,1:T(8,128)(2,1)S(1)}, u32[]{:S(2)}) copy-start(bf16[4096,16]{0,1:T(8,128)(2,1)S(1)} %all_gather.65) | copy-start | bytes 393220
  612.9 197.4 %copy-start.19 = (bf16[1,128,2048]{2,1,0:T(8,128)(2,1)S(1)}, bf16[1,128,2048]{2,1,0:T(8,128)(2,1)}, u32[]{:S(2)}) copy-start(bf16[1,128,2048]{2,1,0:T(8,128)(2,1)} %param.39) | copy-start | bytes 1572868
  949.5 891.4 %all-gather.25.cloned.1.call-start = ((), (), s32[]{:S(2)}) async-start(), calls=%async_computation.13 | async-start | bytes 1179648 | tf_op jit(solution)/shard_map/all_gather | solution.py:20
  960.8 388.5 %copy-start.63 = (bf16[128]{0:T(256)(128)(2,1)S(1)}, bf16[128]{0:T(256)(128)(2,1)}, u32[]{:S(2)}) copy-start(bf16[128]{0:T(256)(128)(2,1)} %param.37) | copy-start | bytes 772
  1349.1 563.2 %all-gather.29.cloned.1.call-start = ((), (), s32[]{:S(2)}) async-start(), calls=%async_computation.15 | async-start | bytes 2359296 | tf_op jit(solution)/shard_map/all_gather | solution.py:39
  1392.0 526.6 %all-gather.27.cloned.1.call-start = ((), (), s32[]{:S(2)}) async-start(), calls=%async_computation.14 | async-start | bytes 2359296 | tf_op jit(solution)/shard_map/all_gather | solution.py:39
  1838.5 801.3 %reduce-scatter.18.cloned.1.call-start = ((), (), s32[]{:S(2)}) async-start(), calls=%async_computation.17 | async-start | bytes 2162688
  2092.2 549.1 %reduce-scatter.16.cloned.1.call-start = ((), (), s32[]{:S(2)}) async-start(), calls=%async_computation.16 | async-start | bytes 2162688
  2118.0 15.0 collective-permute-start.1
  2119.4 523.5 %all-reduce.19.cloned.1.call-start = ((), (), s32[]{:S(2)}) async-start(), calls=%async_computation.19 | async-start | bytes 16777216
  2132.8 4121.9 %all-reduce.17.cloned.1.call-start = ((), (), s32[]{:S(2)}) async-start(), calls=%async_computation.18 | async-start | bytes 536870912
  2480.9 3909.8 %reduce-scatter.12.cloned.1.call-start = ((), (), s32[]{:S(2)}) async-start(), calls=%async_computation.10 | async-start | bytes 270336 | tf_op jit(solution)/shard_map/reduce_scatter | solution.py:440
  2482.5 4033.9 %reduce-scatter.10.cloned.1.call-start = ((), (), s32[]{:S(2)}) async-start(), calls=%async_computation.9 | async-start | bytes 8110080 | tf_op jit(solution)/shard_map/reduce_scatter | solution.py:435
  2487.0 5089.5 %reduce-scatter.14.cloned.1.call-start = ((), (), s32[]{:S(2)}) async-start(), calls=%async_computation.11 | async-start | bytes 103809024 | tf_op jit(solution)/shard_map/reduce_scatter | solution.py:442
  (54 other events, 741.7 us)
Sparse Core Ops, SparseCore 0:
  11.1 520.9 all-gather.14
  535.1 275.1 all-gather.20
  813.1 62.3 all-gather.16
  879.0 60.2 all-gather.18
  949.7 20.6 all-gather.22
  1349.3 20.7 all-gather.24
  1392.1 26.1 all-gather.28
  1838.6 26.1 all-gather.26
  2092.4 139.8 reduce-scatter.17
  2234.5 132.9 reduce-scatter.15
  2373.1 175.5 all-reduce.18
  2555.0 3699.5 all-reduce.16
  6257.4 133.2 reduce-scatter.11
  6397.7 118.6 reduce-scatter.9
  6519.2 1057.2 reduce-scatter.13
where the time goes:
time: 7610 us; the launch traced here: 7580 us
  waiting for transfers between devices  5550 us (73%)
  local copies, waits for them, and re-layouts  881 us (12%)
  other arithmetic  558 us (7%)
  blocking collectives  293 us (4%)
  matrix products  269 us (4%)
    unnamed x19, waiting for transfers between devices  3610 us
    reduce_scatter x1, waiting for transfers between devices, on_device(): lax.psum_scatter(grad_out_weight, ('grp', 'seq'), scatter_dimension=0, ti...  1060 us
    dynamic_slice x512, local copies, waits for them, and re-layouts, local_states(): lax.scan(one_token, zero_state, (step_size, in_select, activated, keep_ma...  388 us
    all_gather x1, waiting for transfers between devices, on_device(): lax.all_gather(in_weight, ('grp', 'seq'), axis=0, tiled=True)  352 us
    transpose x1, local copies, waits for them, and re-layouts, on_device(): jnp.einsum('lmd,lk->dmk', normed_modes, proj_grad, preferred_element_type...  280 us
    dynamic_update_slice x256, other arithmetic, local_states(): lax.scan(one_token, zero_state, (step_size, in_select, activated, keep_ma...  196 us
    all_gather x1, waiting for transfers between devices, on_device(): lax.all_gather(out_weight, ('grp', 'seq'), axis=0, tiled=True)  194 us
  transfers between devices with their start and end apart: 17, of which 8 were waited for; matrix products, arithmetic and copies ran while one was open for 20% of the time, Pallas kernels for 0%

commit v1 on v0

v1 whole, which is shorter than its diff:
```python
import functools
import math

import jax
import jax.numpy as jnp
import numpy as np
from jax import lax
from jax.experimental import pallas as pl
from jax.experimental.pallas import tpu as pltpu
from jax.sharding import PartitionSpec as P

EPS = 1e-05
BF = jnp.bfloat16
F32 = jnp.float32
LOG2E = math.log2(math.e)
RESET = 1e4
VMEM = 48 * 1024 * 1024


def dot(a, b, dims=((1,), (0,))):
    return lax.dot_general(a, b, (dims, ((), ())), preferred_element_type=F32)


def silu_slope(v):
    s = jax.nn.sigmoid(v)
    return s * (1.0 + v * (1.0 - s))


def pick(values, masks):
    count = masks.shape[1]
    width = values.shape[1] // count
    return sum(values[:, m * width : (m + 1) * width] * masks[:, m : m + 1] for m in range(count))


def spread(values, masks):
    return jnp.concatenate(
        [values * masks[:, m : m + 1].astype(values.dtype) for m in range(masks.shape[1])], axis=1
    )


def to_time_major(ref, values, row, count):
    ref[pl.ds(row, count, stride=8), :] = values


def scan_kernel(groups, length, starts, step, act, sel, rate, y, prior, end, sf, du, bc, ys, state):
    copies, count = 8 // groups, rate.shape[0] // 8
    i = pl.program_id(0)

    @pl.when(i == 0)
    def _():
        state[...] = jnp.zeros_like(state)

    position = i * length + lax.broadcasted_iota(jnp.int32, (length, 1), 0)
    for g in range(groups):
        begin = (position == 0) | (position == starts[g])
        fade_step = jnp.where(begin, RESET, step[g])
        drive = step[g] * act[g]
        for j in range(copies):
            to_time_major(sf, fade_step, j * groups + g, length)
            to_time_major(du, drive, j * groups + g, length)
            to_time_major(bc, sel[j, g], j * groups + g, length)
    rates = [rate[s * 8 : s * 8 + 8, :] for s in range(count)]

    def one(p, h):
        row = pl.ds(pl.multiple_of(p * 8, 8), 8)
        step_p, drive_p, sel_p = sf[row, :], du[row, :], bc[row, :]
        read = None
        out = []
        for s in range(count):
            prior[pl.ds(pl.multiple_of((p * count + s) * 8, 8), 8), :] = h[s]
            now = jnp.exp2(step_p * rates[s]) * h[s] + drive_p * sel_p[:, s : s + 1]
            term = now * sel_p[:, count + s : count + s + 1]
            read = term if read is None else read + term
            out.append(now)
        ys[row, :] = read
        return tuple(out)

    first = tuple(state[s * 8 : s * 8 + 8, :] for s in range(count))
    last = lax.fori_loop(0, length, one, first, unroll=4)
    for s in range(count):
        state[s * 8 : s * 8 + 8, :] = last[s]
    end[...] = state[...]
    for g in range(groups):
        y[g] = sum(ys[pl.ds(j * groups + g, length, stride=8), :] for j in range(copies))


def back_kernel(
    groups, length, blocks, starts, step, act, sel, rate, read_grad, prior, end, pick_b, pick_c,
    weighted, faded, sel_grad, rate_grad, sf, du, gy, bc, wt, ft, pb, pc, res, carry, held,
):
    copies, count = 8 // groups, rate.shape[0] // 8
    lanes = step.shape[2]
    i = pl.program_id(0)

    @pl.when(i == 0)
    def _():
        carry[...] = jnp.zeros_like(carry)
        held[...] = end[...]
        rate_grad[...] = jnp.zeros_like(rate_grad)

    position = (blocks - 1 - i) * length + lax.broadcasted_iota(jnp.int32, (length, 1), 0)
    for g in range(groups):
        begin = (position == 0) | (position == starts[g])
        fade_step = jnp.where(begin, RESET, step[g])
        drive = step[g] * act[g]
        for j in range(copies):
            to_time_major(sf, fade_step, j * groups + g, length)
            to_time_major(du, drive, j * groups + g, length)
            to_time_major(gy, read_grad[g], j * groups + g, length)
            to_time_major(bc, sel[j, g], j * groups + g, length)
    rates = [rate[s * 8 : s * 8 + 8, :] for s in range(count)]

    def one(k, loop):
        p = length - 1 - k
        row = pl.ds(pl.multiple_of(p * 8, 8), 8)
        step_p, drive_p, grad_p, sel_p = sf[row, :], du[row, :], gy[row, :], bc[row, :]
        carried, state, total = loop
        weight_sum, fade_sum = None, None
        out_c, out_h, out_r = [], [], []
        for s in range(count):
            before = prior[pl.ds(pl.multiple_of((p * count + s) * 8, 8), 8), :]
            e = grad_p * sel_p[:, count + s : count + s + 1] + carried[s]
            cols = slice(s * lanes, (s + 1) * lanes)
            pc[row, cols] = grad_p * state[s]
            pb[row, cols] = e * drive_p
            term = e * sel_p[:, s : s + 1]
            passed = e * jnp.exp2(step_p * rates[s])
            decay = passed * before
            fade_term = decay * rates[s]
            weight_sum = term if weight_sum is None else weight_sum + term
            fade_sum = fade_term if fade_sum is None else fade_sum + fade_term
            out_c.append(passed)
            out_h.append(before)
            out_r.append(total[s] + decay * step_p)
        wt[row, :] = weight_sum
        ft[row, :] = fade_sum
        return tuple(out_c), tuple(out_h), tuple(out_r)

    def parts(ref):
        return tuple(ref[s * 8 : s * 8 + 8, :] for s in range(count))

    c, h, r = lax.fori_loop(
        0, length, one, (parts(carry), parts(held), parts(rate_grad)), unroll=2
    )
    for s in range(count):
        carry[s * 8 : s * 8 + 8, :] = c[s]
        held[s * 8 : s * 8 + 8, :] = h[s]
        rate_grad[s * 8 : s * 8 + 8, :] = r[s]
    res[...] = dot(pb[...].astype(BF), pick_b[...]) + dot(pc[...].astype(BF), pick_c[...])
    for g in range(groups):
        rows = [pl.ds(j * groups + g, length, stride=8) for j in range(copies)]
        weighted[g] = sum(wt[row, :] for row in rows)
        faded[g] = sum(ft[row, :] for row in rows) * (1.0 / LOG2E)
        for j in range(copies):
            sel_grad[j, g] = res[rows[j], :][:, : 2 * count]


def scan_block(length):
    return math.gcd(length, 64)


def scan(starts, step, act, sel, rate):
    groups, total, lanes = step.shape
    length = scan_block(total)
    copies, count = 8 // groups, rate.shape[0] // 8
    whole = pl.BlockSpec((groups, length, lanes), lambda i: (0, i, 0))
    table = pl.BlockSpec((count * 8, lanes), lambda i: (0, 0))
    return pl.pallas_call(
        functools.partial(scan_kernel, groups, length),
        grid=(total // length,),
        in_specs=[
            pl.BlockSpec(memory_space=pltpu.SMEM),
            whole,
            whole,
            pl.BlockSpec((copies, groups, length, 2 * count), lambda i: (0, 0, i, 0)),
            table,
        ],
        out_specs=[whole, pl.BlockSpec((length * count * 8, lanes), lambda i: (i, 0)), table],
        out_shape=[
            jax.ShapeDtypeStruct(step.shape, F32),
            jax.ShapeDtypeStruct((total * count * 8, lanes), F32),
            jax.ShapeDtypeStruct((count * 8, lanes), F32),
        ],
        scratch_shapes=[
            pltpu.VMEM((length * 8, lanes), F32),
            pltpu.VMEM((length * 8, lanes), F32),
            pltpu.VMEM((length * 8, 2 * count), F32),
            pltpu.VMEM((length * 8, lanes), F32),
            pltpu.VMEM((count * 8, lanes), F32),
        ],
        compiler_params=pltpu.CompilerParams(vmem_limit_bytes=VMEM),
        cost_estimate=pl.CostEstimate(
            flops=total * count * 8 * lanes * 8,
            bytes_accessed=total * count * 8 * lanes * 4,
            transcendentals=total * count * 8 * lanes,
        ),
    )(starts, step, act, sel, rate)


def scan_back(starts, step, act, sel, rate, read_grad, prior, end):
    groups, total, lanes = step.shape
    length = scan_block(total)
    blocks = total // length
    copies, count = 8 // groups, rate.shape[0] // 8
    whole = pl.BlockSpec((groups, length, lanes), lambda i: (0, blocks - 1 - i, 0))
    table = pl.BlockSpec((count * 8, lanes), lambda i: (0, 0))
    chosen = pl.BlockSpec((copies, groups, length, 2 * count), lambda i: (0, 0, blocks - 1 - i, 0))
    ones = np.zeros((2, count * lanes, 128), np.float32)
    for s in range(count):
        ones[0, s * lanes : (s + 1) * lanes, s] = 1
        ones[1, s * lanes : (s + 1) * lanes, count + s] = 1
    matrix = pl.BlockSpec((count * lanes, 128), lambda i: (0, 0))
    tall = pltpu.VMEM((length * 8, lanes), F32)
    wide = pltpu.VMEM((length * 8, count * lanes), F32)
    return pl.pallas_call(
        functools.partial(back_kernel, groups, length, blocks),
        grid=(blocks,),
        in_specs=[
            pl.BlockSpec(memory_space=pltpu.SMEM),
            whole,
            whole,
            chosen,
            table,
            whole,
            pl.BlockSpec((length * count * 8, lanes), lambda i: (blocks - 1 - i, 0)),
            table,
            matrix,
            matrix,
        ],
        out_specs=[whole, whole, chosen, table],
        out_shape=[
            jax.ShapeDtypeStruct(step.shape, F32),
            jax.ShapeDtypeStruct(step.shape, F32),
            jax.ShapeDtypeStruct((copies, groups, total, 2 * count), F32),
            jax.ShapeDtypeStruct((count * 8, lanes), F32),
        ],
        scratch_shapes=[
            tall, tall, tall, pltpu.VMEM((length * 8, 2 * count), F32), tall, tall, wide, wide,
            pltpu.VMEM((length * 8, 128), F32),
            pltpu.VMEM((count * 8, lanes), F32),
            pltpu.VMEM((count * 8, lanes), F32),
        ],
        compiler_params=pltpu.CompilerParams(vmem_limit_bytes=VMEM),
        cost_estimate=pl.CostEstimate(
            flops=total * count * 8 * lanes * 16,
            bytes_accessed=total * count * 8 * lanes * 4,
            transcendentals=total * count * 8 * lanes,
        ),
    )(starts, step, act, sel, rate, read_grad, prior, end, jnp.asarray(ones[0], BF), jnp.asarray(ones[1], BF))


def on_device(
    chan, held,
    hidden, modality, starts, norm_gain, in_weight, conv_weight, conv_bias, xproj_weight,
    dtproj_weight, step_bias, decay_log, skip_weight, out_weight, cotangent,
):
    def collect(x):
        return lax.all_gather(x, held, axis=0, tiled=True) if held else x

    def whole(x):
        return lax.all_gather(x, chan, axis=0, tiled=True)

    def scatter(x):
        return lax.psum_scatter(x, chan, scatter_dimension=0, tiled=True)

    def exchange(x):
        return lax.all_to_all(x, chan, 0, 0, tiled=True)

    def settle(x):
        return lax.psum_scatter(x, held, scatter_dimension=0, tiled=True) if held else x

    parts = math.prod(lax.axis_size(a) for a in chan)
    lots = math.prod(lax.axis_size(a) for a in held) if held else 1
    rows, width = hidden.shape[1:]
    own = conv_weight.shape[0]
    lanes = own * lots
    rank = dtproj_weight.shape[0] * parts * lots
    modes = in_weight.shape[1]
    states = decay_log.shape[1]
    mine = hidden[0]
    cot = cotangent[0]

    def shards(w):
        a, k = w.shape[0], w.shape[2] // (lots * parts * own)
        w = w.reshape(a, modes, k, lots, parts, own)
        return jnp.moveaxis(w, 4, 0).reshape(parts, a, modes, k * lots * own)

    def gathered(w):
        moved = exchange(shards(w))
        return collect(moved.reshape(-1, modes, moved.shape[3]))

    def returned(g, out_rows, k):
        g = settle(g)
        g = exchange(g.reshape(parts, out_rows, modes, k, lots, own))
        return jnp.moveaxis(g, 0, 3).reshape(out_rows, modes, k * lots * parts * own)

    gain = lax.all_gather(norm_gain, tuple(held) + tuple(chan), axis=0, tiled=True).astype(F32)
    mode_ids = whole(modality[0])
    begins = lax.all_gather(starts, "grp", axis=0, tiled=True) if "grp" in chan else starts
    groups = begins.shape[0]
    tokens = whole(mine)
    total = tokens.shape[0]
    length = total // groups
    in_cols = gathered(in_weight).reshape(width, modes, 2 * lanes)
    dt_cols = gathered(dtproj_weight).reshape(rank, modes * lanes)
    in_cols = in_cols.reshape(width, modes * 2 * lanes)
    conv_weight, conv_bias, xproj_weight, step_bias, decay_log, skip_weight, out_weight = (
        collect(w)
        for w in (conv_weight, conv_bias, xproj_weight, step_bias, decay_log, skip_weight, out_weight)
    )
    taps = conv_weight.astype(F32)
    conv_base = conv_bias.astype(F32)
    bias = step_bias.astype(F32)
    skip = skip_weight.astype(F32)
    xproj = xproj_weight.reshape(lanes, -1)
    out_rows = jnp.moveaxis(out_weight, 1, 0).reshape(modes * lanes, width)
    masks = (mode_ids[:, None] == jnp.arange(modes, dtype=jnp.int32)[None, :]).astype(F32)
    position = jnp.tile(jnp.arange(length, dtype=jnp.int32), groups)
    second = jnp.repeat(begins, length, total_repeat_length=total)
    begin = jnp.where(position >= second, second, 0)
    copies = 8 // groups
    count = states // copies
    rate = -jnp.exp(decay_log.astype(F32))
    table = jnp.moveaxis(rate.T.reshape(copies, count, lanes), 0, 1)
    table = jnp.repeat(table.reshape(count * copies, 1, lanes), groups, axis=1).reshape(-1, lanes)

    x = tokens.astype(F32)
    normed = (
        x * lax.rsqrt(jnp.mean(x * x, axis=1, keepdims=True) + EPS) * gain
    ).astype(BF)
    proj = pick(dot(normed, in_cols), masks)
    conv_in, gate_in = proj[:, :lanes], proj[:, lanes:]

    def later(v, by):
        v = v.reshape(groups, length, -1)
        return jnp.pad(v, ((0, 0), (by, 0), (0, 0)))[:, :length].reshape(total, -1)

    def earlier(v, by):
        v = v.reshape(groups, length, -1)
        return jnp.pad(v, ((0, 0), (0, by), (0, 0)))[:, by:].reshape(total, -1)

    valid = [(position - 3 + k >= begin).astype(F32)[:, None] for k in range(4)]
    shifted = [later(conv_in, 3 - k) * valid[k] for k in range(4)]
    pre_act = conv_base + sum(taps[:, k] * shifted[k] for k in range(4))
    act = jax.nn.silu(pre_act)
    act_low = act.astype(BF)
    picked = lax.psum(pick(dot(act_low, xproj), masks), chan)
    rank_low = picked[:, :rank].astype(BF)
    sel_in = picked[:, rank : rank + states]
    sel_out = picked[:, rank + states :]
    pre = pick(dot(rank_low, dt_cols), masks) + sum(
        masks[:, m : m + 1] * bias[:, m] for m in range(modes)
    )
    step = jax.nn.softplus(pre)
    sel = jnp.stack(
        [
            jnp.concatenate([v[:, j * count : (j + 1) * count] for v in (sel_in, sel_out)], axis=1)
            for j in range(copies)
        ]
    ).reshape(copies, groups, length, 2 * count)
    grouped = (groups, length, lanes)
    read, prior, end = scan(
        begins, step.reshape(grouped), act.reshape(grouped), sel, table * LOG2E
    )
    read = read.reshape(total, lanes) + skip * act
    gate_act = jax.nn.silu(gate_in)
    gated = spread((read * gate_act).astype(BF), masks)
    branch = scatter(dot(gated, out_rows).astype(BF))
    output = (mine.astype(F32) + branch.astype(F32)).astype(BF)[None]

    cots = whole(cot)
    grad_gated = pick(dot(cots, out_rows, ((1,), (1,))), masks)
    grad_out_weight = jnp.moveaxis(
        dot(gated, cots, ((0,), (0,))).reshape(modes, lanes, width), 0, 1
    )
    read_grad = grad_gated * gate_act
    gate_grad = grad_gated * read * silu_slope(gate_in)
    grad_skip = jnp.sum(read_grad * act, axis=0)
    weighted, faded, sel_grad, rate_grad = scan_back(
        begins, step.reshape(grouped), act.reshape(grouped), sel, table * LOG2E,
        read_grad.reshape(grouped), prior, end,
    )
    weighted = weighted.reshape(total, lanes)
    grad_step = act * weighted + faded.reshape(total, lanes)
    grad_act = skip * read_grad + step * weighted
    rate_grad = rate_grad.reshape(count, copies, groups, lanes).sum(axis=2)
    grad_decay = jnp.moveaxis(rate_grad, 0, 1).reshape(states, lanes).T * rate
    grad_pre = grad_step * jax.nn.sigmoid(pre)
    grad_bias = jnp.stack(
        [jnp.sum(grad_pre * masks[:, m : m + 1], axis=0) for m in range(modes)], axis=1
    )
    pre_low = spread(grad_pre.astype(BF), masks)
    grad_dt = dot(rank_low, pre_low, ((0,), (0,))).reshape(rank, modes, lanes)
    sel_grad = sel_grad.reshape(copies, total, 2, count)
    sel_grad = jnp.moveaxis(sel_grad, 0, 2).reshape(total, 2 * states)
    grad_picked = lax.psum(
        jnp.concatenate([dot(pre_low, dt_cols, ((1,), (1,))), sel_grad], axis=1), chan
    ).astype(BF)
    grad_spread = spread(grad_picked, masks)
    grad_xproj = dot(act_low, grad_spread, ((0,), (0,))).reshape(lanes, modes, -1)
    grad_act = grad_act + dot(grad_spread, xproj, ((1,), (1,)))
    grad_v = grad_act * silu_slope(pre_act)
    grad_conv_bias = jnp.sum(grad_v, axis=0)
    grad_conv = jnp.stack([jnp.sum(grad_v * shifted[k], axis=0) for k in range(4)], axis=1)
    conv_grad = sum(earlier(grad_v * taps[:, k] * valid[k], 3 - k) for k in range(4))
    proj_grad = spread(jnp.concatenate([conv_grad, gate_grad], axis=1).astype(BF), masks)
    grad_in = returned(
        dot(normed, proj_grad, ((0,), (0,))).reshape(width, modes, 2 * lanes).astype(BF),
        in_weight.shape[0], 2,
    ).astype(F32)
    grad_dt = returned(grad_dt, dtproj_weight.shape[0], 1)
    normed_grad = scatter(dot(proj_grad, in_cols, ((1,), (1,))).astype(BF)).astype(F32)
    grad_gain = jnp.sum(grad_in * in_weight.astype(F32), axis=(1, 2)) / norm_gain.astype(F32)
    xm = mine.astype(F32)
    scale = lax.rsqrt(jnp.mean(xm * xm, axis=1, keepdims=True) + EPS)
    unit = xm * scale
    scaled = normed_grad * gain
    grad_hidden = cot.astype(F32) + scale * (
        scaled - unit * jnp.mean(scaled * unit, axis=1, keepdims=True)
    )
    return (
        output,
        grad_hidden[None],
        grad_gain,
        grad_in,
        settle(grad_conv),
        settle(grad_conv_bias),
        settle(grad_xproj),
        grad_dt,
        settle(grad_bias),
        settle(grad_decay),
        settle(grad_skip),
        settle(grad_out_weight),
    )


def solution(mesh):
    both = ("grp", "seq")
    full = mesh.shape["grp"] * mesh.shape["seq"] <= 32
    chan, held = (both, ()) if full else (("seq",), ("grp",))
    row = P(both)
    return jax.shard_map(
        functools.partial(on_device, chan, held),
        mesh=mesh,
        in_specs=(
            P("grp", "seq", None), P("grp", "seq"), P("grp"),
            row, row, row, row, row, row, row, row, row, row,
            P("grp", "seq", None),
        ),
        out_specs=(P("grp", "seq", None), P("grp", "seq", None)) + (row,) * 10,
        check_vma=False,
    )
```

time: 7610 us -> 1200 us (0.16)
  waiting for transfers between devices: 5550 us -> 499 us
  local copies, waits for them, and re-layouts: 881 us -> 79.5 us
  other arithmetic: 558 us -> 80.6 us
  matrix products: 269 us -> 112 us
  Pallas kernels: 0 us -> 137 us
    unnamed x19 -> x5, waiting for transfers between devices: 3610 us -> 1.43 us
    reduce_scatter x3 -> x2, waiting for transfers between devices: 1300 us -> 245 us  [scatter(): return lax.psum_scatter(x, chan, scatter_dimension=0, tiled=True)]
    all_gather x8 -> x2, waiting for transfers between devices: 638 us -> 26.9 us  [whole(): return lax.all_gather(x, chan, axis=0, tiled=True)]
    dynamic_slice x519 -> x0, local copies, waits for them, and re-layouts: 401 us -> none  [the longest x512 388 us: local_states(): lax.scan(one_token, zero_state, (step_size, in_select, activated, keep_ma...]
    transpose x2, local copies, waits for them, and re-layouts: 290 us -> 0.05 us  [the longest x1 0.04 us: on_device(): sel_grad = jnp.moveaxis(sel_grad, 0, 2).reshape(total, 2 * states)]
    dynamic_update_slice x264 -> x0, other arithmetic: 211 us -> none  [the longest x256 196 us: local_states(): lax.scan(one_token, zero_state, (step_size, in_select, activated, keep_ma...]
    all_gather x5 -> x1, blocking collectives: 202 us -> 40.7 us  [whole(): return lax.all_gather(x, chan, axis=0, tiled=True)]
    dot_general x13 -> x12, matrix products: 266 us -> 112 us  [dot(): return lax.dot_general(a, b, (dims, ((), ())), preferred_element_type=F32)]
  transfers between devices with their start and end apart: 17 -> 9, of which waited for: 8 -> 5; matrix products, arithmetic and copies ran while one was open for 20% -> 15% of each run, Pallas kernels for 0% -> 0%
where the time goes in v1:
time: 1200 us; the launch traced here: 1190 us
  waiting for transfers between devices  499 us (42%)
  blocking collectives  249 us (21%)
  Pallas kernels  137 us (11%)
  matrix products  112 us (9%)
  other arithmetic  80.6 us (7%)
  local copies, waits for them, and re-layouts  79.5 us (7%)
  starting transfers between devices  20.3 us (2%)
  between operations  15.7 us (1%)
    reduce_scatter x2, waiting for transfers between devices, scatter(): return lax.psum_scatter(x, chan, scatter_dimension=0, tiled=True)  245 us
    unnamed x2, blocking collectives  140 us
    psum x1, waiting for transfers between devices, on_device(): picked = lax.psum(pick(dot(act_low, xproj), masks), chan)  130 us
    dot_general x12, matrix products, dot(): return lax.dot_general(a, b, (dims, ((), ())), preferred_element_type=F32)  112 us
    all_to_all x4, waiting for transfers between devices, exchange(): return lax.all_to_all(x, chan, 0, 0, tiled=True)  95.5 us
    pallas_call x1, Pallas kernels, scan_back(): pl.pallas_call(functools.partial(back_kernel, groups, length, blocks), gr...  83.7 us
    psum x1, blocking collectives, on_device(): lax.psum(jnp.concatenate([dot(pre_low, dt_cols, ((1,), (1,))), sel_grad],...  68.3 us
    pallas_call x1, Pallas kernels, scan(): pl.pallas_call(functools.partial(scan_kernel, groups, length), grid=(tota...  53.2 us
  transfers between devices with their start and end apart: 9, of which 5 were waited for; matrix products, arithmetic and copies ran while one was open for 15% of the time, Pallas kernels for 0%

profile of v1, /device:TPU:0, one launch (start us, length us, event | category | flops | bytes accessed | tf_op | source)
XLA Modules:
  0.0 1193.0 jit_solution(13915007193818957613)
XLA Ops:
  11.4 5.2 copy.113
  16.6 6.0 reshape.317
  22.8 7.5 all-to-all-start
  32.2 15.3 %all-reduce.6.starts = s32[4]{0:T(128)S(1)} all-reduce(s32[4]{0:T(128)S(1)} %dynamic-update-slice.3), channel_id=1, replica_groups=mesh['grp'=4,'seq'=8] {'grp'}, use_global_device_ids=true, to_apply=%add.6 | all-reduce | flops 4 | bytes 32
  47.8 124.5 %all-reduce.7 = bf16[2048]{0:T(1024)(128)(2,1)S(1)} all-reduce(bf16[2048]{0:T(1024)(128)(2,1)S(1)} %dynamic-update-slice.4), channel_id=1, replica_groups=mesh['grp'=4,'seq'=8] {'grp','seq'}, use_global_device_ids=true, to_apply=%add.7 | all-reduce | flops 2048 | bytes 8192
  173.3 40.7 %all-gather.1 = s32[1,4096]{1,0:T(1,128)S(1)} all-gather(s32[1,128]{1,0:T(1,128)S(1)} %copy-done.56), channel_id=3, replica_groups=mesh['grp'=4,'seq'=8] {'grp','seq'}, dimensions={1}, use_global_device_ids=true | all-gather | bytes 16896 | tf_op jit(solution)/shard_map/all_gather | solution.py:261
  220.0 4.9 copy.82
  227.4 7.7 fusion
  238.1 18.6 %fusion.10 = f32[4096,768]{1,0:T(8,128)} fusion(bf16[2048,768]{1,0:T(8,128)(2,1)} %bitcast.228, bf16[1,4096,2048]{2,1,0:T(8,128)(2,1)S(1)} %copy-done.23, f32[2048]{0:T(1024)S(1)} %convert_element_type.153, f32[4096]{0:T(1024)S(1)} %add_rsqrt_fusion), kind=kOutput, calls=%fused_computation.18 | convolution fusion | flops 12918456320 | bytes 32530432 | tf_op jit(solution)/shard_map/dot_general | solution.py:21
  256.7 6.0 fusion.12
  267.6 26.9 %all-gather.8.cloned.1.call-done = bf16[1,4096,2048]{2,1,0:T(8,128)(2,1)} async-done(((bf16[1,128,2048]{2,1,0:T(8,128)(2,1)}), bf16[1,4096,2048]{2,1,0:T(8,128)(2,1)}) %all-gather.8.cloned.1.call-update) | async-done | bytes 16777232 | tf_op jit(solution)/shard_map/all_gather | solution.py:261
  294.5 12.3 %fusion.5 = f32[4096,384]{1,0:T(8,128)S(1)} fusion(bf16[384,2048]{1,0:T(8,128)(2,1)S(1)} %bitcast.211, bf16[1,4096,2048]{2,1,0:T(8,128)(2,1)} %all-gather.8.cloned.1.call-done), kind=kOutput, calls=%fused_computation.7 | convolution fusion | flops 6442450944 | bytes 24641536 | tf_op jit(solution)/shard_map/dot_general | solution.py:21
  306.8 7.4 multiply_reduce_fusion.1
  323.7 130.1 %all-reduce.11.cloned.1.call-done = f32[4096,160]{0,1:T(8,128)} async-done(((f32[4096,160]{0,1:T(8,128)}), f32[4096,160]{0,1:T(8,128)}) %all-reduce.11.cloned.1.call-update) | async-done | bytes 2621456 | tf_op jit(solution)/shard_map/psum | solution.py:347
  458.9 4.6 pad_maximum_fusion.1.sel
  468.9 53.2 %shard_map.247 = (f32[4,1024,128]{2,1,0:T(8,128)S(1)}, f32[65536,128]{1,0:T(8,128)}, f32[64,128]{1,0:T(8,128)S(1)}) custom-call(s32[4]{0:T(128)S(1)} %all-reduce.6.starts, f32[4,1024,128]{2,1,0:T(8,128)S(1)} %bitcast.212, f32[4,1024,128]{2,1,0:T(8,128)} %bitcast.223, f32[2,4,1024,16]{3,2,1,0:T(8,128)} %pad_maximum_fusion.1.sel, f32[64,128]{1,0:T(8,128)S(1)} %bitcast.214), custom_call_target="tpu_custom_call" | custom-call | flops 67108864 | bytes 33554432 | tf_op jit(solution)/shard_map/pallas_call | solution.py:168
  523.5 83.7 %shard_map.248 = (f32[4,1024,128]{2,1,0:T(8,128)S(1)}, f32[4,1024,128]{2,1,0:T(8,128)S(1)}, f32[2,4,1024,16]{3,2,1,0:T(8,128)}, f32[64,128]{1,0:T(8,128)S(1)}) custom-call(s32[4]{0:T(128)S(1)} %all-reduce.6.starts, f32[4,1024,128]{2,1,0:T(8,128)} %bitcast.213, f32[4,1024,128]{2,1,0:T(8,128)} %bitcast.224, f32[2,4,1024,16]{3,2,1,0:T(8,128)} %pad_maximum_fusion.1.sel, ...), custom_call_target="tpu_custom_call" | custom-call | flops 134217728 | bytes 33554432 | tf_op jit(solution)/shard_map/pallas_call | solution.py:215
  619.0 6.2 multiply_reduce_fusion.4
  632.7 68.3 %all-reduce.12 = bf16[4096,160]{0,1:T(8,128)(2,1)S(1)} all-reduce(f32[4096,160]{0,1:T(8,128)} %pad_maximum_fusion.5), channel_id=1, replica_groups=mesh['grp'=4,'seq'=8] {'grp','seq'}, use_global_device_ids=true, to_apply=%region_4.5 | all-reduce | flops 655360 | bytes 3932160 | tf_op jit(solution)/shard_map/psum | solution.py:396
  711.1 5.2 fusion.71
  720.0 20.3 %convolution_convert_fusion = bf16[4096,2048]{1,0:T(8,128)(2,1)} fusion(bf16[2048,768]{1,0:T(8,128)(2,1)} %bitcast.229, bf16[4096,256]{1,0:T(8,128)(2,1)} %get-tuple-element.67, bf16[4096,256]{1,0:T(8,128)(2,1)} %get-tuple-element.66, bf16[4096,256]{1,0:T(8,128)(2,1)} %get-tuple-element.65), kind=kOutput, calls=%fused_computation.9 | convolution fusion | flops 12912164864 | bytes 26214400 | tf_op jit(solution)/shard_map/dot_general | solution.py:21
  741.5 13.9 %convolution_convert_fusion.1 = bf16[4096,2048]{1,0:T(8,128)(2,1)} fusion(bf16[384,2048]{1,0:T(8,128)(2,1)S(1)} %bitcast.210, bf16[4096,128]{1,0:T(8,128)(2,1)} %get-tuple-element.91, bf16[4096,128]{1,0:T(8,128)(2,1)} %get-tuple-element.92, bf16[4096,128]{1,0:T(8,128)(2,1)S(1)} %copy-done.33), kind=kOutput, calls=%fused_computation.10 | convolution fusion | flops 6460276736 | bytes 21495808 | tf_op jit(solution)/shard_map/dot_general | solution.py:21
  763.8 21.0 %fusion.14 = bf16[2048,768]{1,0:T(8,128)(2,1)} fusion(bf16[1,4096,2048]{2,1,0:T(8,128)(2,1)} %all-gather.6.cloned.1.call-done, f32[2048]{0:T(1024)S(1)} %copy-done.46, f32[4096]{0:T(1024)S(1)} %copy-done.50, bf16[4096,256]{1,0:T(8,128)(2,1)} %get-tuple-element.67, bf16[4096,256]{1,0:T(8,128)(2,1)} %get-tuple-element.66, bf16[4096,256]{1,0:T(8,128)(2,1)} %get-tuple-element.65), kind=kOutput, calls=%fused_computation.26 | convolution fusion | flops 12938903552 | bytes 26238976 | tf_op jit(solution)/shard_map/dot_general | solution.py:21
  784.8 6.9 convert_element_type.177
  792.4 6.3 all-to-all-start.2
  805.3 12.2 %fusion.3 = f32[384,2048]{1,0:T(8,128)} fusion(bf16[1,4096,2048]{2,1,0:T(8,128)(2,1)} %all-gather.8.cloned.1.call-done, bf16[4096,128]{1,0:T(8,128)(2,1)S(1)} %copy-done.35, bf16[4096,128]{1,0:T(8,128)(2,1)S(1)} %copy-done.36, bf16[4096,128]{1,0:T(8,128)(2,1)S(1)} %copy-done.34), kind=kOutput, calls=%fused_computation.5 | convolution fusion | flops 6451888128 | bytes 23068672 | tf_op jit(solution)/shard_map/dot_general | solution.py:21
  818.2 95.5 %all-to-all-done.2 = bf16[32,64,3,2,1,128]{5,3,2,1,4,0:T(2,128)(2,1)} async-done(((bf16[32,64,3,2,1,128]{5,3,2,1,4,0:T(2,128)(2,1)}), bf16[32,64,3,2,1,128]{5,3,2,1,4,0:T(2,128)(2,1)}, u32[]{:S(2)}, u32[]{:S(2)}) %all-to-all-start.2) | async-done | bytes 3145760 | tf_op jit(solution)/shard_map/all_to_all | solution.py:267
  918.4 6.2 copy.91
  924.6 7.2 reshape.342
  931.8 4.6 multiply_reduce_fusion
  936.9 55.5 %reduce-scatter.5.cloned.1.call-done = bf16[128,2048]{1,0:T(8,128)(2,1)} async-done(((bf16[4096,2048]{1,0:T(8,128)(2,1)}), bf16[128,2048]{1,0:T(8,128)(2,1)}) %reduce-scatter.5.cloned.1.call-update) | async-done | bytes 524304 | tf_op jit(solution)/shard_map/reduce_scatter | solution.py:264
  993.8 189.4 %reduce-scatter.3.cloned.1.call-done = bf16[128,2048]{1,0:T(8,128)(2,1)} async-done(((bf16[4096,2048]{1,0:T(8,128)(2,1)}), bf16[128,2048]{1,0:T(8,128)(2,1)}) %reduce-scatter.3.cloned.1.call-update) | async-done | bytes 524304 | tf_op jit(solution)/shard_map/reduce_scatter | solution.py:264
  (206 shorter events, 103.8 us)
Async XLA Ops:
  7.2 287.3 %copy-start = (bf16[128,3,2048]{2,0,1:T(8,128)(2,1)S(1)}, bf16[128,3,2048]{2,0,1:T(8,128)(2,1)}, u32[]{:S(2)}) copy-start(bf16[128,3,2048]{2,0,1:T(8,128)(2,1)} %param.30) | copy-start | bytes 4718596
  7.2 220.2 %all-gather.6.cloned.1.call-start = ((), (), s32[]{:S(2)}) async-start(), calls=%async_computation.9 | async-start | bytes 17301504 | tf_op jit(solution)/shard_map/all_gather | solution.py:261
  7.9 286.6 %all-gather.8.cloned.1.call-start = ((), (), s32[]{:S(2)}) async-start(), calls=%async_computation.10 | async-start | bytes 17301504 | tf_op jit(solution)/shard_map/all_gather | solution.py:261
  22.7 24.9 %copy-start.54 = (bf16[128,4]{0,1:T(4,128)(2,1)S(1)}, bf16[128,4]{0,1:T(4,128)(2,1)}, u32[]{:S(2)}) copy-start(bf16[128,4]{0,1:T(4,128)(2,1)} %param.23) | copy-start | bytes 3076
  22.7 24.9 %copy-start.59 = (bf16[64]{0:T(256)(128)(2,1)S(1)}, bf16[64]{0:T(256)(128)(2,1)}, u32[]{:S(2)}) copy-start(bf16[64]{0:T(256)(128)(2,1)} %param.21) | copy-start | bytes 388
  22.7 149.7 %copy-start.57 = (bf16[128]{0:T(256)(128)(2,1)S(1)}, bf16[128]{0:T(256)(128)(2,1)}, u32[]{:S(2)}) copy-start(bf16[128]{0:T(256)(128)(2,1)} %param.24) | copy-start | bytes 772
  22.7 149.7 %copy-start.55 = (bf16[128,3]{0,1:T(4,128)(2,1)S(1)}, bf16[128,3]{0,1:T(4,128)(2,1)}, u32[]{:S(2)}) copy-start(bf16[128,3]{0,1:T(4,128)(2,1)} %param.27) | copy-start | bytes 2308
  22.7 149.7 %copy-start.44 = (bf16[4,3,4096]{2,0,1:T(4,128)(2,1)S(1)}, bf16[4,3,4096]{2,0,1:T(4,128)(2,1)}, u32[]{:S(2)}) copy-start(bf16[4,3,4096]{2,0,1:T(4,128)(2,1)} %param.26) | copy-start | bytes 294916
  22.7 150.5 %copy-start.47 = (bf16[128,16]{0,1:T(8,128)(2,1)S(1)}, bf16[128,16]{0,1:T(8,128)(2,1)}, u32[]{:S(2)}) copy-start(bf16[128,16]{0,1:T(8,128)(2,1)} %param.28) | copy-start | bytes 12292
  22.7 150.5 %copy-start.58 = (bf16[128]{0:T(256)(128)(2,1)S(1)}, bf16[128]{0:T(256)(128)(2,1)}, u32[]{:S(2)}) copy-start(bf16[128]{0:T(256)(128)(2,1)} %param.29) | copy-start | bytes 772
  22.7 150.5 %copy-start.56 = (s32[1,128]{1,0:T(1,128)S(1)}, s32[1,128]{1,0:T(1,128)}, u32[]{:S(2)}) copy-start(s32[1,128]{1,0:T(1,128)} %param.19) | copy-start | bytes 1540
  22.7 191.9 %copy-start.51 = (pred[4096]{0:T(1024)(128)(4,1)S(1)}, pred[4096]{0:T(1024)(128)(4,1)}, u32[]{:S(2)}) copy-start(pred[4096]{0:T(1024)(128)(4,1)} %constant.166) | copy-start | bytes 12292
  22.7 191.9 %copy-start.52 = (pred[4096]{0:T(1024)(128)(4,1)S(1)}, pred[4096]{0:T(1024)(128)(4,1)}, u32[]{:S(2)}) copy-start(pred[4096]{0:T(1024)(128)(4,1)} %constant.167) | copy-start | bytes 12292
  22.8 191.9 %copy-start.53 = (pred[4096]{0:T(1024)(128)(4,1)S(1)}, pred[4096]{0:T(1024)(128)(4,1)}, u32[]{:S(2)}) copy-start(pred[4096]{0:T(1024)(128)(4,1)} %constant.168) | copy-start | bytes 12292
  22.8 194.6 %all-to-all-start = ((bf16[32,64,3,256]{3,1,2,0:T(8,128)(2,1)}), bf16[32,64,3,256]{3,1,2,0:T(8,128)(2,1)}, u32[]{:S(2)}, u32[]{:S(2)}) async-start(bf16[32,64,3,256]{3,1,2,0:T(8,128)(2,1)} %reshape.317), calls=%async_computation | async-start | bytes 6291456 | tf_op jit(solution)/shard_map/all_to_all | solution.py:267
  172.4 62.8 %copy-start.45 = (f32[2048]{0:T(1024)}, f32[2048]{0:T(1024)S(1)}, u32[]{:S(2)}) copy-start(f32[2048]{0:T(1024)S(1)} %convert_element_type.153) | copy-start | bytes 24580
  217.3 102.7 %all-to-all-start.1 = ((bf16[32,4,3,128]{3,1,2,0:T(4,128)(2,1)}), bf16[32,4,3,128]{3,1,2,0:T(4,128)(2,1)S(1)}, u32[]{:S(2)}, u32[]{:S(2)}) async-start(bf16[32,4,3,128]{3,1,2,0:T(4,128)(2,1)} %copy.83), calls=%async_computation.1 | async-start | bytes 196608 | tf_op jit(solution)/shard_map/all_to_all | solution.py:267
  219.9 233.9 %all-reduce.11.cloned.1.call-start = ((), (), s32[]{:S(2)}) async-start(), calls=%async_computation.6 | async-start | bytes 5242880 | tf_op jit(solution)/shard_map/psum | solution.py:347
  235.1 21.6 %copy-start.49 = (f32[4096]{0:T(1024)}, f32[4096]{0:T(1024)S(1)}, u32[]{:S(2)}) copy-start(f32[4096]{0:T(1024)S(1)} %add_rsqrt_fusion) | copy-start | bytes 49156
  294.5 12.3 %copy-start.14 = (f32[4096,256]{1,0:T(8,128)S(1)}, f32[4096,256]{1,0:T(8,128)}, u32[]{:S(2)}) copy-start(f32[4096,256]{1,0:T(8,128)} %copy-done.13) | copy-start | bytes 12582916
  294.5 12.3 %copy-start.17 = (f32[4,1024,128]{2,1,0:T(8,128)S(1)}, f32[4,1024,128]{2,1,0:T(8,128)}, u32[]{:S(2)}) copy-start(f32[4,1024,128]{2,1,0:T(8,128)} %get-tuple-element.74) | copy-start | bytes 6291460
  294.5 12.3 %copy-start.19 = (f32[4,1024,128]{2,1,0:T(8,128)S(1)}, f32[4,1024,128]{2,1,0:T(8,128)}, u32[]{:S(2)}) copy-start(f32[4,1024,128]{2,1,0:T(8,128)} %get-tuple-element.75) | copy-start | bytes 6291460
  294.5 12.3 %copy-start.21 = (f32[4,1024,128]{2,1,0:T(8,128)S(1)}, f32[4,1024,128]{2,1,0:T(8,128)}, u32[]{:S(2)}) copy-start(f32[4,1024,128]{2,1,0:T(8,128)} %get-tuple-element.76) | copy-start | bytes 6291460
  319.3 673.1 %reduce-scatter.5.cloned.1.call-start = ((), (), s32[]{:S(2)}) async-start(), calls=%async_computation.8 | async-start | bytes 17301504 | tf_op jit(solution)/shard_map/reduce_scatter | solution.py:264
  468.9 53.3 %copy-start.1 = (f32[4096,128]{1,0:T(8,128)}, f32[4096,128]{1,0:T(8,128)S(1)}, u32[]{:S(2)}) copy-start(f32[4096,128]{1,0:T(8,128)S(1)} %get-tuple-element.56) | copy-start | bytes 6291460
  468.9 54.6 %copy-start.8 = (bf16[1024,128]{1,0:T(8,128)(2,1)S(1)}, bf16[1024,128]{1,0:T(8,128)(2,1)}, u32[]{:S(2)}) copy-start(bf16[1024,128]{1,0:T(8,128)(2,1)} %constant.142.clone.pick_b) | copy-start | bytes 786436
  468.9 54.6 %copy-start.9 = (bf16[1024,128]{1,0:T(8,128)(2,1)S(1)}, bf16[1024,128]{1,0:T(8,128)(2,1)}, u32[]{:S(2)}) copy-start(bf16[1024,128]{1,0:T(8,128)(2,1)} %constant.143.clone.pick_c) | copy-start | bytes 786436
  740.3 442.9 %reduce-scatter.3.cloned.1.call-start = ((), (), s32[]{:S(2)}) async-start(), calls=%async_computation.7 | async-start | bytes 17301504 | tf_op jit(solution)/shard_map/reduce_scatter | solution.py:264
  760.4 31.3 %all-to-all-start.3 = ((f32[32,4,3,1,1,128]{5,1,4,3,2,0:T(4,128)}), f32[32,4,3,1,1,128]{5,1,4,3,2,0:T(4,128)S(1)}, u32[]{:S(2)}, u32[]{:S(2)}) async-start(f32[32,4,3,1,1,128]{5,1,4,3,2,0:T(4,128)} %copy.92), calls=%async_computation.5 | async-start | bytes 393216 | tf_op jit(solution)/shard_map/all_to_all | solution.py:267
  792.4 121.4 %all-to-all-start.2 = ((bf16[32,64,3,2,1,128]{5,3,2,1,4,0:T(2,128)(2,1)}), bf16[32,64,3,2,1,128]{5,3,2,1,4,0:T(2,128)(2,1)}, u32[]{:S(2)}, u32[]{:S(2)}) async-start(bf16[32,64,3,2,1,128]{5,3,2,1,4,0:T(2,128)(2,1)} %bitcast.219), calls=%async_computation.4 | async-start | bytes 6291456 | tf_op jit(solution)/shard_map/all_to_all | solution.py:267
  805.3 12.2 %copy-start.42 = (f32[32,4,3,1,1,128]{5,1,4,3,2,0:T(4,128)S(1)}, f32[32,4,3,1,1,128]{5,1,4,3,2,0:T(4,128)}, u32[]{:S(2)}) copy-start(f32[32,4,3,1,1,128]{5,1,4,3,2,0:T(4,128)} %copy-done.41) | copy-start | bytes 589828
  931.8 251.4 %copy-start.27 = (bf16[1,128,2048]{2,1,0:T(8,128)(2,1)S(1)}, bf16[1,128,2048]{2,1,0:T(8,128)(2,1)}, u32[]{:S(2)}) copy-start(bf16[1,128,2048]{2,1,0:T(8,128)(2,1)} %param.31) | copy-start | bytes 1572868
  (39 other events, 165.3 us)
Sparse Core Ops, SparseCore 0:
  11.0 165.7 all-gather.5
  179.8 114.6 all-gather.7
  319.5 134.3 all-reduce.10
  740.4 251.9 reduce-scatter.4
  994.6 188.4 reduce-scatter.2

commit v2 on v1

v2 whole, which is shorter than its diff:
```python
import functools
import math

import jax
import jax.numpy as jnp
import numpy as np
from jax import lax
from jax.experimental import pallas as pl
from jax.experimental.pallas import tpu as pltpu
from jax.sharding import PartitionSpec as P

EPS = 1e-05
BF = jnp.bfloat16
F32 = jnp.float32
LOG2E = math.log2(math.e)
RESET = 1e4
VMEM = 48 * 1024 * 1024


def dot(a, b, dims=((1,), (0,))):
    return lax.dot_general(a, b, (dims, ((), ())), preferred_element_type=F32)


def silu_slope(v):
    s = jax.nn.sigmoid(v)
    return s * (1.0 + v * (1.0 - s))


def after(x, other):
    return x + (other[(0,) * other.ndim] * 0).astype(x.dtype)


def pick(values, masks):
    count = masks.shape[1]
    width = values.shape[1] // count
    return sum(values[:, m * width : (m + 1) * width] * masks[:, m : m + 1] for m in range(count))


def spread(values, masks):
    return jnp.concatenate(
        [values * masks[:, m : m + 1].astype(values.dtype) for m in range(masks.shape[1])], axis=1
    )


def spread_lanes(source, widen, target):

    @pl.loop(0, source.shape[0] // 128)
    def _(n):
        row = pl.ds(pl.multiple_of(n * 128, 128), 128)
        target[row, :] = dot(source[row, :].astype(BF), widen[...])


def widening(columns, lanes):
    ones = np.zeros((2 * columns, columns * lanes), np.float32)
    for s in range(columns):
        ones[s, s * lanes : (s + 1) * lanes] = 1
        ones[columns + s, s * lanes : (s + 1) * lanes] = 1
    return jnp.asarray(ones, BF)


def dot_t(a, b):
    return dot(a, b, ((1,), (1,)))


def t_dot(a, b):
    return dot(a, b, ((0,), (0,)))


def softplus(x):
    return jnp.maximum(x, 0.0) + jnp.log1p(jnp.exp(-jnp.abs(x)))


def packed(values, width):
    count = 128 // width
    span = values.shape[0] // count
    return jnp.concatenate([values[q * span : (q + 1) * span, :] for q in range(count)], axis=1)


def unpacked(values, width):
    values = values.astype(F32)
    return jnp.concatenate(
        [values[:, q * width : (q + 1) * width] for q in range(128 // width)], axis=0
    )


def to_time_major(ref, values, row, count):
    ref[pl.ds(row, count, stride=8), :] = values


def lay_out(groups, length, states, first, starts, step, act, picked, extra, sf, du, bc, also):
    copies = 8 // groups
    position = first + lax.broadcasted_iota(jnp.int32, (length, 1), 0)
    lane = lax.broadcasted_iota(jnp.int32, (1, 4 * states), 1)
    owner = lane % states // (states // copies)
    for g in range(groups):
        begin = (position == 0) | (position == starts[g])
        fade_step = jnp.where(begin, RESET, step[g])
        drive = step[g] * act[g, 0]
        span = length * 2 * states // 128
        chosen = jnp.concatenate(
            [
                unpacked(picked[g, 0, length + n * span : length + (n + 1) * span, :], 2 * states)
                for n in range(2)
            ],
            axis=1,
        )
        for j in range(copies):
            to_time_major(sf, fade_step, j * groups + g, length)
            to_time_major(du, drive, j * groups + g, length)
            to_time_major(bc, jnp.where(owner == j, chosen, 0.0), j * groups + g, length)
            if also is not None:
                to_time_major(also, extra[g, 0], j * groups + g, length)


def pre_step(picked, mask, dt, bias):
    modes, lanes = bias.shape
    product = dot(picked[: mask.shape[0], :], dt[...])
    return sum(
        (product[:, m * lanes : (m + 1) * lanes] + bias[m : m + 1, :]) * mask[:, m : m + 1]
        for m in range(modes)
    )


def scan_kernel(
    groups, length, states, table, starts, places, act, picked, mask, gate, rate, widen, dt, bias, skip,
    y, gated, spread_gated, pre, prior, end, sf, du, bc, ys, state, ex,
):
    copies, count, lanes = 8 // groups, rate.shape[0] // 8, rate.shape[1]
    i = pl.program_id(0)

    @pl.when(i == 0)
    def _():
        state[...] = jnp.zeros_like(state)

    steps = []
    for g in range(groups):
        raw = pre_step(picked[g, 0], mask[g, 0], dt, bias)
        pre[g, 0] = raw
        steps.append(softplus(raw))
    lay_out(groups, length, states, i * length, starts, steps, act, picked, None, sf, du, bc, None)
    spread_lanes(bc, widen, ex)
    rates = [rate[s * 8 : s * 8 + 8, :] for s in range(count)]

    def one(p, h):
        row = pl.ds(pl.multiple_of(p * 8, 8), 8)
        step_p, drive_p = sf[row, :], du[row, :]
        read = None
        out = []
        for s in range(count):
            prior[pl.ds(pl.multiple_of((p * count + s) * 8, 8), 8), :] = h[s]
            now = jnp.exp2(step_p * rates[s]) * h[s] + drive_p * ex[row, s * lanes : (s + 1) * lanes]
            term = now * ex[row, (count + s) * lanes : (count + s + 1) * lanes]
            read = term if read is None else read + term
            out.append(now)
        ys[row, :] = read
        return tuple(out)

    first = tuple(state[s * 8 : s * 8 + 8, :] for s in range(count))
    last = lax.fori_loop(0, length, one, first, unroll=4)
    for s in range(count):
        state[s * 8 : s * 8 + 8, :] = last[s]
    end[...] = state[...]
    for g in range(groups):
        total = sum(ys[pl.ds(j * groups + g, length, stride=8), :] for j in range(copies))
        total = total + skip[...] * act[g, 0]
        y[g, 0] = total
        opened = gate[g, 0]
        low = (total * (opened * jax.nn.sigmoid(opened))).astype(BF)
        gated[g, 0] = low
        for m in range(bias.shape[0]):
            cols = slice(m * lanes, (m + 1) * lanes)
            spread_gated[places[g], 0, :, cols] = low * mask[g, 0, :, m : m + 1].astype(BF)


def back_kernel(
    groups, length, states, top, blocks, table, starts, act, picked, mask, pre, read_grad, prior,
    begun, rate, widen, dt, bias, skip, pick_b, pick_c, *refs,
):
    act_grad, picked_grad, left, rate_grad, dt_grad, bias_grad, skip_grad = refs[-20:-13]
    sf, du, gy, bc, wt, ft, pb, pc, res, carry, held, ex, step = refs[-13:]
    copies, count = 8 // groups, rate.shape[0] // 8
    lanes = rate.shape[1]
    modes = bias.shape[0]
    rank = dt.shape[0]
    i = pl.program_id(0)

    @pl.when(i == 0)
    def _():
        carry[...] = begun[0 : count * 8, :]
        held[...] = begun[count * 8 :, :]
        rate_grad[...] = jnp.zeros_like(rate_grad)
        dt_grad[...] = jnp.zeros_like(dt_grad)
        bias_grad[...] = jnp.zeros_like(bias_grad)
        skip_grad[...] = jnp.zeros_like(skip_grad)

    for g in range(groups):
        step[g] = softplus(pre[g, 0])
    lay_out(
        groups, length, states, (top - i) * length, starts, step, act, picked, read_grad, sf, du, bc, gy
    )
    spread_lanes(bc, widen, ex)
    rates = [rate[s * 8 : s * 8 + 8, :] for s in range(count)]

    def one(k, loop):
        p = length - 1 - k
        row = pl.ds(pl.multiple_of(p * 8, 8), 8)
        step_p, drive_p, grad_p = sf[row, :], du[row, :], gy[row, :]
        carried, state, total = loop
        weight_sum, fade_sum = None, None
        out_c, out_h, out_r = [], [], []
        for s in range(count):
            before = prior[pl.ds(pl.multiple_of((p * count + s) * 8, 8), 8), :]
            cols = slice(s * lanes, (s + 1) * lanes)
            e = grad_p * ex[row, (count + s) * lanes : (count + s + 1) * lanes] + carried[s]
            pc[row, cols] = grad_p * state[s]
            pb[row, cols] = e * drive_p
            term = e * ex[row, cols]
            passed = e * jnp.exp2(step_p * rates[s])
            decay = passed * before
            fade_term = decay * rates[s]
            weight_sum = term if weight_sum is None else weight_sum + term
            fade_sum = fade_term if fade_sum is None else fade_sum + fade_term
            out_c.append(passed)
            out_h.append(before)
            out_r.append(total[s] + decay * step_p)
        wt[row, :] = weight_sum
        ft[row, :] = fade_sum
        return tuple(out_c), tuple(out_h), tuple(out_r)

    def parts(ref):
        return tuple(ref[s * 8 : s * 8 + 8, :] for s in range(count))

    c, h, r = lax.fori_loop(
        0, length, one, (parts(carry), parts(held), parts(rate_grad)), unroll=2
    )
    for s in range(count):
        carry[s * 8 : s * 8 + 8, :] = c[s]
        held[s * 8 : s * 8 + 8, :] = h[s]
        rate_grad[s * 8 : s * 8 + 8, :] = r[s]
    left[0 : count * 8, :] = carry[...]
    left[count * 8 :, :] = held[...]

    @pl.loop(0, res.shape[0] // 128)
    def _(n):
        row = pl.ds(pl.multiple_of(n * 128, 128), 128)
        res[row, :] = dot(pb[row, :].astype(BF), pick_b[...]) + dot(
            pc[row, :].astype(BF), pick_c[...]
        )

    lane = lax.broadcasted_iota(jnp.int32, (1, 128), 1)
    owner = lane % states // count
    for g in range(groups):
        rows = [pl.ds(j * groups + g, length, stride=8) for j in range(copies)]
        weighted = sum(wt[row, :] for row in rows)
        faded = sum(ft[row, :] for row in rows) * (1.0 / LOG2E)
        chosen = sum(jnp.where(owner == j, res[rows[j], :], 0.0) for j in range(copies))
        grad_y, u = read_grad[g, 0], act[g, 0]
        act_grad[g, 0] = skip[...] * grad_y + step[g] * weighted
        pre_grad = (u * weighted + faded) * jax.nn.sigmoid(pre[g, 0])
        skip_grad[...] += jnp.sum(grad_y * u, axis=0, keepdims=True)
        rank_grad = None
        for m in range(modes):
            own = pre_grad * mask[g, 0, :, m : m + 1]
            bias_grad[m : m + 1, :] += jnp.sum(own, axis=0, keepdims=True)
            own = own.astype(BF)
            cols = slice(m * lanes, (m + 1) * lanes)
            term = dot_t(own, dt[:, cols])
            rank_grad = term if rank_grad is None else rank_grad + term
            dt_grad[:, cols] += t_dot(picked[g, 0, 0:length, :], own)
        picked_grad[g, 0, 0:length, :] = rank_grad
        picked_grad[g, 0, length:, :] = packed(chosen[:, 0 : 2 * states], 2 * states)


def spread_lanes(source, widen, target):

    @pl.loop(0, source.shape[0] // 128)
    def _(n):
        row = pl.ds(pl.multiple_of(n * 128, 128), 128)
        target[row, :] = dot(source[row, :].astype(BF), widen[...])


def widening(states, count, lanes):
    ones = np.zeros((2, 2, states, 2 * count * lanes), np.float32)
    for kind in range(2):
        for s in range(states):
            block = kind * count + s % count
            ones[:, kind, s, block * lanes : (block + 1) * lanes] = 1
    return jnp.asarray(ones.reshape(4 * states, -1), BF)


def picking(states, count, lanes):
    ones = np.zeros((2, count * lanes, 128), np.float32)
    for kind in range(2):
        for s in range(states):
            at = s % count
            ones[kind, at * lanes : (at + 1) * lanes, kind * states + s] = 1
    return jnp.asarray(ones[0], BF), jnp.asarray(ones[1], BF)


def conv_kernel(groups, length, table, starts, x, mask, taps, base, xproj, v, act, part, tail, ext):
    i = pl.program_id(0)

    @pl.when(i == 0)
    def _():
        tail[...] = jnp.zeros_like(tail)

    modes = mask.shape[3]
    width = xproj.shape[1] // modes
    position = i * length + lax.broadcasted_iota(jnp.int32, (length, 1), 0)
    for g in range(groups):
        begin = jnp.where(position >= starts[g], starts[g], 0)
        ext[0:8, :] = tail[g]
        ext[8 : 8 + length, :] = x[g, 0]
        tail[g] = x[g, 0, length - 8 : length, :]
        total = base[...]
        for k in range(4):
            valid = (position - 3 + k >= begin).astype(F32)
            total = total + taps[k : k + 1, :] * ext[5 + k : 5 + k + length, :] * valid
        v[g, 0] = total
        active = total * jax.nn.sigmoid(total)
        act[g, 0] = active
        product = dot(active.astype(BF), xproj[...])
        chosen = sum(
            product[:, m * width : (m + 1) * width] * mask[g, 0, :, m : m + 1] for m in range(modes)
        )
        part[g, 0, 0:length, :] = chosen[:, 0:128]
        part[g, 0, length:, :] = packed(chosen[:, 128:], width - 128)


def conv_back_kernel(
    groups, length, blocks, table, starts, grad, sel_grad, v, act, x, mask, taps, xproj, *refs,
):
    x_grad, tap_grad, base_grad, weight_grad, head, ext = refs[-6:]
    i = pl.program_id(0)

    @pl.when(i == 0)
    def _():
        head[...] = jnp.zeros_like(head)
        weight_grad[...] = jnp.zeros_like(weight_grad)
        tap_grad[...] = jnp.zeros_like(tap_grad)
        base_grad[...] = jnp.zeros_like(base_grad)

    modes = mask.shape[3]
    width = xproj.shape[1] // modes
    position = (blocks - 1 - i) * length + lax.broadcasted_iota(jnp.int32, (length, 1), 0)
    for g in range(groups):
        chosen = jnp.concatenate(
            [
                sel_grad[g, 0, 0:length, :].astype(F32),
                unpacked(sel_grad[g, 0, length:, :], width - 128),
            ],
            axis=1,
        ).astype(BF)
        masked = [chosen * mask[g, 0, :, m : m + 1].astype(BF) for m in range(modes)]
        act_grad = grad[g, 0]
        low = act[g, 0].astype(BF)
        for m in range(modes):
            cols = slice(m * width, (m + 1) * width)
            act_grad = act_grad + dot_t(masked[m], xproj[:, cols])
            weight_grad[:, cols] += t_dot(low, masked[m])
        v_grad = act_grad * silu_slope(v[g, 0])
        ext[0:length, :] = v_grad
        ext[length : length + 8, :] = head[g]
        head[g] = v_grad[0:8, :]
        base_grad[...] += jnp.sum(v_grad, axis=0, keepdims=True)
        total = None
        for k in range(4):
            crosses = (position < starts[g]) & (position + 3 - k >= starts[g])
            shifted = jnp.where(crosses, 0.0, ext[3 - k : 3 - k + length, :])
            term = taps[k : k + 1, :] * shifted
            total = term if total is None else total + term
            tap_grad[k : k + 1, :] += jnp.sum(x[g, 0] * shifted, axis=0, keepdims=True)
        total = total.astype(BF)
        lanes = total.shape[1]
        for m in range(modes):
            x_grad[g, 0, :, m * lanes : (m + 1) * lanes] = total * mask[g, 0, :, m : m + 1].astype(BF)


def inproj_kernel(count, *refs):
    pieces, (gain, weight, mask), (normed, proj) = refs[:count], refs[count : count + 3], refs[-2:]
    rows = mask.shape[1] // count
    for n in range(count):
        x = pieces[n][0:rows, :].astype(F32)
        scale = lax.rsqrt(jnp.mean(x * x, axis=1, keepdims=True) + EPS)
        normed[0, n * rows : (n + 1) * rows, :] = (x * scale * gain[...]).astype(BF)
    product = dot(normed[0], weight[...])
    modes = mask.shape[2]
    width = weight.shape[1] // modes
    proj[0] = sum(
        product[:, m * width : (m + 1) * width] * mask[0, :, m : m + 1] for m in range(modes)
    )


def inproj(at, lots, pieces, gain, weight, mask, so_far):
    tall, width = pieces[0].shape
    count = len(pieces)
    rows = mask.shape[1] // count
    modes = mask.shape[2]
    columns = weight.shape[1] // modes
    here = lambda i: (at, 0, 0)
    size = count * rows
    full = lambda shape: pl.BlockSpec(shape, lambda i: (0,) * len(shape))
    aliases = {} if so_far is None else {count + 3: 0, count + 4: 1}
    return pl.pallas_call(
        functools.partial(inproj_kernel, count),
        grid=(1,),
        in_specs=[full((tall, width))] * count
        + [full((1, width)), full(weight.shape), pl.BlockSpec((1, size, modes), here)]
        + [pl.BlockSpec(memory_space=pl.ANY)] * len(aliases),
        out_specs=[pl.BlockSpec((1, size, width), here), pl.BlockSpec((1, size, columns), here)],
        out_shape=[
            jax.ShapeDtypeStruct((lots, size, width), BF),
            jax.ShapeDtypeStruct((lots, size, columns), F32),
        ],
        input_output_aliases=aliases,
        compiler_params=pltpu.CompilerParams(vmem_limit_bytes=VMEM),
        cost_estimate=pl.CostEstimate(
            flops=2 * size * width * weight.shape[1],
            bytes_accessed=4 * size * width,
            transcendentals=0,
        ),
    )(*pieces, gain, weight, mask, *(so_far or ()))


def conv(table, starts, x, mask, taps, base, xproj):
    groups, blocks, length, lanes = x.shape
    modes = mask.shape[3]
    width = xproj.shape[1] // modes
    at = lambda i, t, b: (0, t[i], 0, 0)
    flat = lambda i, t, b: (0, 0)
    block = pl.BlockSpec((groups, 1, length, lanes), at)
    return pl.pallas_call(
        functools.partial(conv_kernel, groups, length),
        grid_spec=pltpu.PrefetchScalarGridSpec(
            num_scalar_prefetch=2,
            grid=(blocks,),
            in_specs=[
                block,
                pl.BlockSpec((groups, 1, length, modes), at),
                pl.BlockSpec(taps.shape, flat),
                pl.BlockSpec(base.shape, flat),
                pl.BlockSpec(xproj.shape, flat),
            ],
            out_specs=[block, block, pl.BlockSpec((groups, 1, length * width // 128, 128), at)],
            scratch_shapes=[
                pltpu.VMEM((groups, 8, lanes), F32),
                pltpu.VMEM((length + 8, lanes), F32),
            ],
        ),
        out_shape=[
            jax.ShapeDtypeStruct(x.shape, F32),
            jax.ShapeDtypeStruct(x.shape, F32),
            jax.ShapeDtypeStruct((groups, blocks, length * width // 128, 128), F32),
        ],
        compiler_params=pltpu.CompilerParams(vmem_limit_bytes=VMEM),
    )(table, starts, x, mask, taps, base, xproj)


def conv_back(table, starts, grad, sel_grad, v, act, x, mask, taps, xproj, before):
    groups, blocks, length, lanes = x.shape
    modes = mask.shape[3]
    width = xproj.shape[1] // modes
    at = lambda i, t, b: (0, t[blocks - 1 - i], 0, 0)
    flat = lambda i, t, b: (0, 0)
    block = pl.BlockSpec((groups, 1, length, lanes), at)
    return pl.pallas_call(
        functools.partial(conv_back_kernel, groups, length, blocks),
        grid_spec=pltpu.PrefetchScalarGridSpec(
            num_scalar_prefetch=2,
            grid=(blocks,),
            in_specs=[
                block,
                pl.BlockSpec((groups, 1, length * width // 128, 128), at),
                block,
                block,
                block,
                pl.BlockSpec((groups, 1, length, modes), at),
                pl.BlockSpec(taps.shape, flat),
                pl.BlockSpec(xproj.shape, flat),
            ]
            + [pl.BlockSpec(memory_space=pl.ANY)] * len(before),
            out_specs=[
                pl.BlockSpec((groups, 1, length, modes * lanes), at),
                pl.BlockSpec((8, lanes), flat),
                pl.BlockSpec((1, lanes), flat),
                pl.BlockSpec(xproj.shape, flat),
            ],
            scratch_shapes=[
                pltpu.VMEM((groups, 8, lanes), F32),
                pltpu.VMEM((length + 8, lanes), F32),
            ],
        ),
        out_shape=[
            jax.ShapeDtypeStruct((groups, blocks, length, modes * lanes), BF),
            jax.ShapeDtypeStruct((8, lanes), F32),
            jax.ShapeDtypeStruct((1, lanes), F32),
            jax.ShapeDtypeStruct(xproj.shape, F32),
        ],
        compiler_params=pltpu.CompilerParams(vmem_limit_bytes=VMEM),
    )(table, starts, grad, sel_grad, v, act, x, mask, taps, xproj, *before)


def flat(array):
    return pl.BlockSpec(array.shape, lambda i, *_: (0,) * array.ndim)


def scan(table, starts, places, act, picked, mask, gate, rate, dt, bias, skip, states):
    groups, blocks, length, lanes = act.shape
    total = blocks * length
    count = rate.shape[0] // 8
    at = lambda i, t, b, p: (0, t[i], 0, 0)
    modes = bias.shape[0]
    block = lambda a: pl.BlockSpec((groups, 1) + a.shape[2:], at)
    widen = widening(states, count, lanes)
    tall = pltpu.VMEM((length * 8, lanes), F32)
    like = jax.ShapeDtypeStruct(act.shape, F32)
    return pl.pallas_call(
        functools.partial(scan_kernel, groups, length, states),
        grid_spec=pltpu.PrefetchScalarGridSpec(
            num_scalar_prefetch=3,
            grid=(blocks,),
            in_specs=[block(a) for a in (act, picked, mask, gate)]
            + [flat(a) for a in (rate, widen, dt, bias, skip)],
            out_specs=[
                block(act),
                block(act),
                pl.BlockSpec((groups, 1, length, modes * lanes), lambda i, t, b, p: (0, i, 0, 0)),
                block(act),
                pl.BlockSpec((length * count * 8, lanes), lambda i, t, b, p: (i, 0)),
                flat(rate),
            ],
            scratch_shapes=[
                tall,
                tall,
                pltpu.VMEM((length * 8, 4 * states), F32),
                tall,
                pltpu.VMEM((count * 8, lanes), F32),
                pltpu.VMEM((length * 8, 2 * count * lanes), F32),
            ],
        ),
        out_shape=[
            like,
            jax.ShapeDtypeStruct(act.shape, BF),
            jax.ShapeDtypeStruct((groups, blocks, length, modes * lanes), BF),
            like,
            jax.ShapeDtypeStruct((total * count * 8, lanes), F32),
            jax.ShapeDtypeStruct((count * 8, lanes), F32),
        ],
        compiler_params=pltpu.CompilerParams(vmem_limit_bytes=VMEM),
        cost_estimate=pl.CostEstimate(flops=10**10, bytes_accessed=10**8, transcendentals=0),
    )(table, starts, places, act, picked, mask, gate, rate, widen, dt, bias, skip)


def scan_back(
    first, last, table, starts, act, picked, mask, pre, read_grad, prior, begun, rate, dt, bias,
    skip, states, so_far, before,
):
    groups, blocks, length, lanes = act.shape
    count = rate.shape[0] // 8
    rank = dt.shape[0]
    modes = bias.shape[0]
    at = lambda i, t, b: (0, t[last - 1 - i], 0, 0)
    block = lambda a: pl.BlockSpec((groups, 1) + a.shape[2:], at)
    widen = widening(states, count, lanes)
    pick_b, pick_c = picking(states, count, lanes)
    tall = pltpu.VMEM((length * 8, lanes), F32)
    wide = pltpu.VMEM((length * 8, count * lanes), F32)
    tables = pltpu.VMEM((count * 8, lanes), F32)
    shapes = [
        jax.ShapeDtypeStruct(act.shape, F32),
        jax.ShapeDtypeStruct((groups, blocks, length + length * 2 * states // 128, 128), F32),
        jax.ShapeDtypeStruct((2 * count * 8, lanes), F32),
        jax.ShapeDtypeStruct((count * 8, lanes), F32),
        jax.ShapeDtypeStruct((rank, modes * lanes), F32),
        jax.ShapeDtypeStruct((8, lanes), F32),
        jax.ShapeDtypeStruct((1, lanes), F32),
    ]
    loaded = (begun, rate, widen, dt, bias, skip, pick_b, pick_c)
    extra = tuple(so_far or ()) + tuple(before)
    at_input = 2 + 6 + len(loaded)
    return pl.pallas_call(
        functools.partial(back_kernel, groups, length, states, last - 1, blocks),
        grid_spec=pltpu.PrefetchScalarGridSpec(
            num_scalar_prefetch=2,
            grid=(last - first,),
            in_specs=[block(a) for a in (act, picked, mask, pre, read_grad)]
            + [pl.BlockSpec((length * count * 8, lanes), lambda i, t, b: (last - 1 - i, 0))]
            + [flat(a) for a in loaded]
            + [pl.BlockSpec(memory_space=pl.ANY)] * len(extra),
            out_specs=[block(shapes[0]), block(shapes[1])] + [flat(a) for a in shapes[2:]],
            scratch_shapes=[
                tall, tall, tall, pltpu.VMEM((length * 8, 4 * states), F32), tall, tall, wide, wide,
                pltpu.VMEM((length * 8, 128), F32),
                tables,
                tables,
                pltpu.VMEM((length * 8, 2 * count * lanes), F32),
                pltpu.VMEM((groups, length, lanes), F32),
            ],
        ),
        out_shape=shapes,
        input_output_aliases={at_input: 0, at_input + 1: 1} if so_far else {},
        compiler_params=pltpu.CompilerParams(vmem_limit_bytes=VMEM),
        cost_estimate=pl.CostEstimate(
            flops=10**10, bytes_accessed=25 * 10**6 * (last - first), transcendentals=0
        ),
    )(table, starts, act, picked, mask, pre, read_grad, prior, *loaded, *extra)


def cot_kernel(
    lots_at, spans_at, cots, out_rows, mask, gated, read, gate, read_grad, gate_grad, weight_grad, whole
):
    count = spans_at.shape[0]
    rows = whole.shape[0] // count

    @pl.when(pl.program_id(0) == 0)
    def _():
        weight_grad[...] = jnp.zeros_like(weight_grad)

    for n in range(count):
        whole[n * rows : (n + 1) * rows, :] = cots[
            0, pl.ds(pl.multiple_of(spans_at[n] * rows, rows), rows), :
        ]
    product = dot_t(whole[...], out_rows[...])
    modes = mask.shape[2]
    lanes = gated.shape[2]
    masks = [mask[0, :, m : m + 1] for m in range(modes)]
    grad = sum(product[:, m * lanes : (m + 1) * lanes] * masks[m] for m in range(modes))
    opened = gate[0]
    read_grad[0] = grad * (opened * jax.nn.sigmoid(opened))
    gate_low = (grad * read[0] * silu_slope(opened)).astype(BF)
    for m in range(modes):
        own = masks[m].astype(BF)
        cols = slice(m * lanes, (m + 1) * lanes)
        gate_grad[0, :, cols] = gate_low * own
        weight_grad[cols, :] += t_dot(gated[0] * own, whole[...])


def cot_part(lots_at, spans_at, cots, out_rows, mask, gated, read, gate):
    lots, size, width = cots.shape
    lanes = gated.shape[2]
    wide = out_rows.shape[0]
    block = lambda w: pl.BlockSpec((1, size, w), lambda i, a, b: (i, 0, 0))
    return pl.pallas_call(
        cot_kernel,
        grid_spec=pltpu.PrefetchScalarGridSpec(
            num_scalar_prefetch=2,
            grid=(lots,),
            in_specs=[pl.BlockSpec((1, size, width), lambda i, a, b: (a[i], 0, 0)), flat(out_rows)]
            + [block(a.shape[2]) for a in (mask, gated, read, gate)],
            out_specs=[block(lanes), block(wide), flat(out_rows)],
            scratch_shapes=[pltpu.VMEM((size, width), BF)],
        ),
        out_shape=[
            jax.ShapeDtypeStruct((lots, size, lanes), F32),
            jax.ShapeDtypeStruct((lots, size, wide), BF),
            jax.ShapeDtypeStruct(out_rows.shape, F32),
        ],
        compiler_params=pltpu.CompilerParams(vmem_limit_bytes=VMEM),
        cost_estimate=pl.CostEstimate(
            flops=4 * lots * size * width * wide, bytes_accessed=3 * lots * size * width, transcendentals=0
        ),
    )(lots_at, spans_at, cots, out_rows, mask, gated, read, gate)


class Dim:

    def __init__(self, axis, stride, size, length):
        self.axis, self.stride, self.size, self.length = axis, stride, size, length

    def here(self):
        return lax.axis_index(self.axis) // self.stride % self.size

    def fetch(self, x, by):
        pairs = []
        for i in range(self.length):
            c = i // self.stride % self.size
            pairs.append((i + ((c + by) % self.size - c) * self.stride, i))
        return lax.ppermute(x, self.axis, pairs)


def dims_of(chan):
    dims = []
    for axis in chan:
        length = lax.axis_size(axis)
        sizes = []
        rest = length
        if axis == "seq":
            rest //= 2
        radix = 4 if axis == "seq" else 2
        while rest > 1:
            sizes.insert(0, min(radix, rest))
            rest //= sizes[0]
        if axis == "seq":
            sizes.append(2)
        stride = length
        for size in sizes:
            stride //= size
            dims.append(Dim(axis, stride, size, length))
    return dims


def gather_pieces(dims, x):
    others, ring, core = dims[:-2], dims[-2], dims[-1]
    got = {}
    first = x
    for k in range(ring.size):
        if k:
            first = ring.fetch(first, 1)
        order = list(range(len(others)))
        if k % 2:
            order.reverse()
        held = {(0,) * len(others): first}
        for d in order:
            for at, block in list(held.items()):
                for r in range(1, others[d].size):
                    block = others[d].fetch(block, 1)
                    held[at[:d] + (r,) + at[d + 1 :]] = block
        for at, block in held.items():
            got[at + (k, 0)] = block
            got[at + (k, 1)] = core.fetch(block, 1)
    return [got[at] for at in sorted(got)]


def pairs_of(dims):
    return [d.size for d in dims[:-2]] == [2, 2]


def gather_stage(dims, x, d):
    got = [x] + [dims[d].fetch(x, r) for r in range(1, dims[d].size)]
    return jnp.concatenate(got, axis=d)


def gather_small(dims, x):
    x = x.reshape((1,) * len(dims) + x.shape)
    x = gather_stage(dims, x, len(dims) - 2)
    if pairs_of(dims):
        halves = jnp.split(x, 2, axis=len(dims))
        halves = [gather_stage(dims, h, n) for n, h in enumerate(halves)]
        halves = [gather_stage(dims, h, 1 - n) for n, h in enumerate(halves)]
        x = jnp.concatenate(halves, axis=len(dims))
    else:
        for d in range(len(dims) - 2):
            x = gather_stage(dims, x, d)
    return gather_stage(dims, x, len(dims) - 1)


def reduce_stage(dims, x, d, kind):
    block = [lax.slice_in_dim(x, r, r + 1, axis=d) for r in range(dims[d].size)]
    return add_up(
        [block[0]] + [dims[d].fetch(block[r].astype(kind), -r) for r in range(1, len(block))]
    )


def reduce_small(dims, x):
    x = reduce_stage(dims, x, len(dims) - 1, F32)
    if pairs_of(dims):
        halves = jnp.split(x, 2, axis=len(dims))
        halves = [reduce_stage(dims, h, n, BF) for n, h in enumerate(halves)]
        halves = [reduce_stage(dims, h, 1 - n, F32) for n, h in enumerate(halves)]
        x = jnp.concatenate(halves, axis=len(dims))
    else:
        for d in range(len(dims) - 2):
            x = reduce_stage(dims, x, d, F32 if d else BF)
    x = reduce_stage(dims, x, len(dims) - 2, F32)
    return x.reshape(x.shape[len(dims) :])


def add_up(parts):
    return sum(p.astype(F32) for p in parts)


def reduce_parts(dims, x, turn, stages):
    order = list(range(len(dims) - 2))
    if turn % 2:
        order.reverse()
    order = [len(dims) - 1] + order + [len(dims) - 2]
    for n, d in enumerate(order):
        size = dims[d].size
        block = [lax.slice_in_dim(x, r, r + 1, axis=d) for r in range(size)]
        if size == 2:
            x = add_up([block[0]] + [dims[d].fetch(block[r], -r) for r in range(1, size)])
        else:
            moving = block[size - 1]
            for r in range(size - 2, -1, -1):
                x = add_up([block[r], dims[d].fetch(moving, -1)])
                moving = x.astype(BF)
        if n < len(order) - 1:
            x = x.astype(BF)
            stages.append((n, x))
    return x.reshape(x.shape[len(dims) :])


def on_device(
    chan, held,
    hidden, modality, starts, norm_gain, in_weight, conv_weight, conv_bias, xproj_weight,
    dtproj_weight, step_bias, decay_log, skip_weight, out_weight, cotangent,
):
    def collect(x):
        return lax.all_gather(x, held, axis=0, tiled=True) if held else x

    def exchange(x):
        return lax.all_to_all(x, chan, 0, 0, tiled=True)

    def settle(x):
        return lax.psum_scatter(x, held, scatter_dimension=0, tiled=True) if held else x

    dims = dims_of(chan)
    sizes = tuple(d.size for d in dims)
    parts = math.prod(sizes)
    lots = math.prod(lax.axis_size(a) for a in held) if held else 1
    groups = parts // lax.axis_size("seq")
    rows, width = hidden.shape[1:]
    own = conv_weight.shape[0]
    lanes = own * lots
    rank_rows = dtproj_weight.shape[0]
    rank = rank_rows * parts * lots
    modes = in_weight.shape[1]
    states = decay_log.shape[1]
    mine = hidden[0]
    cot = cotangent[0]

    def shards(w):
        w = w.reshape(w.shape[0], modes, lots, parts, own)
        return jnp.moveaxis(w, 3, 0).reshape(parts, w.shape[0], modes, lanes)

    def to_owners(g, out_rows):
        return settle(g).reshape(parts, out_rows * modes, lanes)

    def returned(g, out_rows):
        g = g.reshape(parts, out_rows, modes, lots, own)
        return jnp.moveaxis(g, 0, 3).reshape(out_rows, modes, lots * parts * own)

    inner = lanes * parts
    blocks = parts // groups
    note = jnp.concatenate([modality[0], starts // 64, starts % 64]).astype(BF)
    note = jnp.pad(note[None], ((0, 15), (0, width - rows - 2)))
    pieces = gather_pieces(dims, jnp.concatenate([mine, note], axis=0))
    aux = jnp.stack([piece[rows, : rows + 2] for piece in pieces]).astype(jnp.int32)
    aux = aux.reshape(groups, blocks, rows + 2)
    begins = aux[:, 0, rows] * 64 + aux[:, 0, rows + 1]
    mode_ids = aux[:, :, :rows]
    room = -norm_gain.shape[0] % lanes
    notes = jnp.broadcast_to(jnp.pad(norm_gain, (0, room)), (parts, norm_gain.shape[0] + room))
    moved = collect(exchange(jnp.concatenate(
        [
            shards(in_weight[:, :, :inner]).reshape(parts, -1, lanes),
            shards(dtproj_weight).reshape(parts, -1, lanes),
            notes.reshape(parts, -1, lanes),
        ],
        axis=1,
    )))
    cut = in_weight.shape[0] * modes
    further = cut + rank_rows * modes
    x_cols = moved[:, :cut].reshape(width, modes * lanes)
    dt_cols = moved[:, cut:further].reshape(rank, modes * lanes)
    gain = moved[:, further:].reshape(parts * lots, -1)[:, : norm_gain.shape[0]]
    gain = gain.reshape(1, width).astype(F32)
    conv_weight, conv_bias, xproj_weight, step_bias, decay_log, skip_weight, out_weight = (
        collect(w)
        for w in (conv_weight, conv_bias, xproj_weight, step_bias, decay_log, skip_weight, out_weight)
    )
    taps = conv_weight.astype(F32).T
    bias = step_bias.astype(F32).T
    skip = skip_weight.astype(F32)[None]
    xproj = xproj_weight.reshape(lanes, -1)
    out_rows = jnp.moveaxis(out_weight, 1, 0).reshape(modes * lanes, width)
    masks = (mode_ids[..., None] == jnp.arange(modes, dtype=jnp.int32)).astype(F32)
    total = parts * rows
    copies = 8 // groups
    count = states // copies
    rate = -jnp.exp(decay_log.astype(F32))
    rates = jnp.moveaxis(rate.T.reshape(copies, count, lanes), 0, 1)
    rates = jnp.repeat(rates.reshape(count * copies, 1, lanes), groups, axis=1).reshape(-1, lanes)
    rates = rates * LOG2E
    order = jnp.zeros((), jnp.int32)
    spans = jnp.arange(blocks, dtype=jnp.int32)
    stride = blocks
    for d in dims:
        if d.axis == "seq":
            stride //= d.size
            order = order * d.size + (spans // stride % d.size - d.here()) % d.size
    table = order

    def placed(some):
        at = jnp.zeros((), jnp.int32)
        stride = math.prod(d.size for d in some)
        names = jnp.arange(stride, dtype=jnp.int32)
        for d in some:
            stride //= d.size
            at = at * d.size + (names // stride % d.size + d.here()) % d.size
        return at.reshape(-1)

    places = placed([d for d in dims if d.axis == "grp"])

    step_pieces = sizes[-1] * sizes[-2]
    lots_in = parts // step_pieces
    in_masks = masks.reshape(lots_in, step_pieces * rows, modes)
    so_far = None
    for n in range(lots_in):
        so_far = inproj(
            n, lots_in, pieces[n * step_pieces : (n + 1) * step_pieces], gain, x_cols, in_masks, so_far
        )
    normed, conv_in = so_far
    cots = lax.all_gather(after(cot, conv_in), chan, axis=0, tiled=True)
    gate_cols = collect(exchange(shards(after(in_weight[:, :, inner:], conv_in))).reshape(
        -1, modes, lanes
    )).reshape(width, modes * lanes)
    normed = normed.reshape(total, width)
    grouped = (groups, blocks, rows, lanes)
    pre_act, act, partial = conv(
        table, begins, conv_in.reshape(grouped), masks, taps, conv_bias.astype(F32)[None], xproj
    )
    picked = reduce_small(dims, partial.reshape(sizes + (-1, 128)))
    low = picked.astype(BF)
    rest = (picked[rows:] - low[rows:].astype(F32)).astype(BF)
    picked = gather_small(dims, jnp.concatenate([low, rest], axis=0))
    picked = picked.reshape(groups, blocks, -1, 128)
    flat_masks = masks.reshape(total, modes)
    gate_in = pick(dot(normed, gate_cols), flat_masks).reshape(grouped)
    read, gated, spread_gated, pre, prior, end = scan(
        table, begins, places, act, picked, masks, gate_in, rates, dt_cols, bias, skip, states
    )

    def scatter(x, weight, dim, stages):
        got = []
        chunk = width // 4
        for n in range(4):
            w = lax.slice_in_dim(weight, n * chunk, (n + 1) * chunk, axis=1 - dim)
            product = dot(x, w, ((1,), (dim,))).astype(BF).reshape(sizes + (rows, chunk))
            got.append(reduce_parts(dims, product, n, stages))
        return jnp.concatenate(got, axis=1)

    branch = dot(spread_gated.reshape(total, modes * lanes), out_rows).astype(BF)
    branch = lax.psum_scatter(branch, chan, scatter_dimension=0, tiled=True)
    output = (mine.astype(F32) + branch.astype(F32)).astype(BF)[None]

    lot = (lots_in, step_pieces * rows, -1)
    read_grad, gate_grad, grad_out_weight = cot_part(
        placed(dims[:-2]), placed(dims[-2:]), cots.reshape(lots_in, -1, width), out_rows,
        in_masks, gated.reshape(lot), read.reshape(lot), gate_in.reshape(lot),
    )
    grad_out_weight = jnp.moveaxis(grad_out_weight.reshape(modes, lanes, width), 0, 1)
    gate_grad = gate_grad.reshape(total, modes * lanes)
    in_rows = in_weight.shape[0]
    grad_gate_cols = exchange(to_owners(t_dot(normed, gate_grad).astype(BF), in_rows))
    begun = jnp.concatenate([jnp.zeros_like(end), end], axis=0)
    cuts = [blocks, 0]
    so_far = None
    sums = []
    for n in range(len(cuts) - 1):
        act_grad, picked_grad, begun, *more = scan_back(
            cuts[n + 1], cuts[n], table, begins, act, picked, masks, pre,
            read_grad.reshape(grouped), prior, begun, rates, dt_cols, bias, skip, states, so_far,
            [],
        )
        so_far = (act_grad, picked_grad)
        sums.append(more)
    rate_grad, grad_dt, grad_bias, grad_skip = (sum(parts_of) for parts_of in zip(*sums))
    rate_grad = rate_grad.reshape(count, copies, groups, lanes).sum(axis=2)
    grad_decay = jnp.moveaxis(rate_grad, 0, 1).reshape(states, lanes).T * rate
    picked_grad = reduce_small(dims, picked_grad.reshape(sizes + (-1, 128))).astype(BF)
    picked_grad = gather_small(dims, picked_grad).reshape(groups, blocks, -1, 128)
    x_grad, tap_grad, base_grad, grad_xproj = conv_back(
        table, begins, act_grad, picked_grad, pre_act, act, conv_in.reshape(grouped), masks, taps,
        xproj, [grad_gate_cols],
    )
    x_grad = x_grad.reshape(total, modes * lanes)
    grad_x_cols = exchange(jnp.concatenate(
        [
            to_owners(t_dot(normed, x_grad).astype(BF), in_rows),
            to_owners(grad_dt.astype(BF), rank_rows),
        ],
        axis=1,
    ))
    grad_dt = returned(grad_x_cols[:, in_rows * modes :], rank_rows).astype(F32)
    grad_x_cols = returned(grad_x_cols[:, : in_rows * modes], in_rows)
    grad_gate_cols = returned(grad_gate_cols, in_rows)
    normed_grad = scatter(
        jnp.concatenate([x_grad, gate_grad], axis=1),
        jnp.concatenate([x_cols, gate_cols], axis=1), 1, [],
    )
    grad_in = jnp.concatenate([grad_x_cols, grad_gate_cols], axis=2).astype(F32)
    grad_gain = jnp.sum(grad_in * in_weight.astype(F32), axis=(1, 2)) / norm_gain.astype(F32)
    xm = mine.astype(F32)
    scale = lax.rsqrt(jnp.mean(xm * xm, axis=1, keepdims=True) + EPS)
    unit = xm * scale
    scaled = normed_grad * gain
    grad_hidden = cotangent[0].astype(F32) + scale * (
        scaled - unit * jnp.mean(scaled * unit, axis=1, keepdims=True)
    )
    return (
        output,
        grad_hidden[None],
        grad_gain,
        grad_in,
        settle(tap_grad[:4].T),
        settle(base_grad[0]),
        settle(grad_xproj.reshape(lanes, modes, -1)),
        grad_dt,
        settle(grad_bias[:modes].T),
        settle(grad_decay),
        settle(grad_skip[0]),
        settle(grad_out_weight),
    )


def solution(mesh):
    both = ("grp", "seq")
    full = mesh.shape["grp"] * mesh.shape["seq"] <= 32
    chan, held = (both, ()) if full else (("seq",), ("grp",))
    row = P(both)
    return jax.shard_map(
        functools.partial(on_device, chan, held),
        mesh=mesh,
        in_specs=(
            P("grp", "seq", None), P("grp", "seq"), P("grp"),
            row, row, row, row, row, row, row, row, row, row,
            P("grp", "seq", None),
        ),
        out_specs=(P("grp", "seq", None), P("grp", "seq", None)) + (row,) * 10,
        check_vma=False,
    )
```

time: 1200 us -> 895 us (0.75)
  blocking collectives: 249 us -> 0 us
  waiting for transfers between devices: 499 us -> 333 us
  starting transfers between devices: 20.3 us -> 113 us
  Pallas kernels: 137 us -> 186 us
  local copies, waits for them, and re-layouts: 79.5 us -> 124 us
  matrix products: 112 us -> 69.1 us
  other arithmetic: 80.6 us -> 46.9 us
    ppermute x0 -> x87, waiting for transfers between devices: none -> 333 us  [fetch(): return lax.ppermute(x, self.axis, pairs)]
    reduce_scatter x2 -> x1, waiting for transfers between devices: 245 us -> 0.02 us  [on_device(): branch = lax.psum_scatter(branch, chan, scatter_dimension=0, tiled=True)]
    unnamed x2 -> x0, blocking collectives: 140 us -> none
    psum x1 -> x0, waiting for transfers between devices: 130 us -> none  [on_device(): picked = lax.psum(pick(dot(act_low, xproj), masks), chan)]
    all_to_all x4, waiting for transfers between devices: 95.5 us -> 0.01 us  [exchange(): return lax.all_to_all(x, chan, 0, 0, tiled=True)]
    ppermute x0 -> x87, starting transfers between devices: none -> 94.8 us  [fetch(): return lax.ppermute(x, self.axis, pairs)]
    psum x1 -> x0, blocking collectives: 68.3 us -> none  [on_device(): lax.psum(jnp.concatenate([dot(pre_low, dt_cols, ((1,), (1,))), sel_grad],...]
    pallas_call x2 -> x9, Pallas kernels: 137 us -> 186 us  [the longest x1 72 us: scan_back(): pl.pallas_call(functools.partial(back_kernel, groups, length, states, las...]
  transfers between devices with their start and end apart: 9 -> 93, of which waited for: 5 -> 46; matrix products, arithmetic and copies ran while one was open for 15% -> 21% of each run, Pallas kernels for 0% -> 18%
where the time goes in v2:
time: 895 us; the launch traced here: 889 us
  waiting for transfers between devices  333 us (37%)
  Pallas kernels  186 us (21%)
  local copies, waits for them, and re-layouts  124 us (14%)
  starting transfers between devices  113 us (13%)
  matrix products  69.1 us (8%)
  other arithmetic  46.9 us (5%)
  between operations  17.4 us (2%)
    ppermute x87, waiting for transfers between devices, fetch(): return lax.ppermute(x, self.axis, pairs)  333 us
    ppermute x87, starting transfers between devices, fetch(): return lax.ppermute(x, self.axis, pairs)  94.8 us
    pallas_call x1, Pallas kernels, scan_back(): pl.pallas_call(functools.partial(back_kernel, groups, length, states, las...  72 us
    dot_general x8, matrix products, dot(): return lax.dot_general(a, b, (dims, ((), ())), preferred_element_type=F32)  69.1 us
    pallas_call x1, Pallas kernels, scan(): pl.pallas_call(functools.partial(scan_kernel, groups, length, states), gr...  40.4 us
    unnamed x235, local copies, waits for them, and re-layouts  40.2 us
    pallas_call x4, Pallas kernels, inproj(): pl.pallas_call(functools.partial(inproj_kernel, count), grid=(1,), in_spe...  23.5 us
    pallas_call x1, Pallas kernels, cot_part(): pl.pallas_call(cot_kernel, grid_spec=pltpu.PrefetchScalarGridSpec(num_sca...  21.6 us
  transfers between devices with their start and end apart: 93, of which 46 were waited for; matrix products, arithmetic and copies ran while one was open for 21% of the time, Pallas kernels for 18%

profile of v2, /device:TPU:0, one launch (start us, length us, event | category | flops | bytes accessed | tf_op | source)
XLA Modules:
  0.0 888.5 jit_solution(9158814558721741601)
XLA Ops:
  17.8 8.2 collective-permute-done.15.refs_0_
  33.3 5.1 all-to-all-start
  45.9 23.4 %collective-permute-done.17.refs_2_ = bf16[144,2048]{1,0:T(8,128)(2,1)S(1)} collective-permute-done((bf16[144,2048]{1,0:T(8,128)(2,1)S(1)}, bf16[144,2048]{1,0:T(8,128)(2,1)S(1)}, u32[]{:S(2)}, u32[]{:S(2)}) %collective-permute-start.17) | collective-permute-done | bytes 589856 | tf_op jit(solution)/shard_map/ppermute | solution.py:678
  70.2 11.9 %collective-permute-done.3.refs_4_ = bf16[144,2048]{1,0:T(8,128)(2,1)S(1)} collective-permute-done((bf16[144,2048]{1,0:T(8,128)(2,1)S(1)}, bf16[144,2048]{1,0:T(8,128)(2,1)S(1)}, u32[]{:S(2)}, u32[]{:S(2)}) %collective-permute-start.3) | collective-permute-done | bytes 589856 | tf_op jit(solution)/shard_map/ppermute | solution.py:678
  87.7 18.1 %collective-permute-done.5.refs_6_ = bf16[144,2048]{1,0:T(8,128)(2,1)S(1)} collective-permute-done((bf16[144,2048]{1,0:T(8,128)(2,1)S(1)}, bf16[144,2048]{1,0:T(8,128)(2,1)S(1)}, u32[]{:S(2)}, u32[]{:S(2)}) %collective-permute-start.5) | collective-permute-done | bytes 589856 | tf_op jit(solution)/shard_map/ppermute | solution.py:678
  109.6 12.5 %collective-permute-done.13.refs_6_ = bf16[144,2048]{1,0:T(8,128)(2,1)S(1)} collective-permute-done((bf16[144,2048]{1,0:T(8,128)(2,1)S(1)}, bf16[144,2048]{1,0:T(8,128)(2,1)S(1)}, u32[]{:S(2)}, u32[]{:S(2)}) %collective-permute-start.13) | collective-permute-done | bytes 589856 | tf_op jit(solution)/shard_map/ppermute | solution.py:678
  123.6 10.1 %collective-permute-done.27.refs_4_ = bf16[144,2048]{1,0:T(8,128)(2,1)S(1)} collective-permute-done((bf16[144,2048]{1,0:T(8,128)(2,1)S(1)}, bf16[144,2048]{1,0:T(8,128)(2,1)S(1)}, u32[]{:S(2)}, u32[]{:S(2)}) %collective-permute-start.27) | collective-permute-done | bytes 589856 | tf_op jit(solution)/shard_map/ppermute | solution.py:678
  183.3 5.3 stack.3
  194.7 5.9 shard_map.265
  200.7 5.7 shard_map.266
  206.5 5.8 shard_map.267
  212.4 6.0 shard_map.268
  224.4 11.5 %shard_map.269 = (f32[4,8,128,128]{3,2,1,0:T(8,128)S(1)}, f32[4,8,128,128]{3,2,1,0:T(8,128)S(1)}, f32[4,8,160,128]{3,2,1,0:T(8,128)}) custom-call(s32[8]{0:T(128)S(1)} %fusion.45.table, s32[4]{0:T(128)S(1)} %add_bitcast_fusion.starts, f32[4,8,128,128]{3,2,1,0:T(8,128)} %bitcast.180, f32[4,8,128,3]{3,2,1,0:T(8,128)} %fusion.3.mask, ...), custom_call_target="tpu_custom_call" | custom-call | tf_op jit(solution)/shard_map/pallas_call | solution.py:432
  271.9 10.8 %collective-permute-done.37 = f32[1,1,1,1,160,128]{5,4,3,2,1,0:T(8,128)S(1)} collective-permute-done((f32[1,1,1,1,160,128]{5,4,3,2,1,0:T(8,128)S(1)}, f32[1,1,1,1,160,128]{5,4,3,2,1,0:T(8,128)S(1)}, u32[]{:S(2)}, u32[]{:S(2)}) %collective-permute-start.37) | collective-permute-done | bytes 81952 | tf_op jit(solution)/shard_map/ppermute | solution.py:678
  287.8 24.4 %collective-permute-done.41 = bf16[1,1,1,1,192,128]{5,4,3,2,1,0:T(8,128)(2,1)S(1)} collective-permute-done((bf16[1,1,1,1,192,128]{5,4,3,2,1,0:T(8,128)(2,1)S(1)}, bf16[1,1,1,1,192,128]{5,4,3,2,1,0:T(8,128)(2,1)S(1)}, u32[]{:S(2)}, u32[]{:S(2)}) %collective-permute-start.41) | collective-permute-done | bytes 49184 | tf_op jit(solution)/shard_map/ppermute | solution.py:678
  312.1 39.7 %collective-permute-done.40 = bf16[1,1,1,1,192,128]{5,4,3,2,1,0:T(8,128)(2,1)S(1)} collective-permute-done((bf16[1,1,1,1,192,128]{5,4,3,2,1,0:T(8,128)(2,1)S(1)}, bf16[1,1,1,1,192,128]{5,4,3,2,1,0:T(8,128)(2,1)S(1)}, u32[]{:S(2)}, u32[]{:S(2)}) %collective-permute-start.40) | collective-permute-done | bytes 49184 | tf_op jit(solution)/shard_map/ppermute | solution.py:678
  370.5 12.7 %fusion.4 = f32[4096,384]{1,0:T(8,128)S(1)} fusion(bf16[4096,2048]{1,0:T(8,128)(2,1)} %bitcast.176, bf16[256,8,3,128]{3,2,1,0:T(4,128)(2,1)S(1)} %bitcast.183), kind=kOutput, calls=%fused_computation.30 | convolution fusion | flops 6442450944 | bytes 24641536 | tf_op jit(solution)/shard_map/dot_general | solution.py:21
  387.2 40.4 %shard_map.270 = (f32[4,8,128,128]{3,2,1,0:T(8,128)S(1)}, bf16[4,8,128,128]{3,2,1,0:T(8,128)(2,1)S(1)}, bf16[4,8,128,384]{3,2,1,0:T(8,128)(2,1)}, f32[4,8,128,12...) custom-call(s32[8]{0:T(128)S(1)} %fusion.45.table, s32[4]{0:T(128)S(1)} %add_bitcast_fusion.starts, ...), custom_call_target="tpu_custom_call" | custom-call | flops 10000000000 | bytes 100000000 | tf_op jit(solution)/shard_map/pallas_call | solution.py:517
  429.9 14.2 %convolution_convert_fusion = bf16[4096,2048]{1,0:T(8,128)(2,1)} fusion(bf16[4096,384]{1,0:T(8,128)(2,1)} %bitcast.232, bf16[384,2048]{1,0:T(8,128)(2,1)S(1)} %bitcast.172), kind=kOutput, calls=%fused_computation | convolution fusion | flops 6450839552 | bytes 21495808 | tf_op jit(solution)/shard_map/dot_general | solution.py:21
  446.8 21.6 %shard_map.271 = (f32[4,1024,128]{2,1,0:T(8,128)S(1)}, bf16[4,1024,384]{2,1,0:T(8,128)(2,1)}, f32[384,2048]{1,0:T(8,128)}) custom-call(s32[4]{0:T(128)S(1)} %fusion.47.places.lots_at, s32[8]{0:T(128)S(1)} %fusion.48.spans_at, bf16[4,1024,2048]{2,1,0:T(8,128)(2,1)} %bitcast.219, bf16[384,2048]{1,0:T(8,128)(2,1)S(1)} %bitcast.173, ...), custom_call_target="tpu_custom_call" | custom-call | flops 12884901888 | bytes 25165824 | tf_op jit(solution)/shard_map/pallas_call | solution.py:643
  469.8 72.0 %shard_map.272 = (f32[4,8,128,128]{3,2,1,0:T(8,128)S(1)}, f32[4,8,160,128]{3,2,1,0:T(8,128)}, f32[128,128]{1,0:T(8,128)}, f32[64,128]{1,0:T(8,128)S(1)}, f32[128...) custom-call(s32[8]{0:T(128)S(1)} %fusion.45.table, s32[4]{0:T(128)S(1)} %add_bitcast_fusion.starts, ...), custom_call_target="tpu_custom_call" | custom-call | flops 10000000000 | bytes 200000000 | tf_op jit(solution)/shard_map/pallas_call | solution.py:581
  548.9 12.5 %bitcast_convert_fusion = bf16[2048,384]{1,0:T(8,128)(2,1)S(1)} fusion(bf16[4,1024,2048]{2,1,0:T(8,128)(2,1)} %get-tuple-element.51, bf16[4,1024,384]{2,1,0:T(8,128)(2,1)S(1)} %copy-done.107), kind=kOutput, calls=%fused_computation.12 | convolution fusion | flops 6443237376 | bytes 21495808 | tf_op jit(solution)/shard_map/dot_general | solution.py:21
  571.9 17.0 %collective-permute-done.50 = bf16[2,1,4,1,80,128]{5,4,3,2,1,0:T(8,128)(2,1)S(1)} collective-permute-done((bf16[2,1,4,1,80,128]{5,4,3,2,1,0:T(8,128)(2,1)S(1)}, bf16[2,1,4,1,80,128]{5,4,3,2,1,0:T(8,128)(2,1)S(1)}, u32[]{:S(2)}, u32[]{:S(2)}) %collective-permute-start.50) | collective-permute-done | bytes 163872 | tf_op jit(solution)/shard_map/ppermute | solution.py:678
  601.5 23.4 %collective-permute-done.52 = f32[1,1,1,1,160,128]{5,4,3,2,1,0:T(8,128)S(1)} collective-permute-done((f32[1,1,1,1,160,128]{5,4,3,2,1,0:T(8,128)S(1)}, f32[1,1,1,1,160,128]{5,4,3,2,1,0:T(8,128)S(1)}, u32[]{:S(2)}, u32[]{:S(2)}) %collective-permute-start.52) | collective-permute-done | bytes 81952 | tf_op jit(solution)/shard_map/ppermute | solution.py:678
  624.9 17.9 %collective-permute-done.53 = f32[1,1,1,1,160,128]{5,4,3,2,1,0:T(8,128)S(1)} collective-permute-done((f32[1,1,1,1,160,128]{5,4,3,2,1,0:T(8,128)S(1)}, f32[1,1,1,1,160,128]{5,4,3,2,1,0:T(8,128)S(1)}, u32[]{:S(2)}, u32[]{:S(2)}) %collective-permute-start.53) | collective-permute-done | bytes 81952 | tf_op jit(solution)/shard_map/ppermute | solution.py:678
  675.3 17.3 %shard_map.273 = (bf16[4,8,128,384]{3,2,1,0:T(8,128)(2,1)}, f32[8,128]{1,0:T(8,128)S(1)}, f32[1,128]{1,0:T(1,128)}, f32[128,480]{1,0:T(8,128)S(1)}) custom-call(s32[8]{0:T(128)S(1)} %fusion.45.table, s32[4]{0:T(128)S(1)} %add_bitcast_fusion.starts, f32[4,8,128,128]{3,2,1,0:T(8,128)S(1)} %copy-done.3, bf16[4,8,160,128]{3,2,1,0:T(8,128)(2,1)S(1)} %bitcast.167, ...), custom_call_target="tpu_custom_call" | custom-call | tf_op jit(solution)/shard_map/pallas_call | solution.py:466
  692.7 5.4 convolution_convert_fusion.3
  716.4 6.6 convolution_convert_fusion.4
  727.1 10.2 %convolution_convert_fusion.5 = bf16[2048,384]{1,0:T(8,128)(2,1)} fusion(bf16[4096,2048]{1,0:T(8,128)(2,1)S(1)} %bitcast.179, bf16[4096,384]{1,0:T(8,128)(2,1)S(1)} %bitcast.224), kind=kOutput, calls=%fused_computation.13 | convolution fusion | flops 6443237376 | bytes 21495808 | tf_op jit(solution)/shard_map/dot_general | solution.py:21
  769.6 23.7 %collective-permute-done.70 = bf16[2,1,4,1,128,512]{5,4,3,2,1,0:T(8,128)(2,1)S(1)} collective-permute-done((bf16[2,1,4,1,128,512]{5,4,3,2,1,0:T(8,128)(2,1)S(1)}, bf16[2,1,4,1,128,512]{5,4,3,2,1,0:T(8,128)(2,1)S(1)}, u32[]{:S(2)}, u32[]{:S(2)}) %collective-permute-start.70) | collective-permute-done | bytes 1048608 | tf_op jit(solution)/shard_map/ppermute | solution.py:678
  798.8 18.8 %collective-permute-done.64 = bf16[1,2,4,1,128,512]{5,4,3,2,1,0:T(8,128)(2,1)S(1)} collective-permute-done((bf16[1,2,4,1,128,512]{5,4,3,2,1,0:T(8,128)(2,1)S(1)}, bf16[1,2,4,1,128,512]{5,4,3,2,1,0:T(8,128)(2,1)S(1)}, u32[]{:S(2)}, u32[]{:S(2)}) %collective-permute-start.64) | collective-permute-done | bytes 1048608 | tf_op jit(solution)/shard_map/ppermute | solution.py:678
  830.2 5.6 multiply_reduce_fusion
  (593 shorter events, 347.3 us)
Async XLA Ops:
  33.3 140.1 %all-to-all-start = ((bf16[32,205,128]{2,1,0:T(8,128)(2,1)}), bf16[32,205,128]{2,1,0:T(8,128)(2,1)}, u32[]{:S(2)}, u32[]{:S(2)}) async-start(bf16[32,205,128]{2,1,0:T(8,128)(2,1)} %copy.105), calls=%async_computation | async-start | bytes 3407872 | tf_op jit(solution)/shard_map/all_to_all | solution.py:802
  38.4 405.7 %all-gather.3.cloned.1.call-start = ((), (), s32[]{:S(2)}) async-start(), calls=%async_computation.6 | async-start | bytes 17301504 | tf_op jit(solution)/shard_map/all_gather | solution.py:904
  38.7 30.5 %collective-permute-start.17 = (bf16[144,2048]{1,0:T(8,128)(2,1)S(1)}, bf16[144,2048]{1,0:T(8,128)(2,1)S(1)}, u32[]{:S(2)}, u32[]{:S(2)}) collective-permute-start(bf16[144,2048]{1,0:T(8,128)(2,1)S(1)} %collective-permute-done.1.refs_2_), channel_id=1, source_target_pairs={{16,0},{24,8},{0,16},{8,24},{17,1},{25,9},{1,17},{9,25},{18,2},{26... | collective-permute-start | bytes 1769480 | tf_op jit(solution)/shard_map/ppermute | solution.py:678
  40.4 28.8 %collective-permute-start.9 = (bf16[144,2048]{1,0:T(8,128)(2,1)S(1)}, bf16[144,2048]{1,0:T(8,128)(2,1)S(1)}, u32[]{:S(2)}, u32[]{:S(2)}) collective-permute-start(bf16[144,2048]{1,0:T(8,128)(2,1)S(1)} %collective-permute-done.1.refs_2_), channel_id=1, source_target_pairs={{8,0},{0,8},{24,16},{16,24},{9,1},{1,9},{25,17},{17,25},{10,2},{2,... | collective-permute-start | bytes 1769480 | tf_op jit(solution)/shard_map/ppermute | solution.py:678
  41.9 40.3 %collective-permute-start.3 = (bf16[144,2048]{1,0:T(8,128)(2,1)S(1)}, bf16[144,2048]{1,0:T(8,128)(2,1)S(1)}, u32[]{:S(2)}, u32[]{:S(2)}) collective-permute-start(bf16[144,2048]{1,0:T(8,128)(2,1)S(1)} %collective-permute-done.1.refs_2_), channel_id=1, source_target_pairs={{2,0},{3,1},{4,2},{5,3},{6,4},{7,5},{0,6},{1,7},{10,8},{11,9},{12,... | collective-permute-start | bytes 1769480 | tf_op jit(solution)/shard_map/ppermute | solution.py:678
  45.4 36.8 %collective-permute-start.2 = (bf16[144,2048]{1,0:T(8,128)(2,1)S(1)}, bf16[144,2048]{1,0:T(8,128)(2,1)S(1)}, u32[]{:S(2)}, u32[]{:S(2)}) collective-permute-start(bf16[144,2048]{1,0:T(8,128)(2,1)S(1)} %collective-permute-done.1.refs_2_), channel_id=1, source_target_pairs={{1,0},{0,1},{3,2},{2,3},{5,4},{4,5},{7,6},{6,7},{9,8},{8,9},{11,10... | collective-permute-start | bytes 1769480 | tf_op jit(solution)/shard_map/ppermute | solution.py:678
  45.4 38.1 %collective-permute-start.24 = (bf16[144,2048]{1,0:T(8,128)(2,1)S(1)}, bf16[144,2048]{1,0:T(8,128)(2,1)S(1)}, u32[]{:S(2)}, u32[]{:S(2)}) collective-permute-start(bf16[144,2048]{1,0:T(8,128)(2,1)S(1)} %collective-permute-done.23.refs_0_), channel_id=1, source_target_pairs={{1,0},{0,1},{3,2},{2,3},{5,4},{4,5},{7,6},{6,7},{9,8},{8,9},{11,10... | collective-permute-start | bytes 1769480 | tf_op jit(solution)/shard_map/ppermute | solution.py:678
  133.7 32.7 %collective-permute-start.6 = (bf16[144,2048]{1,0:T(8,128)(2,1)S(1)}, bf16[144,2048]{1,0:T(8,128)(2,1)S(1)}, u32[]{:S(2)}, u32[]{:S(2)}) collective-permute-start(bf16[144,2048]{1,0:T(8,128)(2,1)S(1)} %collective-permute-done.5.refs_6_), channel_id=1, source_target_pairs={{1,0},{0,1},{3,2},{2,3},{5,4},{4,5},{7,6},{6,7},{9,8},{8,9},{11,10... | collective-permute-start | bytes 1769480 | tf_op jit(solution)/shard_map/ppermute | solution.py:678
  133.7 35.3 %collective-permute-start.28 = (bf16[144,2048]{1,0:T(8,128)(2,1)S(1)}, bf16[144,2048]{1,0:T(8,128)(2,1)S(1)}, u32[]{:S(2)}, u32[]{:S(2)}) collective-permute-start(bf16[144,2048]{1,0:T(8,128)(2,1)S(1)} %collective-permute-done.27.refs_4_), channel_id=1, source_target_pairs={{1,0},{0,1},{3,2},{2,3},{5,4},{4,5},{7,6},{6,7},{9,8},{8,9},{11,10... | collective-permute-start | bytes 1769480 | tf_op jit(solution)/shard_map/ppermute | solution.py:678
  134.2 36.3 %collective-permute-start.22 = (bf16[144,2048]{1,0:T(8,128)(2,1)S(1)}, bf16[144,2048]{1,0:T(8,128)(2,1)S(1)}, u32[]{:S(2)}, u32[]{:S(2)}) collective-permute-start(bf16[144,2048]{1,0:T(8,128)(2,1)S(1)} %collective-permute-done.21.refs_6_), channel_id=1, source_target_pairs={{1,0},{0,1},{3,2},{2,3},{5,4},{4,5},{7,6},{6,7},{9,8},{8,9},{11,10... | collective-permute-start | bytes 1769480 | tf_op jit(solution)/shard_map/ppermute | solution.py:678
  134.3 37.6 %collective-permute-start.14 = (bf16[144,2048]{1,0:T(8,128)(2,1)S(1)}, bf16[144,2048]{1,0:T(8,128)(2,1)S(1)}, u32[]{:S(2)}, u32[]{:S(2)}) collective-permute-start(bf16[144,2048]{1,0:T(8,128)(2,1)S(1)} %collective-permute-done.13.refs_6_), channel_id=1, source_target_pairs={{1,0},{0,1},{3,2},{2,3},{5,4},{4,5},{7,6},{6,7},{9,8},{8,9},{11,10... | collective-permute-start | bytes 1769480 | tf_op jit(solution)/shard_map/ppermute | solution.py:678
  136.4 45.6 %collective-permute-start.30 = (bf16[144,2048]{1,0:T(8,128)(2,1)}, bf16[144,2048]{1,0:T(8,128)(2,1)}, u32[]{:S(2)}, u32[]{:S(2)}) collective-permute-start(bf16[144,2048]{1,0:T(8,128)(2,1)} %collective-permute-done.29.refs_6_), channel_id=1, source_target_pairs={{1,0},{0,1},{3,2},{2,3},{5,4},{4,5},{7,6},{6,7},{9,8},{8,9},{11,10... | collective-permute-start | bytes 1769480 | tf_op jit(solution)/shard_map/ppermute | solution.py:678
  269.0 100.0 %all-to-all-start.1 = ((bf16[32,64,3,128]{3,1,2,0:T(8,128)(2,1)}), bf16[32,64,3,128]{3,1,2,0:T(8,128)(2,1)S(1)}, u32[]{:S(2)}, u32[]{:S(2)}) async-start(bf16[32,64,3,128]{3,1,2,0:T(8,128)(2,1)} %copy.108), calls=%async_computation.1 | async-start | bytes 3145728 | tf_op jit(solution)/shard_map/all_to_all | solution.py:802
  271.9 606.1 %reduce-scatter.2.cloned.1.call-start = ((), (), s32[]{:S(2)}) async-start(), calls=%async_computation.5 | async-start | bytes 17301504 | tf_op jit(solution)/shard_map/reduce_scatter | solution.py:934
  282.7 29.4 %collective-permute-start.41 = (bf16[1,1,1,1,192,128]{5,4,3,2,1,0:T(8,128)(2,1)S(1)}, bf16[1,1,1,1,192,128]{5,4,3,2,1,0:T(8,128)(2,1)S(1)}, u32[]{:S(2)}, u32[]{:S(2)}) collective-permute-start(bf16[1,1,1,1,192,128]{5,4,3,2,1,0:T(8,128)(2,1)S(1)} %maximum_bitcast_fusion), channel_id=1, source_target_pairs={{6,0},{7,1},{0,2},{1,3},{2,4},{3,5},{4,6},{5,7},{14,8},{15,9},{8,1... | collective-permute-start | bytes 147464 | tf_op jit(solution)/shard_map/ppermute | solution.py:678
  283.6 68.3 %collective-permute-start.40 = (bf16[1,1,1,1,192,128]{5,4,3,2,1,0:T(8,128)(2,1)S(1)}, bf16[1,1,1,1,192,128]{5,4,3,2,1,0:T(8,128)(2,1)S(1)}, u32[]{:S(2)}, u32[]{:S(2)}) collective-permute-start(bf16[1,1,1,1,192,128]{5,4,3,2,1,0:T(8,128)(2,1)S(1)} %maximum_bitcast_fusion), channel_id=1, source_target_pairs={{4,0},{5,1},{6,2},{7,3},{0,4},{1,5},{2,6},{3,7},{12,8},{13,9},{14,... | collective-permute-start | bytes 147464 | tf_op jit(solution)/shard_map/ppermute | solution.py:678
  287.7 64.2 %collective-permute-start.39 = (bf16[1,1,1,1,192,128]{5,4,3,2,1,0:T(8,128)(2,1)S(1)}, bf16[1,1,1,1,192,128]{5,4,3,2,1,0:T(8,128)(2,1)S(1)}, u32[]{:S(2)}, u32[]{:S(2)}) collective-permute-start(bf16[1,1,1,1,192,128]{5,4,3,2,1,0:T(8,128)(2,1)S(1)} %maximum_bitcast_fusion), channel_id=1, source_target_pairs={{2,0},{3,1},{4,2},{5,3},{6,4},{7,5},{0,6},{1,7},{10,8},{11,9},{12,... | collective-permute-start | bytes 147464 | tf_op jit(solution)/shard_map/ppermute | solution.py:678
  563.0 110.7 %all-to-all-start.2 = ((bf16[32,192,128]{2,1,0:T(8,128)(2,1)}), bf16[32,192,128]{2,1,0:T(8,128)(2,1)S(1)}, u32[]{:S(2)}, u32[]{:S(2)}) async-start(bf16[32,192,128]{2,1,0:T(8,128)(2,1)} %reshape.400), calls=%async_computation.3 | async-start | bytes 3145728 | tf_op jit(solution)/shard_map/all_to_all | solution.py:802
  597.6 27.3 %collective-permute-start.52 = (f32[1,1,1,1,160,128]{5,4,3,2,1,0:T(8,128)S(1)}, f32[1,1,1,1,160,128]{5,4,3,2,1,0:T(8,128)S(1)}, u32[]{:S(2)}, u32[]{:S(2)}) collective-permute-start(f32[1,1,1,1,160,128]{5,4,3,2,1,0:T(8,128)S(1)} %get-tuple-element.114), channel_id=1, source_target_pairs={{6,0},{7,1},{0,2},{1,3},{2,4},{3,5},{4,6},{5,7},{14,8},{15,9},{8,1... | collective-permute-start | bytes 245768 | tf_op jit(solution)/shard_map/ppermute | solution.py:678
  597.7 27.2 %collective-permute-start.54 = (f32[1,1,1,1,160,128]{5,4,3,2,1,0:T(8,128)S(1)}, f32[1,1,1,1,160,128]{5,4,3,2,1,0:T(8,128)S(1)}, u32[]{:S(2)}, u32[]{:S(2)}) collective-permute-start(f32[1,1,1,1,160,128]{5,4,3,2,1,0:T(8,128)S(1)} %get-tuple-element.115), channel_id=1, source_target_pairs={{2,0},{3,1},{4,2},{5,3},{6,4},{7,5},{0,6},{1,7},{10,8},{11,9},{12,... | collective-permute-start | bytes 245768 | tf_op jit(solution)/shard_map/ppermute | solution.py:678
  601.5 41.3 %collective-permute-start.53 = (f32[1,1,1,1,160,128]{5,4,3,2,1,0:T(8,128)S(1)}, f32[1,1,1,1,160,128]{5,4,3,2,1,0:T(8,128)S(1)}, u32[]{:S(2)}, u32[]{:S(2)}) collective-permute-start(f32[1,1,1,1,160,128]{5,4,3,2,1,0:T(8,128)S(1)} %get-tuple-element.116), channel_id=1, source_target_pairs={{4,0},{5,1},{6,2},{7,3},{0,4},{1,5},{2,6},{3,7},{12,8},{13,9},{14,... | collective-permute-start | bytes 245768 | tf_op jit(solution)/shard_map/ppermute | solution.py:678
  701.2 53.0 %collective-permute-start.69 = (bf16[2,2,4,1,128,512]{5,4,3,2,1,0:T(8,128)(2,1)}, bf16[2,2,4,1,128,512]{5,4,3,2,1,0:T(8,128)(2,1)}, u32[]{:S(2)}, u32[]{:S(2)}) collective-permute-start(bf16[2,2,4,1,128,512]{5,4,3,2,1,0:T(8,128)(2,1)} %slice.607), channel_id=1, source_target_pairs={{1,0},{0,1},{3,2},{2,3},{5,4},{4,5},{7,6},{6,7},{9,8},{8,9},{11,10... | collective-permute-start | bytes 6291464 | tf_op jit(solution)/shard_map/ppermute | solution.py:678
  708.6 50.6 %collective-permute-start.75 = (bf16[2,2,4,1,128,512]{5,4,3,2,1,0:T(8,128)(2,1)}, bf16[2,2,4,1,128,512]{5,4,3,2,1,0:T(8,128)(2,1)}, u32[]{:S(2)}, u32[]{:S(2)}) collective-permute-start(bf16[2,2,4,1,128,512]{5,4,3,2,1,0:T(8,128)(2,1)} %slice.618), channel_id=1, source_target_pairs={{1,0},{0,1},{3,2},{2,3},{5,4},{4,5},{7,6},{6,7},{9,8},{8,9},{11,10... | collective-permute-start | bytes 6291464 | tf_op jit(solution)/shard_map/ppermute | solution.py:678
  726.2 37.0 %collective-permute-start.63 = (bf16[2,2,4,1,128,512]{5,4,3,2,1,0:T(8,128)(2,1)}, bf16[2,2,4,1,128,512]{5,4,3,2,1,0:T(8,128)(2,1)}, u32[]{:S(2)}, u32[]{:S(2)}) collective-permute-start(bf16[2,2,4,1,128,512]{5,4,3,2,1,0:T(8,128)(2,1)} %slice.596), channel_id=1, source_target_pairs={{1,0},{0,1},{3,2},{2,3},{5,4},{4,5},{7,6},{6,7},{9,8},{8,9},{11,10... | collective-permute-start | bytes 6291464 | tf_op jit(solution)/shard_map/ppermute | solution.py:678
  726.2 40.1 %collective-permute-start.81 = (bf16[2,2,4,1,128,512]{5,4,3,2,1,0:T(8,128)(2,1)}, bf16[2,2,4,1,128,512]{5,4,3,2,1,0:T(8,128)(2,1)}, u32[]{:S(2)}, u32[]{:S(2)}) collective-permute-start(bf16[2,2,4,1,128,512]{5,4,3,2,1,0:T(8,128)(2,1)} %slice.629), channel_id=1, source_target_pairs={{1,0},{0,1},{3,2},{2,3},{5,4},{4,5},{7,6},{6,7},{9,8},{8,9},{11,10... | collective-permute-start | bytes 6291464 | tf_op jit(solution)/shard_map/ppermute | solution.py:678
  743.8 78.5 %all-to-all-start.3 = ((bf16[32,204,128]{2,1,0:T(8,128)(2,1)}), bf16[32,204,128]{2,1,0:T(8,128)(2,1)}, u32[]{:S(2)}, u32[]{:S(2)}) async-start(bf16[32,204,128]{2,1,0:T(8,128)(2,1)} %pad_maximum_fusion.1), calls=%async_computation.4 | async-start | bytes 3407872 | tf_op jit(solution)/shard_map/all_to_all | solution.py:802
  757.4 35.9 %collective-permute-start.70 = (bf16[2,1,4,1,128,512]{5,4,3,2,1,0:T(8,128)(2,1)S(1)}, bf16[2,1,4,1,128,512]{5,4,3,2,1,0:T(8,128)(2,1)S(1)}, u32[]{:S(2)}, u32[]{:S(2)}) collective-permute-start(bf16[2,1,4,1,128,512]{5,4,3,2,1,0:T(8,128)(2,1)S(1)} %slice.609), channel_id=1, source_target_pairs={{8,0},{0,8},{24,16},{16,24},{9,1},{1,9},{25,17},{17,25},{10,2},{2,... | collective-permute-start | bytes 3145736 | tf_op jit(solution)/shard_map/ppermute | solution.py:678
  761.7 34.5 %collective-permute-start.76 = (bf16[1,2,4,1,128,512]{5,4,3,2,1,0:T(8,128)(2,1)S(1)}, bf16[1,2,4,1,128,512]{5,4,3,2,1,0:T(8,128)(2,1)S(1)}, u32[]{:S(2)}, u32[]{:S(2)}) collective-permute-start(bf16[1,2,4,1,128,512]{5,4,3,2,1,0:T(8,128)(2,1)S(1)} %slice.620), channel_id=1, source_target_pairs={{16,0},{24,8},{0,16},{8,24},{17,1},{25,9},{1,17},{9,25},{18,2},{26... | collective-permute-start | bytes 3145736 | tf_op jit(solution)/shard_map/ppermute | solution.py:678
  765.7 51.9 %collective-permute-start.64 = (bf16[1,2,4,1,128,512]{5,4,3,2,1,0:T(8,128)(2,1)S(1)}, bf16[1,2,4,1,128,512]{5,4,3,2,1,0:T(8,128)(2,1)S(1)}, u32[]{:S(2)}, u32[]{:S(2)}) collective-permute-start(bf16[1,2,4,1,128,512]{5,4,3,2,1,0:T(8,128)(2,1)S(1)} %slice.598), channel_id=1, source_target_pairs={{16,0},{24,8},{0,16},{8,24},{17,1},{25,9},{1,17},{9,25},{18,2},{26... | collective-permute-start | bytes 3145736 | tf_op jit(solution)/shard_map/ppermute | solution.py:678
  768.6 51.3 %collective-permute-start.82 = (bf16[2,1,4,1,128,512]{5,4,3,2,1,0:T(8,128)(2,1)S(1)}, bf16[2,1,4,1,128,512]{5,4,3,2,1,0:T(8,128)(2,1)S(1)}, u32[]{:S(2)}, u32[]{:S(2)}) collective-permute-start(bf16[2,1,4,1,128,512]{5,4,3,2,1,0:T(8,128)(2,1)S(1)} %slice.631), channel_id=1, source_target_pairs={{8,0},{0,8},{24,16},{16,24},{9,1},{1,9},{25,17},{17,25},{10,2},{2,... | collective-permute-start | bytes 3145736 | tf_op jit(solution)/shard_map/ppermute | solution.py:678
  794.5 43.7 %collective-permute-start.71 = (bf16[1,1,4,1,128,512]{5,4,3,2,1,0:T(8,128)(2,1)}, bf16[1,1,4,1,128,512]{5,4,3,2,1,0:T(8,128)(2,1)}, u32[]{:S(2)}, u32[]{:S(2)}) collective-permute-start(bf16[1,1,4,1,128,512]{5,4,3,2,1,0:T(8,128)(2,1)} %slice.611), channel_id=1, source_target_pairs={{16,0},{24,8},{0,16},{8,24},{17,1},{25,9},{1,17},{9,25},{18,2},{26... | collective-permute-start | bytes 1572872 | tf_op jit(solution)/shard_map/ppermute | solution.py:678
  797.4 44.8 %collective-permute-start.77 = (bf16[1,1,4,1,128,512]{5,4,3,2,1,0:T(8,128)(2,1)}, bf16[1,1,4,1,128,512]{5,4,3,2,1,0:T(8,128)(2,1)}, u32[]{:S(2)}, u32[]{:S(2)}) collective-permute-start(bf16[1,1,4,1,128,512]{5,4,3,2,1,0:T(8,128)(2,1)} %slice.622), channel_id=1, source_target_pairs={{8,0},{0,8},{24,16},{16,24},{9,1},{1,9},{25,17},{17,25},{10,2},{2,... | collective-permute-start | bytes 1572872 | tf_op jit(solution)/shard_map/ppermute | solution.py:678
  (175 other events, 1729.3 us)
Sparse Core Ops, SparseCore 0:
  221.5 148.9 all-gather.2
  444.2 225.4 reduce-scatter.1

commit v3 on v2

--- a/solution.py
+++ b/solution.py
@@ -44,10 +44,9 @@
 
 def spread_lanes(source, widen, target):
 
-    @pl.loop(0, source.shape[0] // 128)
-    def _(n):
-        row = pl.ds(pl.multiple_of(n * 128, 128), 128)
-        target[row, :] = dot(source[row, :].astype(BF), widen[...])
+    low = source[...].astype(BF)
+    for c in range(0, target.shape[1], 256):
+        target[:, c : c + 256] = dot(low, widen[:, c : c + 256])
 
 
 def widening(columns, lanes):
@@ -122,8 +121,7 @@
 
 
 def scan_kernel(
-    groups, length, states, table, starts, places, act, picked, mask, gate, rate, widen, dt, bias, skip,
-    y, gated, spread_gated, pre, prior, end, sf, du, bc, ys, state, ex,
+    groups, length, states, table, starts, act, picked, mask, rate, widen, dt, bias, skip, y, pre, prior, end, sf, du, bc, ys, state, ex,
 ):
     copies, count, lanes = 8 // groups, rate.shape[0] // 8, rate.shape[1]
     i = pl.program_id(0)
@@ -164,12 +162,6 @@
         total = sum(ys[pl.ds(j * groups + g, length, stride=8), :] for j in range(copies))
         total = total + skip[...] * act[g, 0]
         y[g, 0] = total
-        opened = gate[g, 0]
-        low = (total * (opened * jax.nn.sigmoid(opened))).astype(BF)
-        gated[g, 0] = low
-        for m in range(bias.shape[0]):
-            cols = slice(m * lanes, (m + 1) * lanes)
-            spread_gated[places[g], 0, :, cols] = low * mask[g, 0, :, m : m + 1].astype(BF)
 
 
 def back_kernel(
@@ -239,14 +231,7 @@
         rate_grad[s * 8 : s * 8 + 8, :] = r[s]
     left[0 : count * 8, :] = carry[...]
     left[count * 8 :, :] = held[...]
-
-    @pl.loop(0, res.shape[0] // 128)
-    def _(n):
-        row = pl.ds(pl.multiple_of(n * 128, 128), 128)
-        res[row, :] = dot(pb[row, :].astype(BF), pick_b[...]) + dot(
-            pc[row, :].astype(BF), pick_c[...]
-        )
-
+    res[...] = dot(pb[...].astype(BF), pick_b[...]) + dot(pc[...].astype(BF), pick_c[...])
     lane = lax.broadcasted_iota(jnp.int32, (1, 128), 1)
     owner = lane % states // count
     for g in range(groups):
@@ -377,49 +362,58 @@
 
 
 def inproj_kernel(count, *refs):
-    pieces, (gain, weight, mask), (normed, proj) = refs[:count], refs[count : count + 3], refs[-2:]
+    pieces, (gain, weight), (normed, proj, mask, notes) = refs[:count], refs[count : count + 2], refs[-4:]
+    modes = mask.shape[2]
     rows = mask.shape[1] // count
+    square = (rows, rows)
+    same = lax.broadcasted_iota(jnp.int32, square, 0) == lax.broadcasted_iota(jnp.int32, square, 1)
+    kind = lax.broadcasted_iota(jnp.int32, (1, modes), 1).astype(F32)
     for n in range(count):
+        span = slice(n * rows, (n + 1) * rows)
         x = pieces[n][0:rows, :].astype(F32)
         scale = lax.rsqrt(jnp.mean(x * x, axis=1, keepdims=True) + EPS)
-        normed[0, n * rows : (n + 1) * rows, :] = (x * scale * gain[...]).astype(BF)
+        normed[0, span, :] = (x * scale * gain[...]).astype(BF)
+        note = pieces[n][rows : rows + 16, 0:rows].astype(F32)
+        column = jnp.sum(jnp.where(same, note[0:1, :], 0.0), axis=1, keepdims=True)
+        mask[0, span, :] = (column == kind).astype(F32)
+        if n == 0:
+            notes[0] = note[0:8, :]
     product = dot(normed[0], weight[...])
-    modes = mask.shape[2]
     width = weight.shape[1] // modes
     proj[0] = sum(
         product[:, m * width : (m + 1) * width] * mask[0, :, m : m + 1] for m in range(modes)
     )
 
 
-def inproj(at, lots, pieces, gain, weight, mask, so_far):
+def inproj(at, lots, rows, modes, pieces, gain, weight, so_far):
     tall, width = pieces[0].shape
     count = len(pieces)
-    rows = mask.shape[1] // count
-    modes = mask.shape[2]
     columns = weight.shape[1] // modes
     here = lambda i: (at, 0, 0)
     size = count * rows
-    full = lambda shape: pl.BlockSpec(shape, lambda i: (0,) * len(shape))
-    aliases = {} if so_far is None else {count + 3: 0, count + 4: 1}
+    extra = tuple(so_far or ())
     return pl.pallas_call(
         functools.partial(inproj_kernel, count),
         grid=(1,),
-        in_specs=[full((tall, width))] * count
-        + [full((1, width)), full(weight.shape), pl.BlockSpec((1, size, modes), here)]
-        + [pl.BlockSpec(memory_space=pl.ANY)] * len(aliases),
-        out_specs=[pl.BlockSpec((1, size, width), here), pl.BlockSpec((1, size, columns), here)],
+        in_specs=[flat(a) for a in (*pieces, gain, weight)]
+        + [pl.BlockSpec(memory_space=pl.ANY)] * len(extra),
+        out_specs=[pl.BlockSpec((1,) + shape, here) for shape in (
+            (size, width), (size, columns), (size, modes), (8, rows)
+        )],
         out_shape=[
             jax.ShapeDtypeStruct((lots, size, width), BF),
             jax.ShapeDtypeStruct((lots, size, columns), F32),
+            jax.ShapeDtypeStruct((lots, size, modes), F32),
+            jax.ShapeDtypeStruct((lots, 8, rows), F32),
         ],
-        input_output_aliases=aliases,
+        input_output_aliases={count + 2 + n: n for n in range(len(extra))},
         compiler_params=pltpu.CompilerParams(vmem_limit_bytes=VMEM),
         cost_estimate=pl.CostEstimate(
             flops=2 * size * width * weight.shape[1],
-            bytes_accessed=4 * size * width,
+            bytes_accessed=6 * size * width,
             transcendentals=0,
         ),
-    )(*pieces, gain, weight, mask, *(so_far or ()))
+    )(*pieces, gain, weight, *extra)
 
 
 def conv(table, starts, x, mask, taps, base, xproj):
@@ -504,12 +498,11 @@
     return pl.BlockSpec(array.shape, lambda i, *_: (0,) * array.ndim)
 
 
-def scan(table, starts, places, act, picked, mask, gate, rate, dt, bias, skip, states):
+def scan(table, starts, act, picked, mask, rate, dt, bias, skip, states):
     groups, blocks, length, lanes = act.shape
     total = blocks * length
     count = rate.shape[0] // 8
-    at = lambda i, t, b, p: (0, t[i], 0, 0)
-    modes = bias.shape[0]
+    at = lambda i, t, b: (0, t[i], 0, 0)
     block = lambda a: pl.BlockSpec((groups, 1) + a.shape[2:], at)
     widen = widening(states, count, lanes)
     tall = pltpu.VMEM((length * 8, lanes), F32)
@@ -517,16 +510,14 @@
     return pl.pallas_call(
         functools.partial(scan_kernel, groups, length, states),
         grid_spec=pltpu.PrefetchScalarGridSpec(
-            num_scalar_prefetch=3,
+            num_scalar_prefetch=2,
             grid=(blocks,),
-            in_specs=[block(a) for a in (act, picked, mask, gate)]
+            in_specs=[block(a) for a in (act, picked, mask)]
             + [flat(a) for a in (rate, widen, dt, bias, skip)],
             out_specs=[
                 block(act),
                 block(act),
-                pl.BlockSpec((groups, 1, length, modes * lanes), lambda i, t, b, p: (0, i, 0, 0)),
-                block(act),
-                pl.BlockSpec((length * count * 8, lanes), lambda i, t, b, p: (i, 0)),
+                pl.BlockSpec((length * count * 8, lanes), lambda i, t, b: (i, 0)),
                 flat(rate),
             ],
             scratch_shapes=[
@@ -540,15 +531,58 @@
         ),
         out_shape=[
             like,
-            jax.ShapeDtypeStruct(act.shape, BF),
-            jax.ShapeDtypeStruct((groups, blocks, length, modes * lanes), BF),
             like,
             jax.ShapeDtypeStruct((total * count * 8, lanes), F32),
             jax.ShapeDtypeStruct((count * 8, lanes), F32),
         ],
         compiler_params=pltpu.CompilerParams(vmem_limit_bytes=VMEM),
         cost_estimate=pl.CostEstimate(flops=10**10, bytes_accessed=10**8, transcendentals=0),
-    )(table, starts, places, act, picked, mask, gate, rate, widen, dt, bias, skip)
+    )(table, starts, act, picked, mask, rate, widen, dt, bias, skip)
+
+
+def gate_kernel(lots_at, spans_at, normed, weight, mask, read, gate, gated, spread_gated):
+    modes = mask.shape[2]
+    lanes = read.shape[2]
+    count = spans_at.shape[0]
+    rows = read.shape[1] // count
+    product = dot(normed[0], weight[...])
+    masks = [mask[0, :, m : m + 1] for m in range(modes)]
+    opened = sum(product[:, m * lanes : (m + 1) * lanes] * masks[m] for m in range(modes))
+    gate[0] = opened
+    low = (read[0] * (opened * jax.nn.sigmoid(opened))).astype(BF)
+    gated[0] = low
+    for m in range(modes):
+        own = low * masks[m].astype(BF)
+        for n in range(count):
+            place = pl.ds(pl.multiple_of(spans_at[n] * rows, rows), rows)
+            spread_gated[0, place, m * lanes : (m + 1) * lanes] = own[n * rows : (n + 1) * rows, :]
+
+
+def gate_part(lots_at, spans_at, normed, weight, mask, read):
+    lots, size, width = normed.shape
+    lanes = read.shape[2]
+    wide = weight.shape[1]
+    block = lambda w: pl.BlockSpec((1, size, w), lambda i, a, b: (i, 0, 0))
+    return pl.pallas_call(
+        gate_kernel,
+        grid_spec=pltpu.PrefetchScalarGridSpec(
+            num_scalar_prefetch=2,
+            grid=(lots,),
+            in_specs=[block(width), flat(weight), block(mask.shape[2]), block(lanes)],
+            out_specs=[
+                block(lanes), block(lanes), pl.BlockSpec((1, size, wide), lambda i, a, b: (a[i], 0, 0))
+            ],
+        ),
+        out_shape=[
+            jax.ShapeDtypeStruct(read.shape, F32),
+            jax.ShapeDtypeStruct(read.shape, BF),
+            jax.ShapeDtypeStruct((lots, size, wide), BF),
+        ],
+        compiler_params=pltpu.CompilerParams(vmem_limit_bytes=VMEM),
+        cost_estimate=pl.CostEstimate(
+            flops=2 * lots * size * width * wide, bytes_accessed=3 * lots * size * width, transcendentals=0
+        ),
+    )(lots_at, spans_at, normed, weight, mask, read)
 
 
 def scan_back(
@@ -699,6 +733,16 @@
     return dims
 
 
+def fence(*arrays):
+    return list(pl.pallas_call(
+        lambda *refs: None,
+        in_specs=[pl.BlockSpec(memory_space=pl.ANY)] * len(arrays),
+        out_specs=[pl.BlockSpec(memory_space=pl.ANY)] * len(arrays),
+        out_shape=[jax.ShapeDtypeStruct(x.shape, x.dtype) for x in arrays],
+        input_output_aliases={n: n for n in range(len(arrays))},
+    )(*arrays))
+
+
 def gather_pieces(dims, x):
     others, ring, core = dims[:-2], dims[-2], dims[-1]
     got = {}
@@ -832,13 +876,10 @@
 
     inner = lanes * parts
     blocks = parts // groups
-    note = jnp.concatenate([modality[0], starts // 64, starts % 64]).astype(BF)
-    note = jnp.pad(note[None], ((0, 15), (0, width - rows - 2)))
+    note = jnp.pad(jnp.stack([starts[0] >> 6, starts[0] & 63])[None], ((0, 0), (0, rows - 2)))
+    note = jnp.concatenate([modality, note], axis=0).astype(BF)
+    note = jnp.pad(note, ((0, 14), (0, width - rows)))
     pieces = gather_pieces(dims, jnp.concatenate([mine, note], axis=0))
-    aux = jnp.stack([piece[rows, : rows + 2] for piece in pieces]).astype(jnp.int32)
-    aux = aux.reshape(groups, blocks, rows + 2)
-    begins = aux[:, 0, rows] * 64 + aux[:, 0, rows + 1]
-    mode_ids = aux[:, :, :rows]
     room = -norm_gain.shape[0] % lanes
     notes = jnp.broadcast_to(jnp.pad(norm_gain, (0, room)), (parts, norm_gain.shape[0] + room))
     moved = collect(exchange(jnp.concatenate(
@@ -864,7 +905,6 @@
     skip = skip_weight.astype(F32)[None]
     xproj = xproj_weight.reshape(lanes, -1)
     out_rows = jnp.moveaxis(out_weight, 1, 0).reshape(modes * lanes, width)
-    masks = (mode_ids[..., None] == jnp.arange(modes, dtype=jnp.int32)).astype(F32)
     total = parts * rows
     copies = 8 // groups
     count = states // copies
@@ -890,21 +930,19 @@
             at = at * d.size + (names // stride % d.size + d.here()) % d.size
         return at.reshape(-1)
 
-    places = placed([d for d in dims if d.axis == "grp"])
 
     step_pieces = sizes[-1] * sizes[-2]
     lots_in = parts // step_pieces
-    in_masks = masks.reshape(lots_in, step_pieces * rows, modes)
     so_far = None
     for n in range(lots_in):
         so_far = inproj(
-            n, lots_in, pieces[n * step_pieces : (n + 1) * step_pieces], gain, x_cols, in_masks, so_far
+            n, lots_in, rows, modes, pieces[n * step_pieces : (n + 1) * step_pieces], gain, x_cols, so_far
         )
-    normed, conv_in = so_far
+    normed, conv_in, in_masks, notes = so_far
+    masks = in_masks.reshape(groups, blocks, rows, modes)
+    notes = notes.reshape(groups, -1, 8, rows)[:, 0, 1].astype(jnp.int32)
+    begins = notes[:, 0] * 64 + notes[:, 1]
     cots = lax.all_gather(after(cot, conv_in), chan, axis=0, tiled=True)
-    gate_cols = collect(exchange(shards(after(in_weight[:, :, inner:], conv_in))).reshape(
-        -1, modes, lanes
-    )).reshape(width, modes * lanes)
     normed = normed.reshape(total, width)
     grouped = (groups, blocks, rows, lanes)
     pre_act, act, partial = conv(
@@ -915,10 +953,16 @@
     rest = (picked[rows:] - low[rows:].astype(F32)).astype(BF)
     picked = gather_small(dims, jnp.concatenate([low, rest], axis=0))
     picked = picked.reshape(groups, blocks, -1, 128)
-    flat_masks = masks.reshape(total, modes)
-    gate_in = pick(dot(normed, gate_cols), flat_masks).reshape(grouped)
-    read, gated, spread_gated, pre, prior, end = scan(
-        table, begins, places, act, picked, masks, gate_in, rates, dt_cols, bias, skip, states
+    gate_cols = collect(exchange(shards(after(in_weight[:, :, inner:], picked))).reshape(
+        -1, modes, lanes
+    )).reshape(width, modes * lanes)
+    read, pre, prior, end = scan(
+        table, begins, act, picked, masks, rates, dt_cols, bias, skip, states
+    )
+    lot = (lots_in, step_pieces * rows, -1)
+    lots_at, spans_at = placed(dims[:-2]), placed(dims[-2:])
+    gate_in, gated, spread_gated = gate_part(
+        lots_at, spans_at, normed.reshape(lot), gate_cols, in_masks, read.reshape(lot)
     )
 
     def scatter(x, weight, dim, stages):
@@ -934,15 +978,14 @@
     branch = lax.psum_scatter(branch, chan, scatter_dimension=0, tiled=True)
     output = (mine.astype(F32) + branch.astype(F32)).astype(BF)[None]
 
-    lot = (lots_in, step_pieces * rows, -1)
     read_grad, gate_grad, grad_out_weight = cot_part(
-        placed(dims[:-2]), placed(dims[-2:]), cots.reshape(lots_in, -1, width), out_rows,
-        in_masks, gated.reshape(lot), read.reshape(lot), gate_in.reshape(lot),
+        lots_at, spans_at, cots.reshape(lots_in, -1, width), out_rows, in_masks, gated,
+        read.reshape(lot), gate_in,
     )
     grad_out_weight = jnp.moveaxis(grad_out_weight.reshape(modes, lanes, width), 0, 1)
     gate_grad = gate_grad.reshape(total, modes * lanes)
     in_rows = in_weight.shape[0]
-    grad_gate_cols = exchange(to_owners(t_dot(normed, gate_grad).astype(BF), in_rows))
+    gate_sent = to_owners(t_dot(normed, gate_grad).astype(BF), in_rows)
     begun = jnp.concatenate([jnp.zeros_like(end), end], axis=0)
     cuts = [blocks, 0]
     so_far = None
@@ -960,9 +1003,10 @@
     grad_decay = jnp.moveaxis(rate_grad, 0, 1).reshape(states, lanes).T * rate
     picked_grad = reduce_small(dims, picked_grad.reshape(sizes + (-1, 128))).astype(BF)
     picked_grad = gather_small(dims, picked_grad).reshape(groups, blocks, -1, 128)
+    grad_gate_cols = exchange(after(gate_sent, picked_grad))
     x_grad, tap_grad, base_grad, grad_xproj = conv_back(
         table, begins, act_grad, picked_grad, pre_act, act, conv_in.reshape(grouped), masks, taps,
-        xproj, [grad_gate_cols],
+        xproj, [],
     )
     x_grad = x_grad.reshape(total, modes * lanes)
     grad_x_cols = exchange(jnp.concatenate(

time: 895 us -> 782 us (0.87)
  waiting for transfers between devices: 333 us -> 257 us
  local copies, waits for them, and re-layouts: 124 us -> 103 us
  matrix products: 69.1 us -> 58.5 us
  starting transfers between devices: 113 us -> 104 us
    ppermute x87, waiting for transfers between devices: 333 us -> 235 us  [fetch(): return lax.ppermute(x, self.axis, pairs)]
    all_to_all x4, waiting for transfers between devices: 0.01 us -> 21.7 us  [exchange(): return lax.all_to_all(x, chan, 0, 0, tiled=True)]
    slice x33 -> x0, local copies, waits for them, and re-layouts: 20 us -> none  [the longest x31 19.1 us: on_device(): piece[rows, :rows + 2]]
    pallas_call x0 -> x1, Pallas kernels: none -> 13.9 us  [gate_part(): pl.pallas_call(gate_kernel, grid_spec=pltpu.PrefetchScalarGridSpec(num_sc...]
    dot_general x8 -> x7, matrix products: 69.1 us -> 58.5 us  [dot(): return lax.dot_general(a, b, (dims, ((), ())), preferred_element_type=F32)]
    ppermute x87, starting transfers between devices: 94.8 us -> 84.5 us  [fetch(): return lax.ppermute(x, self.axis, pairs)]
    pallas_call x1, Pallas kernels: 72 us -> 62.1 us  [scan_back(): pl.pallas_call(functools.partial(back_kernel, groups, length, states, las...]
    unnamed x235 -> x198, local copies, waits for them, and re-layouts: 40.2 us -> 41.9 us
  transfers between devices with their start and end apart: 93 -> 93, of which waited for: 46 -> 54; matrix products, arithmetic and copies ran while one was open for 21% -> 21% of each run, Pallas kernels for 18% -> 24%
where the time goes in v3:
time: 782 us; the launch traced here: 776 us
  waiting for transfers between devices  257 us (33%)
  Pallas kernels  191 us (24%)
  starting transfers between devices  104 us (13%)
  local copies, waits for them, and re-layouts  103 us (13%)
  matrix products  58.5 us (7%)
  other arithmetic  42.7 us (5%)
  between operations  18.6 us (2%)
    ppermute x87, waiting for transfers between devices, fetch(): return lax.ppermute(x, self.axis, pairs)  235 us
    ppermute x87, starting transfers between devices, fetch(): return lax.ppermute(x, self.axis, pairs)  84.5 us
    pallas_call x1, Pallas kernels, scan_back(): pl.pallas_call(functools.partial(back_kernel, groups, length, states, las...  62.1 us
    dot_general x7, matrix products, dot(): return lax.dot_general(a, b, (dims, ((), ())), preferred_element_type=F32)  58.5 us
    unnamed x198, local copies, waits for them, and re-layouts  41.9 us
    pallas_call x1, Pallas kernels, scan(): pl.pallas_call(functools.partial(scan_kernel, groups, length, states), gr...  38.9 us
    pallas_call x4, Pallas kernels, inproj(): pl.pallas_call(functools.partial(inproj_kernel, count), grid=(1,), in_spe...  26.3 us
    all_to_all x4, waiting for transfers between devices, exchange(): return lax.all_to_all(x, chan, 0, 0, tiled=True)  21.7 us
  transfers between devices with their start and end apart: 93, of which 54 were waited for; matrix products, arithmetic and copies ran while one was open for 21% of the time, Pallas kernels for 24%

profile of v3, /device:TPU:0, one launch (start us, length us, event | category | flops | bytes accessed | tf_op | source)
XLA Modules:
  0.0 775.7 jit_solution(8014859810008276404)
XLA Ops:
  36.1 18.4 %collective-permute-done.21.refs_0_ = bf16[144,2048]{1,0:T(8,128)(2,1)S(1)} collective-permute-done((bf16[144,2048]{1,0:T(8,128)(2,1)S(1)}, bf16[144,2048]{1,0:T(8,128)(2,1)S(1)}, u32[]{:S(2)}, u32[]{:S(2)}) %collective-permute-start.21) | collective-permute-done | bytes 589856 | tf_op jit(solution)/shard_map/ppermute | solution.py:712
  57.1 13.6 %collective-permute-done.1.refs_0_ = bf16[144,2048]{1,0:T(8,128)(2,1)S(1)} collective-permute-done((bf16[144,2048]{1,0:T(8,128)(2,1)S(1)}, bf16[144,2048]{1,0:T(8,128)(2,1)S(1)}, u32[]{:S(2)}, u32[]{:S(2)}) %collective-permute-start.1) | collective-permute-done | bytes 589856 | tf_op jit(solution)/shard_map/ppermute | solution.py:712
  70.6 12.2 %collective-permute-done.4.refs_2_ = bf16[144,2048]{1,0:T(8,128)(2,1)S(1)} collective-permute-done((bf16[144,2048]{1,0:T(8,128)(2,1)S(1)}, bf16[144,2048]{1,0:T(8,128)(2,1)S(1)}, u32[]{:S(2)}, u32[]{:S(2)}) %collective-permute-start.4) | collective-permute-done | bytes 589856 | tf_op jit(solution)/shard_map/ppermute | solution.py:712
  93.0 5.9 collective-permute-done.5.refs_2_
  99.3 11.9 %collective-permute-done.8.refs_4_ = bf16[144,2048]{1,0:T(8,128)(2,1)S(1)} collective-permute-done((bf16[144,2048]{1,0:T(8,128)(2,1)S(1)}, bf16[144,2048]{1,0:T(8,128)(2,1)S(1)}, u32[]{:S(2)}, u32[]{:S(2)}) %collective-permute-start.8) | collective-permute-done | bytes 589856 | tf_op jit(solution)/shard_map/ppermute | solution.py:712
  119.2 9.0 %collective-permute-done.9.refs_4_ = bf16[144,2048]{1,0:T(8,128)(2,1)S(1)} collective-permute-done((bf16[144,2048]{1,0:T(8,128)(2,1)S(1)}, bf16[144,2048]{1,0:T(8,128)(2,1)S(1)}, u32[]{:S(2)}, u32[]{:S(2)}) %collective-permute-start.9) | collective-permute-done | bytes 589856 | tf_op jit(solution)/shard_map/ppermute | solution.py:712
  128.2 12.4 %collective-permute-done.12.refs_6_ = bf16[144,2048]{1,0:T(8,128)(2,1)} collective-permute-done((bf16[144,2048]{1,0:T(8,128)(2,1)}, bf16[144,2048]{1,0:T(8,128)(2,1)}, u32[]{:S(2)}, u32[]{:S(2)}) %collective-permute-start.12) | collective-permute-done | bytes 589856 | tf_op jit(solution)/shard_map/ppermute | solution.py:712
  162.0 6.5 shard_map.265
  168.6 6.5 shard_map.266
  175.2 6.2 shard_map.267
  181.5 7.0 shard_map.268
  193.0 11.5 %shard_map.269 = (f32[4,8,128,128]{3,2,1,0:T(8,128)S(1)}, f32[4,8,128,128]{3,2,1,0:T(8,128)S(1)}, f32[4,8,160,128]{3,2,1,0:T(8,128)}) custom-call(s32[8]{0:T(128)S(1)} %fusion.41.table, s32[4]{0:T(128)S(1)} %add_reduce_fusion.starts, f32[4,8,128,128]{3,2,1,0:T(8,128)} %bitcast.175, f32[4,8,128,3]{3,2,1,0:T(8,128)} %bitcast.171, ...), custom_call_target="tpu_custom_call" | custom-call | tf_op jit(solution)/shard_map/pallas_call | solution.py:426
  231.7 11.8 %collective-permute-done.37 = f32[1,1,1,1,160,128]{5,4,3,2,1,0:T(8,128)S(1)} collective-permute-done((f32[1,1,1,1,160,128]{5,4,3,2,1,0:T(8,128)S(1)}, f32[1,1,1,1,160,128]{5,4,3,2,1,0:T(8,128)S(1)}, u32[]{:S(2)}, u32[]{:S(2)}) %collective-permute-start.37) | collective-permute-done | bytes 81952 | tf_op jit(solution)/shard_map/ppermute | solution.py:712
  284.6 38.9 %shard_map.270 = (f32[4,8,128,128]{3,2,1,0:T(8,128)S(1)}, f32[4,8,128,128]{3,2,1,0:T(8,128)S(1)}, f32[65536,128]{1,0:T(8,128)}, f32[64,128]{1,0:T(8,128)S(1)}) custom-call(s32[8]{0:T(128)S(1)} %fusion.41.table, s32[4]{0:T(128)S(1)} %add_reduce_fusion.starts, f32[4,8,128,128]{3,2,1,0:T(8,128)} %copy-done, bf16[4,8,192,128]{3,2,1,0:T(8,128)(2,1)S(1)} %bitcast.153, ...), custom_call_target="tpu_custom_call" | custom-call | flops 10000000000 | bytes 100000000 | tf_op jit(solution)/shard_map/pallas_call | solution.py:510
  326.1 20.6 %all-to-all-done.1 = bf16[32,64,3,128]{3,1,2,0:T(8,128)(2,1)} async-done(((bf16[32,64,3,128]{3,1,2,0:T(8,128)(2,1)}), bf16[32,64,3,128]{3,1,2,0:T(8,128)(2,1)}, u32[]{:S(2)}, u32[]{:S(2)}) %all-to-all-start.1) | async-done | bytes 1572896 | tf_op jit(solution)/shard_map/all_to_all | solution.py:846
  352.0 13.9 %shard_map.271 = (f32[4,1024,128]{2,1,0:T(8,128)S(1)}, bf16[4,1024,128]{2,1,0:T(8,128)(2,1)S(1)}, bf16[4,1024,384]{2,1,0:T(8,128)(2,1)}) custom-call(s32[4]{0:T(128)S(1)} %fusion.39.lots_at, s32[8]{0:T(128)S(1)} %fusion.40.spans_at, bf16[4,1024,2048]{2,1,0:T(8,128)(2,1)} %get-tuple-element.63.normed, bf16[2048,384]{1,0:T(8,128)(2,1)S(1)} %get-tuple-element.119.weight, ...), custom_call_target="tpu_custom_call" | custom-call | flops 6442450944 | bytes 25165824 | tf_op jit(solution)/shard_map/pallas_call | solution.py:566
  368.2 14.2 %convolution_convert_fusion = bf16[4096,2048]{1,0:T(8,128)(2,1)} fusion(bf16[4096,384]{1,0:T(8,128)(2,1)} %bitcast.221, bf16[384,2048]{1,0:T(8,128)(2,1)S(1)} %bitcast.162), kind=kOutput, calls=%fused_computation | convolution fusion | flops 6450839552 | bytes 21495808 | tf_op jit(solution)/shard_map/dot_general | solution.py:21
  385.2 21.7 %shard_map.272 = (f32[4,1024,128]{2,1,0:T(8,128)S(1)}, bf16[4,1024,384]{2,1,0:T(8,128)(2,1)}, f32[384,2048]{1,0:T(8,128)}) custom-call(s32[4]{0:T(128)S(1)} %fusion.39.lots_at, s32[8]{0:T(128)S(1)} %fusion.40.spans_at, bf16[4,1024,2048]{2,1,0:T(8,128)(2,1)} %bitcast.208, bf16[384,2048]{1,0:T(8,128)(2,1)S(1)} %bitcast.163, ...), custom_call_target="tpu_custom_call" | custom-call | flops 12884901888 | bytes 25165824 | tf_op jit(solution)/shard_map/pallas_call | solution.py:677
  408.2 62.1 %shard_map.273 = (f32[4,8,128,128]{3,2,1,0:T(8,128)S(1)}, f32[4,8,160,128]{3,2,1,0:T(8,128)}, f32[128,128]{1,0:T(8,128)}, f32[64,128]{1,0:T(8,128)S(1)}, f32[128...) custom-call(s32[8]{0:T(128)S(1)} %fusion.41.table, s32[4]{0:T(128)S(1)} %add_reduce_fusion.starts, ...), custom_call_target="tpu_custom_call" | custom-call | flops 10000000000 | bytes 200000000 | tf_op jit(solution)/shard_map/pallas_call | solution.py:615
  477.5 8.2 %collective-permute-done.48 = bf16[1,2,4,1,80,128]{5,4,3,2,1,0:T(8,128)(2,1)S(1)} collective-permute-done((bf16[1,2,4,1,80,128]{5,4,3,2,1,0:T(8,128)(2,1)S(1)}, bf16[1,2,4,1,80,128]{5,4,3,2,1,0:T(8,128)(2,1)S(1)}, u32[]{:S(2)}, u32[]{:S(2)}) %collective-permute-start.48) | collective-permute-done | bytes 163872 | tf_op jit(solution)/shard_map/ppermute | solution.py:712
  487.7 7.2 collective-permute-done.49
  497.4 6.3 collective-permute-done.54
  538.6 16.9 %shard_map.274 = (bf16[4,8,128,384]{3,2,1,0:T(8,128)(2,1)}, f32[8,128]{1,0:T(8,128)S(1)}, f32[1,128]{1,0:T(1,128)}, f32[128,480]{1,0:T(8,128)S(1)}) custom-call(s32[8]{0:T(128)S(1)} %fusion.41.table, s32[4]{0:T(128)S(1)} %add_reduce_fusion.starts, f32[4,8,128,128]{3,2,1,0:T(8,128)S(1)} %copy-done.4, bf16[4,8,160,128]{3,2,1,0:T(8,128)(2,1)S(1)} %bitcast.156, ...), custom_call_target="tpu_custom_call" | custom-call | tf_op jit(solution)/shard_map/pallas_call | solution.py:460
  555.6 5.7 convolution_convert_fusion.1
  565.0 6.2 convolution_convert_fusion.2
  575.5 9.2 %fusion = bf16[2048,384]{1,0:T(8,128)(2,1)S(1)} fusion(bf16[4,1024,2048]{2,1,0:T(8,128)(2,1)S(1)} %bitcast.167, bf16[4,1024,384]{2,1,0:T(8,128)(2,1)S(1)} %copy-done.87, bf16[]{:T(256)} %bitcast.59), kind=kOutput, calls=%fused_computation.14 | convolution fusion | flops 6444023808 | bytes 21495810 | tf_op jit(solution)/shard_map/dot_general | solution.py:21
  586.3 5.9 all-to-all-start.3
  592.2 6.6 convolution_convert_fusion.3
  602.8 6.6 convolution_convert_fusion.4
  613.5 10.0 %convolution_convert_fusion.5 = bf16[2048,384]{1,0:T(8,128)(2,1)} fusion(bf16[4096,2048]{1,0:T(8,128)(2,1)S(1)} %bitcast.170, bf16[4096,384]{1,0:T(8,128)(2,1)S(1)} %bitcast.213), kind=kOutput, calls=%fused_computation.13 | convolution fusion | flops 6443237376 | bytes 21495808 | tf_op jit(solution)/shard_map/dot_general | solution.py:21
  664.5 15.6 %collective-permute-done.82 = bf16[2,1,4,1,128,512]{5,4,3,2,1,0:T(8,128)(2,1)} collective-permute-done((bf16[2,1,4,1,128,512]{5,4,3,2,1,0:T(8,128)(2,1)}, bf16[2,1,4,1,128,512]{5,4,3,2,1,0:T(8,128)(2,1)}, u32[]{:S(2)}, u32[]{:S(2)}) %collective-permute-start.82) | collective-permute-done | bytes 1048608 | tf_op jit(solution)/shard_map/ppermute | solution.py:712
  688.3 14.3 %collective-permute-done.70 = bf16[2,1,4,1,128,512]{5,4,3,2,1,0:T(8,128)(2,1)} collective-permute-done((bf16[2,1,4,1,128,512]{5,4,3,2,1,0:T(8,128)(2,1)}, bf16[2,1,4,1,128,512]{5,4,3,2,1,0:T(8,128)(2,1)}, u32[]{:S(2)}, u32[]{:S(2)}) %collective-permute-start.70) | collective-permute-done | bytes 1048608 | tf_op jit(solution)/shard_map/ppermute | solution.py:712
  (521 shorter events, 333.9 us)
Async XLA Ops:
  20.6 122.9 %all-to-all-start = ((bf16[32,205,128]{2,1,0:T(8,128)(2,1)}), bf16[32,205,128]{2,1,0:T(8,128)(2,1)}, u32[]{:S(2)}, u32[]{:S(2)}) async-start(bf16[32,205,128]{2,1,0:T(8,128)(2,1)} %copy.101), calls=%async_computation | async-start | bytes 3407872 | tf_op jit(solution)/shard_map/all_to_all | solution.py:846
  24.0 358.5 %all-gather.3.cloned.1.call-start = ((), (), s32[]{:S(2)}) async-start(), calls=%async_computation.6 | async-start | bytes 17301504 | tf_op jit(solution)/shard_map/all_gather | solution.py:945
  24.0 30.5 %collective-permute-start.21 = (bf16[144,2048]{1,0:T(8,128)(2,1)S(1)}, bf16[144,2048]{1,0:T(8,128)(2,1)S(1)}, u32[]{:S(2)}, u32[]{:S(2)}) collective-permute-start(bf16[144,2048]{1,0:T(8,128)(2,1)S(1)} %fusion.13.refs_0_), channel_id=1, source_target_pairs={{8,0},{0,8},{24,16},{16,24},{9,1},{1,9},{25,17},{17,25},{10,2},{2,... | collective-permute-start | bytes 1769480 | tf_op jit(solution)/shard_map/ppermute | solution.py:712
  25.7 28.9 %collective-permute-start.27 = (bf16[144,2048]{1,0:T(8,128)(2,1)S(1)}, bf16[144,2048]{1,0:T(8,128)(2,1)S(1)}, u32[]{:S(2)}, u32[]{:S(2)}) collective-permute-start(bf16[144,2048]{1,0:T(8,128)(2,1)S(1)} %fusion.13.refs_0_), channel_id=1, source_target_pairs={{1,0},{0,1},{3,2},{2,3},{5,4},{4,5},{7,6},{6,7},{9,8},{8,9},{11,10... | collective-permute-start | bytes 1769480 | tf_op jit(solution)/shard_map/ppermute | solution.py:712
  26.3 44.3 %collective-permute-start.1 = (bf16[144,2048]{1,0:T(8,128)(2,1)S(1)}, bf16[144,2048]{1,0:T(8,128)(2,1)S(1)}, u32[]{:S(2)}, u32[]{:S(2)}) collective-permute-start(bf16[144,2048]{1,0:T(8,128)(2,1)S(1)} %collective-permute-done.refs_0_), channel_id=1, source_target_pairs={{8,0},{0,8},{24,16},{16,24},{9,1},{1,9},{25,17},{17,25},{10,2},{2,... | collective-permute-start | bytes 1769480 | tf_op jit(solution)/shard_map/ppermute | solution.py:712
  30.3 52.5 %collective-permute-start.4 = (bf16[144,2048]{1,0:T(8,128)(2,1)S(1)}, bf16[144,2048]{1,0:T(8,128)(2,1)S(1)}, u32[]{:S(2)}, u32[]{:S(2)}) collective-permute-start(bf16[144,2048]{1,0:T(8,128)(2,1)S(1)} %collective-permute-done.3.refs_2_), channel_id=1, source_target_pairs={{8,0},{0,8},{24,16},{16,24},{9,1},{1,9},{25,17},{17,25},{10,2},{2,... | collective-permute-start | bytes 1769480 | tf_op jit(solution)/shard_map/ppermute | solution.py:712
  31.8 51.0 %collective-permute-start.7 = (bf16[144,2048]{1,0:T(8,128)(2,1)S(1)}, bf16[144,2048]{1,0:T(8,128)(2,1)S(1)}, u32[]{:S(2)}, u32[]{:S(2)}) collective-permute-start(bf16[144,2048]{1,0:T(8,128)(2,1)S(1)} %collective-permute-done.3.refs_2_), channel_id=1, source_target_pairs={{2,0},{3,1},{4,2},{5,3},{6,4},{7,5},{0,6},{1,7},{10,8},{11,9},{12,... | collective-permute-start | bytes 1769480 | tf_op jit(solution)/shard_map/ppermute | solution.py:712
  54.6 29.8 %collective-permute-start.15 = (bf16[144,2048]{1,0:T(8,128)(2,1)S(1)}, bf16[144,2048]{1,0:T(8,128)(2,1)S(1)}, u32[]{:S(2)}, u32[]{:S(2)}) collective-permute-start(bf16[144,2048]{1,0:T(8,128)(2,1)S(1)} %collective-permute-done.refs_0_), channel_id=1, source_target_pairs={{1,0},{0,1},{3,2},{2,3},{5,4},{4,5},{7,6},{6,7},{9,8},{8,9},{11,10... | collective-permute-start | bytes 1769480 | tf_op jit(solution)/shard_map/ppermute | solution.py:712
  55.4 30.3 %collective-permute-start.16 = (bf16[144,2048]{1,0:T(8,128)(2,1)S(1)}, bf16[144,2048]{1,0:T(8,128)(2,1)S(1)}, u32[]{:S(2)}, u32[]{:S(2)}) collective-permute-start(bf16[144,2048]{1,0:T(8,128)(2,1)S(1)} %collective-permute-done.3.refs_2_), channel_id=1, source_target_pairs={{16,0},{24,8},{0,16},{8,24},{17,1},{25,9},{1,17},{9,25},{18,2},{26... | collective-permute-start | bytes 1769480 | tf_op jit(solution)/shard_map/ppermute | solution.py:712
  85.7 26.4 %collective-permute-start.11 = (bf16[144,2048]{1,0:T(8,128)(2,1)S(1)}, bf16[144,2048]{1,0:T(8,128)(2,1)}, u32[]{:S(2)}, u32[]{:S(2)}) collective-permute-start(bf16[144,2048]{1,0:T(8,128)(2,1)S(1)} %collective-permute-done.7.refs_4_), channel_id=1, source_target_pairs={{2,0},{3,1},{4,2},{5,3},{6,4},{7,5},{0,6},{1,7},{10,8},{11,9},{12,... | collective-permute-start | bytes 1769480 | tf_op jit(solution)/shard_map/ppermute | solution.py:712
  113.2 27.3 %collective-permute-start.12 = (bf16[144,2048]{1,0:T(8,128)(2,1)}, bf16[144,2048]{1,0:T(8,128)(2,1)}, u32[]{:S(2)}, u32[]{:S(2)}) collective-permute-start(bf16[144,2048]{1,0:T(8,128)(2,1)} %collective-permute-done.11.refs_6_), channel_id=1, source_target_pairs={{8,0},{0,8},{24,16},{16,24},{9,1},{1,9},{25,17},{17,25},{10,2},{2,... | collective-permute-start | bytes 1769480 | tf_op jit(solution)/shard_map/ppermute | solution.py:712
  115.7 26.4 %collective-permute-start.18 = (bf16[144,2048]{1,0:T(8,128)(2,1)S(1)}, bf16[144,2048]{1,0:T(8,128)(2,1)S(1)}, u32[]{:S(2)}, u32[]{:S(2)}) collective-permute-start(bf16[144,2048]{1,0:T(8,128)(2,1)S(1)} %collective-permute-done.8.refs_4_), channel_id=1, source_target_pairs={{1,0},{0,1},{3,2},{2,3},{5,4},{4,5},{7,6},{6,7},{9,8},{8,9},{11,10... | collective-permute-start | bytes 1769480 | tf_op jit(solution)/shard_map/ppermute | solution.py:712
  116.6 26.4 %collective-permute-start.19 = (bf16[144,2048]{1,0:T(8,128)(2,1)}, bf16[144,2048]{1,0:T(8,128)(2,1)}, u32[]{:S(2)}, u32[]{:S(2)}) collective-permute-start(bf16[144,2048]{1,0:T(8,128)(2,1)} %collective-permute-done.11.refs_6_), channel_id=1, source_target_pairs={{16,0},{24,8},{0,16},{8,24},{17,1},{25,9},{1,17},{9,25},{18,2},{26... | collective-permute-start | bytes 1769480 | tf_op jit(solution)/shard_map/ppermute | solution.py:712
  119.0 32.0 %collective-permute-start.25 = (bf16[144,2048]{1,0:T(8,128)(2,1)}, bf16[144,2048]{1,0:T(8,128)(2,1)}, u32[]{:S(2)}, u32[]{:S(2)}) collective-permute-start(bf16[144,2048]{1,0:T(8,128)(2,1)} %collective-permute-done.24.refs_4_), channel_id=1, source_target_pairs={{1,0},{0,1},{3,2},{2,3},{5,4},{4,5},{7,6},{6,7},{9,8},{8,9},{11,10... | collective-permute-start | bytes 1769480 | tf_op jit(solution)/shard_map/ppermute | solution.py:712
  143.0 32.1 %collective-permute-start.20 = (bf16[144,2048]{1,0:T(8,128)(2,1)}, bf16[144,2048]{1,0:T(8,128)(2,1)}, u32[]{:S(2)}, u32[]{:S(2)}) collective-permute-start(bf16[144,2048]{1,0:T(8,128)(2,1)} %collective-permute-done.19.refs_6_), channel_id=1, source_target_pairs={{1,0},{0,1},{3,2},{2,3},{5,4},{4,5},{7,6},{6,7},{9,8},{8,9},{11,10... | collective-permute-start | bytes 1769480 | tf_op jit(solution)/shard_map/ppermute | solution.py:712
  150.9 30.5 %collective-permute-start.2 = (bf16[144,2048]{1,0:T(8,128)(2,1)S(1)}, bf16[144,2048]{1,0:T(8,128)(2,1)}, u32[]{:S(2)}, u32[]{:S(2)}) collective-permute-start(bf16[144,2048]{1,0:T(8,128)(2,1)S(1)} %collective-permute-done.1.refs_0_), channel_id=1, source_target_pairs={{1,0},{0,1},{3,2},{2,3},{5,4},{4,5},{7,6},{6,7},{9,8},{8,9},{11,10... | collective-permute-start | bytes 1769480 | tf_op jit(solution)/shard_map/ppermute | solution.py:712
  151.0 30.4 %collective-permute-start.6 = (bf16[144,2048]{1,0:T(8,128)(2,1)S(1)}, bf16[144,2048]{1,0:T(8,128)(2,1)}, u32[]{:S(2)}, u32[]{:S(2)}) collective-permute-start(bf16[144,2048]{1,0:T(8,128)(2,1)S(1)} %collective-permute-done.5.refs_2_), channel_id=1, source_target_pairs={{1,0},{0,1},{3,2},{2,3},{5,4},{4,5},{7,6},{6,7},{9,8},{8,9},{11,10... | collective-permute-start | bytes 1769480 | tf_op jit(solution)/shard_map/ppermute | solution.py:712
  275.3 71.5 %all-to-all-start.1 = ((bf16[32,64,3,128]{3,1,2,0:T(8,128)(2,1)}), bf16[32,64,3,128]{3,1,2,0:T(8,128)(2,1)}, u32[]{:S(2)}, u32[]{:S(2)}) async-start(bf16[32,64,3,128]{3,1,2,0:T(8,128)(2,1)} %copy.104), calls=%async_computation.1 | async-start | bytes 3145728 | tf_op jit(solution)/shard_map/all_to_all | solution.py:846
  280.6 484.5 %reduce-scatter.2.cloned.1.call-start = ((), (), s32[]{:S(2)}) async-start(), calls=%async_computation.5 | async-start | bytes 17301504 | tf_op jit(solution)/shard_map/reduce_scatter | solution.py:978
  564.9 73.3 %collective-permute-start.81 = (bf16[2,2,4,1,128,512]{5,4,3,2,1,0:T(8,128)(2,1)}, bf16[2,2,4,1,128,512]{5,4,3,2,1,0:T(8,128)(2,1)}, u32[]{:S(2)}, u32[]{:S(2)}) collective-permute-start(bf16[2,2,4,1,128,512]{5,4,3,2,1,0:T(8,128)(2,1)} %slice.449), channel_id=1, source_target_pairs={{1,0},{0,1},{3,2},{2,3},{5,4},{4,5},{7,6},{6,7},{9,8},{8,9},{11,10... | collective-permute-start | bytes 6291464 | tf_op jit(solution)/shard_map/ppermute | solution.py:712
  574.4 69.9 %collective-permute-start.75 = (bf16[2,2,4,1,128,512]{5,4,3,2,1,0:T(8,128)(2,1)}, bf16[2,2,4,1,128,512]{5,4,3,2,1,0:T(8,128)(2,1)}, u32[]{:S(2)}, u32[]{:S(2)}) collective-permute-start(bf16[2,2,4,1,128,512]{5,4,3,2,1,0:T(8,128)(2,1)} %slice.438), channel_id=1, source_target_pairs={{1,0},{0,1},{3,2},{2,3},{5,4},{4,5},{7,6},{6,7},{9,8},{8,9},{11,10... | collective-permute-start | bytes 6291464 | tf_op jit(solution)/shard_map/ppermute | solution.py:712
  586.3 44.8 %all-to-all-start.3 = ((bf16[32,192,128]{2,1,0:T(8,128)(2,1)}), bf16[32,192,128]{2,1,0:T(8,128)(2,1)S(1)}, u32[]{:S(2)}, u32[]{:S(2)}) async-start(bf16[32,192,128]{2,1,0:T(8,128)(2,1)} %add.363), calls=%async_computation.4 | async-start | bytes 3145728 | tf_op jit(solution)/shard_map/all_to_all | solution.py:846
  602.5 46.9 %collective-permute-start.69 = (bf16[2,2,4,1,128,512]{5,4,3,2,1,0:T(8,128)(2,1)}, bf16[2,2,4,1,128,512]{5,4,3,2,1,0:T(8,128)(2,1)}, u32[]{:S(2)}, u32[]{:S(2)}) collective-permute-start(bf16[2,2,4,1,128,512]{5,4,3,2,1,0:T(8,128)(2,1)} %slice.427), channel_id=1, source_target_pairs={{1,0},{0,1},{3,2},{2,3},{5,4},{4,5},{7,6},{6,7},{9,8},{8,9},{11,10... | collective-permute-start | bytes 6291464 | tf_op jit(solution)/shard_map/ppermute | solution.py:712
  612.5 41.0 %collective-permute-start.63 = (bf16[2,2,4,1,128,512]{5,4,3,2,1,0:T(8,128)(2,1)}, bf16[2,2,4,1,128,512]{5,4,3,2,1,0:T(8,128)(2,1)}, u32[]{:S(2)}, u32[]{:S(2)}) collective-permute-start(bf16[2,2,4,1,128,512]{5,4,3,2,1,0:T(8,128)(2,1)} %slice.416), channel_id=1, source_target_pairs={{1,0},{0,1},{3,2},{2,3},{5,4},{4,5},{7,6},{6,7},{9,8},{8,9},{11,10... | collective-permute-start | bytes 6291464 | tf_op jit(solution)/shard_map/ppermute | solution.py:712
  631.1 79.1 %all-to-all-start.2 = ((bf16[32,204,128]{2,1,0:T(8,128)(2,1)}), bf16[32,204,128]{2,1,0:T(8,128)(2,1)}, u32[]{:S(2)}, u32[]{:S(2)}) async-start(bf16[32,204,128]{2,1,0:T(8,128)(2,1)} %pad_maximum_fusion.1), calls=%async_computation.3 | async-start | bytes 3407872 | tf_op jit(solution)/shard_map/all_to_all | solution.py:846
  642.4 37.8 %collective-permute-start.82 = (bf16[2,1,4,1,128,512]{5,4,3,2,1,0:T(8,128)(2,1)}, bf16[2,1,4,1,128,512]{5,4,3,2,1,0:T(8,128)(2,1)}, u32[]{:S(2)}, u32[]{:S(2)}) collective-permute-start(bf16[2,1,4,1,128,512]{5,4,3,2,1,0:T(8,128)(2,1)} %slice.451), channel_id=1, source_target_pairs={{8,0},{0,8},{24,16},{16,24},{9,1},{1,9},{25,17},{17,25},{10,2},{2,... | collective-permute-start | bytes 3145736 | tf_op jit(solution)/shard_map/ppermute | solution.py:712
  647.9 37.0 %collective-permute-start.76 = (bf16[1,2,4,1,128,512]{5,4,3,2,1,0:T(8,128)(2,1)}, bf16[1,2,4,1,128,512]{5,4,3,2,1,0:T(8,128)(2,1)}, u32[]{:S(2)}, u32[]{:S(2)}) collective-permute-start(bf16[1,2,4,1,128,512]{5,4,3,2,1,0:T(8,128)(2,1)} %slice.440), channel_id=1, source_target_pairs={{16,0},{24,8},{0,16},{8,24},{17,1},{25,9},{1,17},{9,25},{18,2},{26... | collective-permute-start | bytes 3145736 | tf_op jit(solution)/shard_map/ppermute | solution.py:712
  653.0 49.7 %collective-permute-start.70 = (bf16[2,1,4,1,128,512]{5,4,3,2,1,0:T(8,128)(2,1)}, bf16[2,1,4,1,128,512]{5,4,3,2,1,0:T(8,128)(2,1)}, u32[]{:S(2)}, u32[]{:S(2)}) collective-permute-start(bf16[2,1,4,1,128,512]{5,4,3,2,1,0:T(8,128)(2,1)} %slice.429), channel_id=1, source_target_pairs={{8,0},{0,8},{24,16},{16,24},{9,1},{1,9},{25,17},{17,25},{10,2},{2,... | collective-permute-start | bytes 3145736 | tf_op jit(solution)/shard_map/ppermute | solution.py:712
  656.9 49.6 %collective-permute-start.64 = (bf16[1,2,4,1,128,512]{5,4,3,2,1,0:T(8,128)(2,1)}, bf16[1,2,4,1,128,512]{5,4,3,2,1,0:T(8,128)(2,1)}, u32[]{:S(2)}, u32[]{:S(2)}) collective-permute-start(bf16[1,2,4,1,128,512]{5,4,3,2,1,0:T(8,128)(2,1)} %slice.418), channel_id=1, source_target_pairs={{16,0},{24,8},{0,16},{8,24},{17,1},{25,9},{1,17},{9,25},{18,2},{26... | collective-permute-start | bytes 3145736 | tf_op jit(solution)/shard_map/ppermute | solution.py:712
  683.5 42.5 %collective-permute-start.83 = (bf16[1,1,4,1,128,512]{5,4,3,2,1,0:T(8,128)(2,1)}, bf16[1,1,4,1,128,512]{5,4,3,2,1,0:T(8,128)(2,1)}, u32[]{:S(2)}, u32[]{:S(2)}) collective-permute-start(bf16[1,1,4,1,128,512]{5,4,3,2,1,0:T(8,128)(2,1)} %slice.453), channel_id=1, source_target_pairs={{16,0},{24,8},{0,16},{8,24},{17,1},{25,9},{1,17},{9,25},{18,2},{26... | collective-permute-start | bytes 1572872 | tf_op jit(solution)/shard_map/ppermute | solution.py:712
  687.3 41.3 %collective-permute-start.77 = (bf16[1,1,4,1,128,512]{5,4,3,2,1,0:T(8,128)(2,1)}, bf16[1,1,4,1,128,512]{5,4,3,2,1,0:T(8,128)(2,1)}, u32[]{:S(2)}, u32[]{:S(2)}) collective-permute-start(bf16[1,1,4,1,128,512]{5,4,3,2,1,0:T(8,128)(2,1)} %slice.442), channel_id=1, source_target_pairs={{8,0},{0,8},{24,16},{16,24},{9,1},{1,9},{25,17},{17,25},{10,2},{2,... | collective-permute-start | bytes 1572872 | tf_op jit(solution)/shard_map/ppermute | solution.py:712
  705.1 26.1 %collective-permute-start.71 = (bf16[1,1,4,1,128,512]{5,4,3,2,1,0:T(8,128)(2,1)}, bf16[1,1,4,1,128,512]{5,4,3,2,1,0:T(8,128)(2,1)}, u32[]{:S(2)}, u32[]{:S(2)}) collective-permute-start(bf16[1,1,4,1,128,512]{5,4,3,2,1,0:T(8,128)(2,1)} %slice.431), channel_id=1, source_target_pairs={{16,0},{24,8},{0,16},{8,24},{17,1},{25,9},{1,17},{9,25},{18,2},{26... | collective-permute-start | bytes 1572872 | tf_op jit(solution)/shard_map/ppermute | solution.py:712
  (158 other events, 1362.6 us)
Sparse Core Ops, SparseCore 0:
  191.9 152.7 all-gather.2
  382.6 191.8 reduce-scatter.1

commit v4 on v3

--- a/solution.py
+++ b/solution.py
@@ -14,7 +14,7 @@
 F32 = jnp.float32
 LOG2E = math.log2(math.e)
 RESET = 1e4
-VMEM = 48 * 1024 * 1024
+VMEM = 60 * 1024 * 1024
 
 
 def dot(a, b, dims=((1,), (0,))):
@@ -361,59 +361,94 @@
             x_grad[g, 0, :, m * lanes : (m + 1) * lanes] = total * mask[g, 0, :, m : m + 1].astype(BF)
 
 
-def inproj_kernel(count, *refs):
-    pieces, (gain, weight), (normed, proj, mask, notes) = refs[:count], refs[count : count + 2], refs[-4:]
+def inproj_kernel(lots, *refs):
+    pieces = refs[:-9]
+    gain, weight, normed, proj, mask, notes, cols, whole, arrived = refs[-9:]
     modes = mask.shape[2]
+    lanes = weight.shape[2]
+    count = len(pieces) // lots
     rows = mask.shape[1] // count
+    part = cols.shape[0] // weight.shape[0]
+    i = pl.program_id(0)
+
+    def copies(lot):
+        return [
+            pltpu.make_async_copy(
+                pieces[lot * count + n], whole.at[lot % 2, n], arrived.at[lot % 2, n]
+            )
+            for n in range(count)
+        ]
+
+    @pl.when(i == 0)
+    def _():
+        for copy in copies(0):
+            copy.start()
+        for n in range(weight.shape[0]):
+            for m in range(modes):
+                cols[n * part : (n + 1) * part, m * lanes : (m + 1) * lanes] = weight[
+                    n, m * part : (m + 1) * part, :
+                ]
+
+    for lot in range(lots):
+
+        @pl.when(i == lot)
+        def _(lot=lot):
+            if lot + 1 < lots:
+                for copy in copies(lot + 1):
+                    copy.start()
+            for copy in copies(lot):
+                copy.wait()
+
+    slot = lax.rem(i, 2)
     square = (rows, rows)
     same = lax.broadcasted_iota(jnp.int32, square, 0) == lax.broadcasted_iota(jnp.int32, square, 1)
     kind = lax.broadcasted_iota(jnp.int32, (1, modes), 1).astype(F32)
     for n in range(count):
         span = slice(n * rows, (n + 1) * rows)
-        x = pieces[n][0:rows, :].astype(F32)
+        x = whole[slot, n, 0:rows, :].astype(F32)
         scale = lax.rsqrt(jnp.mean(x * x, axis=1, keepdims=True) + EPS)
         normed[0, span, :] = (x * scale * gain[...]).astype(BF)
-        note = pieces[n][rows : rows + 16, 0:rows].astype(F32)
+        note = whole[slot, n, rows : rows + 16, 0:rows].astype(F32)
         column = jnp.sum(jnp.where(same, note[0:1, :], 0.0), axis=1, keepdims=True)
         mask[0, span, :] = (column == kind).astype(F32)
         if n == 0:
             notes[0] = note[0:8, :]
-    product = dot(normed[0], weight[...])
-    width = weight.shape[1] // modes
+    product = dot(normed[0], cols[...])
     proj[0] = sum(
-        product[:, m * width : (m + 1) * width] * mask[0, :, m : m + 1] for m in range(modes)
-    )
-
-
-def inproj(at, lots, rows, modes, pieces, gain, weight, so_far):
+        product[:, m * lanes : (m + 1) * lanes] * mask[0, :, m : m + 1] for m in range(modes)
+    )
+
+
+def inproj(lots, rows, modes, pieces, gain, weight):
     tall, width = pieces[0].shape
-    count = len(pieces)
-    columns = weight.shape[1] // modes
-    here = lambda i: (at, 0, 0)
+    lanes = weight.shape[2]
+    count = len(pieces) // lots
     size = count * rows
-    extra = tuple(so_far or ())
+    block = lambda *shape: pl.BlockSpec((1,) + shape, lambda i: (i, 0, 0))
+    shapes = [
+        jax.ShapeDtypeStruct((lots, size, width), BF),
+        jax.ShapeDtypeStruct((lots, size, lanes), F32),
+        jax.ShapeDtypeStruct((lots, size, modes), F32),
+        jax.ShapeDtypeStruct((lots, 8, rows), F32),
+        jax.ShapeDtypeStruct((width, modes * lanes), BF),
+    ]
     return pl.pallas_call(
-        functools.partial(inproj_kernel, count),
-        grid=(1,),
-        in_specs=[flat(a) for a in (*pieces, gain, weight)]
-        + [pl.BlockSpec(memory_space=pl.ANY)] * len(extra),
-        out_specs=[pl.BlockSpec((1,) + shape, here) for shape in (
-            (size, width), (size, columns), (size, modes), (8, rows)
-        )],
-        out_shape=[
-            jax.ShapeDtypeStruct((lots, size, width), BF),
-            jax.ShapeDtypeStruct((lots, size, columns), F32),
-            jax.ShapeDtypeStruct((lots, size, modes), F32),
-            jax.ShapeDtypeStruct((lots, 8, rows), F32),
+        functools.partial(inproj_kernel, lots),
+        grid=(lots,),
+        in_specs=[pl.BlockSpec(memory_space=pl.ANY)] * len(pieces) + [flat(gain), flat(weight)],
+        out_specs=[block(*a.shape[1:]) for a in shapes[:4]] + [flat(shapes[4])],
+        out_shape=shapes,
+        scratch_shapes=[
+            pltpu.VMEM((2, count, tall, width), BF),
+            pltpu.SemaphoreType.DMA((2, count)),
         ],
-        input_output_aliases={count + 2 + n: n for n in range(len(extra))},
         compiler_params=pltpu.CompilerParams(vmem_limit_bytes=VMEM),
         cost_estimate=pl.CostEstimate(
-            flops=2 * size * width * weight.shape[1],
-            bytes_accessed=6 * size * width,
+            flops=2 * lots * size * width * modes * lanes,
+            bytes_accessed=6 * lots * size * width,
             transcendentals=0,
         ),
-    )(*pieces, gain, weight, *extra)
+    )(*pieces, gain, weight)
 
 
 def conv(table, starts, x, mask, taps, base, xproj):
@@ -884,7 +919,7 @@
     notes = jnp.broadcast_to(jnp.pad(norm_gain, (0, room)), (parts, norm_gain.shape[0] + room))
     moved = collect(exchange(jnp.concatenate(
         [
-            shards(in_weight[:, :, :inner]).reshape(parts, -1, lanes),
+            jnp.swapaxes(shards(in_weight[:, :, :inner]), 1, 2).reshape(parts, -1, lanes),
             shards(dtproj_weight).reshape(parts, -1, lanes),
             notes.reshape(parts, -1, lanes),
         ],
@@ -892,7 +927,6 @@
     )))
     cut = in_weight.shape[0] * modes
     further = cut + rank_rows * modes
-    x_cols = moved[:, :cut].reshape(width, modes * lanes)
     dt_cols = moved[:, cut:further].reshape(rank, modes * lanes)
     gain = moved[:, further:].reshape(parts * lots, -1)[:, : norm_gain.shape[0]]
     gain = gain.reshape(1, width).astype(F32)
@@ -933,12 +967,7 @@
 
     step_pieces = sizes[-1] * sizes[-2]
     lots_in = parts // step_pieces
-    so_far = None
-    for n in range(lots_in):
-        so_far = inproj(
-            n, lots_in, rows, modes, pieces[n * step_pieces : (n + 1) * step_pieces], gain, x_cols, so_far
-        )
-    normed, conv_in, in_masks, notes = so_far
+    normed, conv_in, in_masks, notes, x_cols = inproj(lots_in, rows, modes, pieces, gain, moved)
     masks = in_masks.reshape(groups, blocks, rows, modes)
     notes = notes.reshape(groups, -1, 8, rows)[:, 0, 1].astype(jnp.int32)
     begins = notes[:, 0] * 64 + notes[:, 1]
@@ -967,8 +996,8 @@
 
     def scatter(x, weight, dim, stages):
         got = []
-        chunk = width // 4
-        for n in range(4):
+        chunk = width // 2
+        for n in range(2):
             w = lax.slice_in_dim(weight, n * chunk, (n + 1) * chunk, axis=1 - dim)
             product = dot(x, w, ((1,), (dim,))).astype(BF).reshape(sizes + (rows, chunk))
             got.append(reduce_parts(dims, product, n, stages))

time: 782 us -> 746 us (0.954)
  local copies, waits for them, and re-layouts: 103 us -> 64.5 us
  starting transfers between devices: 104 us -> 91.3 us
  waiting for transfers between devices: 257 us -> 268 us
    unnamed x198 -> x128, local copies, waits for them, and re-layouts: 41.9 us -> 15.8 us
    ppermute x87 -> x75, waiting for transfers between devices: 235 us -> 250 us  [fetch(): return lax.ppermute(x, self.axis, pairs)]
    pallas_call x4 -> x1, Pallas kernels: 26.3 us -> 18.7 us  [inproj(): pl.pallas_call(functools.partial(inproj_kernel, lots), grid=(lots,), in_s...]
    ppermute x87 -> x75, starting transfers between devices: 84.5 us -> 78.9 us  [fetch(): return lax.ppermute(x, self.axis, pairs)]
    convert_element_type x12 -> x6, other arithmetic: 21.1 us -> 20.5 us  [reduce_parts(): x = x.astype(BF)]
    dot_general x7 -> x5, matrix products: 58.5 us -> 58.3 us  [dot(): return lax.dot_general(a, b, (dims, ((), ())), preferred_element_type=F32)]
  transfers between devices with their start and end apart: 93 -> 81, of which waited for: 54 -> 53; matrix products, arithmetic and copies ran while one was open for 21% -> 20% of each run, Pallas kernels for 24% -> 23%
where the time goes in v4:
time: 746 us; the launch traced here: 737 us
  waiting for transfers between devices  268 us (36%)
  Pallas kernels  189 us (25%)
  starting transfers between devices  91.3 us (12%)
  local copies, waits for them, and re-layouts  64.5 us (9%)
  matrix products  58.3 us (8%)
  other arithmetic  47.9 us (6%)
  between operations  18.4 us (2%)
    ppermute x75, waiting for transfers between devices, fetch(): return lax.ppermute(x, self.axis, pairs)  250 us
    ppermute x75, starting transfers between devices, fetch(): return lax.ppermute(x, self.axis, pairs)  78.9 us
    pallas_call x1, Pallas kernels, scan_back(): pl.pallas_call(functools.partial(back_kernel, groups, length, states, las...  62.5 us
    dot_general x5, matrix products, dot(): return lax.dot_general(a, b, (dims, ((), ())), preferred_element_type=F32)  58.3 us
    pallas_call x1, Pallas kernels, scan(): pl.pallas_call(functools.partial(scan_kernel, groups, length, states), gr...  39.4 us
    pallas_call x1, Pallas kernels, cot_part(): pl.pallas_call(cot_kernel, grid_spec=pltpu.PrefetchScalarGridSpec(num_sca...  23.3 us
    convert_element_type x6, other arithmetic, reduce_parts(): x = x.astype(BF)  20.5 us
    pallas_call x1, Pallas kernels, inproj(): pl.pallas_call(functools.partial(inproj_kernel, lots), grid=(lots,), in_s...  18.7 us
  transfers between devices with their start and end apart: 81, of which 53 were waited for; matrix products, arithmetic and copies ran while one was open for 20% of the time, Pallas kernels for 23%

profile of v4, /device:TPU:0, one launch (start us, length us, event | category | flops | bytes accessed | tf_op | source)
XLA Modules:
  0.0 736.6 jit_solution(16169357190510263989)
XLA Ops:
  19.4 8.1 %collective-permute-done.1.refs_2_ = bf16[144,2048]{1,0:T(8,128)(2,1)S(1)} collective-permute-done((bf16[144,2048]{1,0:T(8,128)(2,1)S(1)}, bf16[144,2048]{1,0:T(8,128)(2,1)S(1)}, u32[]{:S(2)}, u32[]{:S(2)}) %collective-permute-start.1) | collective-permute-done | bytes 589856 | tf_op jit(solution)/shard_map/ppermute | solution.py:747
  45.7 7.2 collective-permute-done.9.refs_10_
  52.9 15.7 %collective-permute-done.17.refs_18_ = bf16[144,2048]{1,0:T(8,128)(2,1)S(1)} collective-permute-done((bf16[144,2048]{1,0:T(8,128)(2,1)S(1)}, bf16[144,2048]{1,0:T(8,128)(2,1)S(1)}, u32[]{:S(2)}, u32[]{:S(2)}) %collective-permute-start.17) | collective-permute-done | bytes 589856 | tf_op jit(solution)/shard_map/ppermute | solution.py:747
  78.8 9.0 %collective-permute-done.5.refs_6_ = bf16[144,2048]{1,0:T(8,128)(2,1)S(1)} collective-permute-done((bf16[144,2048]{1,0:T(8,128)(2,1)}, bf16[144,2048]{1,0:T(8,128)(2,1)S(1)}, u32[]{:S(2)}, u32[]{:S(2)}) %collective-permute-start.5) | collective-permute-done | bytes 589856 | tf_op jit(solution)/shard_map/ppermute | solution.py:747
  90.8 8.3 %collective-permute-done.25.refs_26_ = bf16[144,2048]{1,0:T(8,128)(2,1)} collective-permute-done((bf16[144,2048]{1,0:T(8,128)(2,1)}, bf16[144,2048]{1,0:T(8,128)(2,1)}, u32[]{:S(2)}, u32[]{:S(2)}) %collective-permute-start.25) | collective-permute-done | bytes 589856 | tf_op jit(solution)/shard_map/ppermute | solution.py:747
  106.0 6.5 collective-permute-done.21.refs_22_
  119.1 5.4 collective-permute-done.29.refs_30_
  127.0 18.7 %shard_map.265 = (bf16[4,1024,2048]{2,1,0:T(8,128)(2,1)}, f32[4,1024,128]{2,1,0:T(8,128)}, f32[4,1024,3]{2,1,0:T(8,128)}, f32[4,8,128]{2,1,0:T(8,128)}, bf16[2048,384]{1,0:T(8,128)(2,1)}) custom-call(bf16[144,2048]{1,0:T(8,128)(2,1)} %copy-done.23, bf16[144,2048]{1,0:T(8,128)(2,1)} %collective-permute-done.refs_1_, bf16[144,2048]{1,0:T(8,128)(2,1)} %copy-done.40, ...), custom_call_target="tpu_custom_call" | custom-call | flops 6442450944 | bytes 50331648 | tf_op jit(solution)/shard_map/pallas_call | solution.py:435
  152.4 12.3 %shard_map.266 = (f32[4,8,128,128]{3,2,1,0:T(8,128)}, f32[4,8,128,128]{3,2,1,0:T(8,128)}, f32[4,8,160,128]{3,2,1,0:T(8,128)}) custom-call(s32[8]{0:T(128)} %fusion.35.table, s32[4]{0:T(128)} %add_reduce_fusion.starts, f32[4,8,128,128]{3,2,1,0:T(8,128)} %bitcast.156, f32[4,8,128,3]{3,2,1,0:T(8,128)} %bitcast.146, f32[4,128]{1,0:T(4,128)} %convert_bitcast_fusion.2.taps, ...), custom_call_target="tpu_custom_call" | custom-call | tf_op jit(solution)/shard_map/pallas_call | solution.py:461
  196.0 5.7 collective-permute-done.37
  201.8 7.8 %collective-permute-start.39 = (bf16[1,1,1,1,192,128]{5,4,3,2,1,0:T(8,128)(2,1)S(1)}, bf16[1,1,1,1,192,128]{5,4,3,2,1,0:T(8,128)(2,1)S(1)}, u32[]{:S(2)}, u32[]{:S(2)}) collective-permute-start(bf16[1,1,1,1,192,128]{5,4,3,2,1,0:T(8,128)(2,1)S(1)} %maximum_bitcast_fusion), channel_id=1, source_target_pairs={{2,0},{3,1},{4,2},{5,3},{6,4},{7,5},{0,6},{1,7},{10,8},{11,9},{12,... | collective-permute-start | bytes 147464 | tf_op jit(solution)/shard_map/ppermute | solution.py:747
  224.0 8.0 %collective-permute-done.43 = bf16[2,1,4,1,96,128]{5,4,3,2,1,0:T(8,128)(2,1)S(1)} collective-permute-done((bf16[2,1,4,1,96,128]{5,4,3,2,1,0:T(8,128)(2,1)S(1)}, bf16[2,1,4,1,96,128]{5,4,3,2,1,0:T(8,128)(2,1)S(1)}, u32[]{:S(2)}, u32[]{:S(2)}) %collective-permute-start.43) | collective-permute-done | bytes 196640 | tf_op jit(solution)/shard_map/ppermute | solution.py:747
  248.3 39.4 %shard_map.267 = (f32[4,8,128,128]{3,2,1,0:T(8,128)}, f32[4,8,128,128]{3,2,1,0:T(8,128)}, f32[65536,128]{1,0:T(8,128)}, f32[64,128]{1,0:T(8,128)}) custom-call(s32[8]{0:T(128)} %fusion.35.table, s32[4]{0:T(128)} %add_reduce_fusion.starts, f32[4,8,128,128]{3,2,1,0:T(8,128)} %get-tuple-element.45.act, bf16[4,8,192,128]{3,2,1,0:T(8,128)(2,1)} %bitcast.166, ...), custom_call_target="tpu_custom_call" | custom-call | flops 10000000000 | bytes 100000000 | tf_op jit(solution)/shard_map/pallas_call | solution.py:545
  287.7 16.6 %all-to-all-done.1 = bf16[32,64,3,128]{3,1,2,0:T(8,128)(2,1)S(1)} async-done(((bf16[32,64,3,128]{3,1,2,0:T(8,128)(2,1)}), bf16[32,64,3,128]{3,1,2,0:T(8,128)(2,1)S(1)}, u32[]{:S(2)}, u32[]{:S(2)}) %all-to-all-start.1) | async-done | bytes 1572896 | tf_op jit(solution)/shard_map/all_to_all | solution.py:881
  309.4 15.3 %shard_map.268 = (f32[4,1024,128]{2,1,0:T(8,128)}, bf16[4,1024,128]{2,1,0:T(8,128)(2,1)}, bf16[4,1024,384]{2,1,0:T(8,128)(2,1)}) custom-call(s32[4]{0:T(128)} %fusion.33.lots_at, s32[8]{0:T(128)} %fusion.34.spans_at, bf16[4,1024,2048]{2,1,0:T(8,128)(2,1)} %get-tuple-element.40.normed, bf16[2048,384]{1,0:T(8,128)(2,1)} %get-tuple-element.95.weight, ...), custom_call_target="tpu_custom_call" | custom-call | flops 6442450944 | bytes 25165824 | tf_op jit(solution)/shard_map/pallas_call | solution.py:601
  324.8 14.4 %convolution_convert_fusion = bf16[4096,2048]{1,0:T(8,128)(2,1)} fusion(bf16[4096,384]{1,0:T(8,128)(2,1)} %bitcast.201, bf16[384,2048]{1,0:T(8,128)(2,1)S(1)} %bitcast.194), kind=kOutput, calls=%fused_computation | convolution fusion | flops 6450839552 | bytes 21495808 | tf_op jit(solution)/shard_map/dot_general | solution.py:21
  340.5 23.3 %shard_map.269 = (f32[4,1024,128]{2,1,0:T(8,128)}, bf16[4,1024,384]{2,1,0:T(8,128)(2,1)}, f32[384,2048]{1,0:T(8,128)}) custom-call(s32[4]{0:T(128)} %fusion.33.lots_at, s32[8]{0:T(128)} %fusion.34.spans_at, bf16[4,1024,2048]{2,1,0:T(8,128)(2,1)} %bitcast.189, bf16[384,2048]{1,0:T(8,128)(2,1)} %bitcast.193, f32[4,1024,3]{2,1,0:T(8,128)} %get-tuple-element.43.mask, ...), custom_call_target="tpu_custom_call" | custom-call | flops 12884901888 | bytes 25165824 | tf_op jit(solution)/shard_map/pallas_call | solution.py:712
  363.8 62.5 %shard_map.270 = (f32[4,8,128,128]{3,2,1,0:T(8,128)}, f32[4,8,160,128]{3,2,1,0:T(8,128)}, f32[128,128]{1,0:T(8,128)}, f32[64,128]{1,0:T(8,128)}, f32[128,384]{1,...) custom-call(s32[8]{0:T(128)} %fusion.35.table, s32[4]{0:T(128)} %add_reduce_fusion.starts, ...), custom_call_target="tpu_custom_call" | custom-call | flops 10000000000 | bytes 200000000 | tf_op jit(solution)/shard_map/pallas_call | solution.py:650
  432.4 8.7 %collective-permute-done.50 = bf16[2,1,4,1,80,128]{5,4,3,2,1,0:T(8,128)(2,1)S(1)} collective-permute-done((bf16[2,1,4,1,80,128]{5,4,3,2,1,0:T(8,128)(2,1)S(1)}, bf16[2,1,4,1,80,128]{5,4,3,2,1,0:T(8,128)(2,1)S(1)}, u32[]{:S(2)}, u32[]{:S(2)}) %collective-permute-start.50) | collective-permute-done | bytes 163872 | tf_op jit(solution)/shard_map/ppermute | solution.py:747
  442.3 8.0 %collective-permute-done.51 = f32[1,1,4,1,80,128]{5,4,3,2,1,0:T(8,128)S(1)} collective-permute-done((f32[1,1,4,1,80,128]{5,4,3,2,1,0:T(8,128)S(1)}, f32[1,1,4,1,80,128]{5,4,3,2,1,0:T(8,128)S(1)}, u32[]{:S(2)}, u32[]{:S(2)}) %collective-permute-start.51) | collective-permute-done | bytes 163872 | tf_op jit(solution)/shard_map/ppermute | solution.py:747
  454.8 5.2 collective-permute-done.52
  470.2 5.2 collective-permute-done.56
  494.0 17.1 %shard_map.271 = (bf16[4,8,128,384]{3,2,1,0:T(8,128)(2,1)}, f32[8,128]{1,0:T(8,128)}, f32[1,128]{1,0:T(1,128)}, f32[128,480]{1,0:T(8,128)}) custom-call(s32[8]{0:T(128)} %fusion.35.table, s32[4]{0:T(128)} %add_reduce_fusion.starts, f32[4,8,128,128]{3,2,1,0:T(8,128)} %get-tuple-element.54.grad, bf16[4,8,160,128]{3,2,1,0:T(8,128)(2,1)} %bitcast.168, ...), custom_call_target="tpu_custom_call" | custom-call | tf_op jit(solution)/shard_map/pallas_call | solution.py:495
  511.1 9.9 %convolution_convert_fusion.2 = bf16[4096,1024]{1,0:T(8,128)(2,1)S(1)} fusion(bf16[4096,384]{1,0:T(8,128)(2,1)} %bitcast.199, bf16[4096,384]{1,0:T(8,128)(2,1)} %bitcast.190, bf16[2048,768]{1,0:T(8,128)(2,1)S(1)} %copy-done.22), kind=kOutput, calls=%fused_computation.4 | convolution fusion | flops 6459228160 | bytes 16252928 | tf_op jit(solution)/shard_map/dot_general | solution.py:21
  528.4 7.2 convolution_convert_fusion.1
  542.2 12.5 %fusion = bf16[2048,384]{1,0:T(8,128)(2,1)S(1)} fusion(bf16[4,1024,2048]{2,1,0:T(8,128)(2,1)} %get-tuple-element.40.normed, bf16[4,1024,384]{2,1,0:T(8,128)(2,1)S(1)} %copy-done.60, bf16[]{:T(256)} %bitcast.54), kind=kOutput, calls=%fused_computation.12 | convolution fusion | flops 6444023808 | bytes 21495810 | tf_op jit(solution)/shard_map/dot_general | solution.py:21
  559.5 14.2 %convolution_convert_fusion.3 = bf16[2048,384]{1,0:T(8,128)(2,1)} fusion(bf16[4096,2048]{1,0:T(8,128)(2,1)} %bitcast.197, bf16[4096,384]{1,0:T(8,128)(2,1)} %bitcast.191), kind=kOutput, calls=%fused_computation.11 | convolution fusion | flops 6443237376 | bytes 21495808 | tf_op jit(solution)/shard_map/dot_general | solution.py:21
  576.3 5.6 add_convert_fusion.1
  586.5 5.6 add_convert_fusion
  602.2 47.5 %collective-permute-done.64 = bf16[1,2,4,1,128,1024]{5,4,3,2,1,0:T(8,128)(2,1)} collective-permute-done((bf16[1,2,4,1,128,1024]{5,4,3,2,1,0:T(8,128)(2,1)}, bf16[1,2,4,1,128,1024]{5,4,3,2,1,0:T(8,128)(2,1)}, u32[]{:S(2)}, u32[]{:S(2)}) %collective-permute-start.64) | collective-permute-done | bytes 2097184 | tf_op jit(solution)/shard_map/ppermute | solution.py:747
  701.8 5.8 collective-permute-done.67
  707.7 5.5 collective-permute-done.73
  (399 shorter events, 276.1 us)
Async XLA Ops:
  9.8 17.7 %collective-permute-start.1 = (bf16[144,2048]{1,0:T(8,128)(2,1)S(1)}, bf16[144,2048]{1,0:T(8,128)(2,1)S(1)}, u32[]{:S(2)}, u32[]{:S(2)}) collective-permute-start(bf16[144,2048]{1,0:T(8,128)(2,1)S(1)} %fusion.11.refs_0_), channel_id=1, source_target_pairs={{2,0},{3,1},{4,2},{5,3},{6,4},{7,5},{0,6},{1,7},{10,8},{11,9},{12,... | collective-permute-start | bytes 1769480 | tf_op jit(solution)/shard_map/ppermute | solution.py:747
  14.9 22.5 %collective-permute-start.15 = (bf16[144,2048]{1,0:T(8,128)(2,1)S(1)}, bf16[144,2048]{1,0:T(8,128)(2,1)}, u32[]{:S(2)}, u32[]{:S(2)}) collective-permute-start(bf16[144,2048]{1,0:T(8,128)(2,1)S(1)} %fusion.11.refs_0_), channel_id=1, source_target_pairs={{16,0},{24,8},{0,16},{8,24},{17,1},{25,9},{1,17},{9,25},{18,2},{26... | collective-permute-start | bytes 1769480 | tf_op jit(solution)/shard_map/ppermute | solution.py:747
  16.4 22.7 %collective-permute-start.7 = (bf16[144,2048]{1,0:T(8,128)(2,1)S(1)}, bf16[144,2048]{1,0:T(8,128)(2,1)}, u32[]{:S(2)}, u32[]{:S(2)}) collective-permute-start(bf16[144,2048]{1,0:T(8,128)(2,1)S(1)} %fusion.11.refs_0_), channel_id=1, source_target_pairs={{8,0},{0,8},{24,16},{16,24},{9,1},{1,9},{25,17},{17,25},{10,2},{2,... | collective-permute-start | bytes 1769480 | tf_op jit(solution)/shard_map/ppermute | solution.py:747
  17.9 21.2 %collective-permute-start = (bf16[144,2048]{1,0:T(8,128)(2,1)S(1)}, bf16[144,2048]{1,0:T(8,128)(2,1)}, u32[]{:S(2)}, u32[]{:S(2)}) collective-permute-start(bf16[144,2048]{1,0:T(8,128)(2,1)S(1)} %fusion.11.refs_0_), channel_id=1, source_target_pairs={{1,0},{0,1},{3,2},{2,3},{5,4},{4,5},{7,6},{6,7},{9,8},{8,9},{11,10... | collective-permute-start | bytes 1769480 | tf_op jit(solution)/shard_map/ppermute | solution.py:747
  27.5 18.1 %collective-permute-start.3 = (bf16[144,2048]{1,0:T(8,128)(2,1)S(1)}, bf16[144,2048]{1,0:T(8,128)(2,1)}, u32[]{:S(2)}, u32[]{:S(2)}) collective-permute-start(bf16[144,2048]{1,0:T(8,128)(2,1)S(1)} %collective-permute-done.1.refs_2_), channel_id=1, source_target_pairs={{2,0},{3,1},{4,2},{5,3},{6,4},{7,5},{0,6},{1,7},{10,8},{11,9},{12,... | collective-permute-start | bytes 1769480 | tf_op jit(solution)/shard_map/ppermute | solution.py:747
  31.8 21.1 %collective-permute-start.9 = (bf16[144,2048]{1,0:T(8,128)(2,1)S(1)}, bf16[144,2048]{1,0:T(8,128)(2,1)}, u32[]{:S(2)}, u32[]{:S(2)}) collective-permute-start(bf16[144,2048]{1,0:T(8,128)(2,1)S(1)} %collective-permute-done.1.refs_2_), channel_id=1, source_target_pairs={{8,0},{0,8},{24,16},{16,24},{9,1},{1,9},{25,17},{17,25},{10,2},{2,... | collective-permute-start | bytes 1769480 | tf_op jit(solution)/shard_map/ppermute | solution.py:747
  34.6 90.0 %all-to-all-start = ((bf16[32,205,128]{2,1,0:T(8,128)(2,1)}), bf16[32,205,128]{2,1,0:T(8,128)(2,1)S(1)}, u32[]{:S(2)}, u32[]{:S(2)}) async-start(bf16[32,205,128]{2,1,0:T(8,128)(2,1)} %pad_maximum_fusion.3), calls=%async_computation | async-start | bytes 3407872 | tf_op jit(solution)/shard_map/all_to_all | solution.py:881
  37.3 303.2 %all-gather.3.cloned.1.call-start = ((), (), s32[]{:S(2)}) async-start(), calls=%async_computation.6 | async-start | bytes 17301504 | tf_op jit(solution)/shard_map/all_gather | solution.py:974
  37.4 31.2 %collective-permute-start.17 = (bf16[144,2048]{1,0:T(8,128)(2,1)S(1)}, bf16[144,2048]{1,0:T(8,128)(2,1)S(1)}, u32[]{:S(2)}, u32[]{:S(2)}) collective-permute-start(bf16[144,2048]{1,0:T(8,128)(2,1)S(1)} %collective-permute-done.1.refs_2_), channel_id=1, source_target_pairs={{16,0},{24,8},{0,16},{8,24},{17,1},{25,9},{1,17},{9,25},{18,2},{26... | collective-permute-start | bytes 1769480 | tf_op jit(solution)/shard_map/ppermute | solution.py:747
  39.1 31.3 %collective-permute-start.2 = (bf16[144,2048]{1,0:T(8,128)(2,1)S(1)}, bf16[144,2048]{1,0:T(8,128)(2,1)S(1)}, u32[]{:S(2)}, u32[]{:S(2)}) collective-permute-start(bf16[144,2048]{1,0:T(8,128)(2,1)S(1)} %collective-permute-done.1.refs_2_), channel_id=1, source_target_pairs={{1,0},{0,1},{3,2},{2,3},{5,4},{4,5},{7,6},{6,7},{9,8},{8,9},{11,10... | collective-permute-start | bytes 1769480 | tf_op jit(solution)/shard_map/ppermute | solution.py:747
  39.1 35.8 %collective-permute-start.23 = (bf16[144,2048]{1,0:T(8,128)(2,1)}, bf16[144,2048]{1,0:T(8,128)(2,1)S(1)}, u32[]{:S(2)}, u32[]{:S(2)}) collective-permute-start(bf16[144,2048]{1,0:T(8,128)(2,1)} %collective-permute-done.15.refs_16_), channel_id=1, source_target_pairs={{8,0},{0,8},{24,16},{16,24},{9,1},{1,9},{25,17},{17,25},{10,2},{2,... | collective-permute-start | bytes 1769480 | tf_op jit(solution)/shard_map/ppermute | solution.py:747
  45.7 31.3 %collective-permute-start.16 = (bf16[144,2048]{1,0:T(8,128)(2,1)}, bf16[144,2048]{1,0:T(8,128)(2,1)S(1)}, u32[]{:S(2)}, u32[]{:S(2)}) collective-permute-start(bf16[144,2048]{1,0:T(8,128)(2,1)} %collective-permute-done.15.refs_16_), channel_id=1, source_target_pairs={{1,0},{0,1},{3,2},{2,3},{5,4},{4,5},{7,6},{6,7},{9,8},{8,9},{11,10... | collective-permute-start | bytes 1769480 | tf_op jit(solution)/shard_map/ppermute | solution.py:747
  52.9 24.1 %collective-permute-start.8 = (bf16[144,2048]{1,0:T(8,128)(2,1)}, bf16[144,2048]{1,0:T(8,128)(2,1)S(1)}, u32[]{:S(2)}, u32[]{:S(2)}) collective-permute-start(bf16[144,2048]{1,0:T(8,128)(2,1)} %collective-permute-done.7.refs_8_), channel_id=1, source_target_pairs={{1,0},{0,1},{3,2},{2,3},{5,4},{4,5},{7,6},{6,7},{9,8},{8,9},{11,10... | collective-permute-start | bytes 1769480 | tf_op jit(solution)/shard_map/ppermute | solution.py:747
  68.6 19.2 %collective-permute-start.5 = (bf16[144,2048]{1,0:T(8,128)(2,1)}, bf16[144,2048]{1,0:T(8,128)(2,1)S(1)}, u32[]{:S(2)}, u32[]{:S(2)}) collective-permute-start(bf16[144,2048]{1,0:T(8,128)(2,1)} %collective-permute-done.3.refs_4_), channel_id=1, source_target_pairs={{2,0},{3,1},{4,2},{5,3},{6,4},{7,5},{0,6},{1,7},{10,8},{11,9},{12,... | collective-permute-start | bytes 1769480 | tf_op jit(solution)/shard_map/ppermute | solution.py:747
  70.5 18.8 %collective-permute-start.19 = (bf16[144,2048]{1,0:T(8,128)(2,1)}, bf16[144,2048]{1,0:T(8,128)(2,1)S(1)}, u32[]{:S(2)}, u32[]{:S(2)}) collective-permute-start(bf16[144,2048]{1,0:T(8,128)(2,1)} %collective-permute-done.3.refs_4_), channel_id=1, source_target_pairs={{16,0},{24,8},{0,16},{8,24},{17,1},{25,9},{1,17},{9,25},{18,2},{26... | collective-permute-start | bytes 1769480 | tf_op jit(solution)/shard_map/ppermute | solution.py:747
  74.9 14.7 %collective-permute-start.11 = (bf16[144,2048]{1,0:T(8,128)(2,1)}, bf16[144,2048]{1,0:T(8,128)(2,1)S(1)}, u32[]{:S(2)}, u32[]{:S(2)}) collective-permute-start(bf16[144,2048]{1,0:T(8,128)(2,1)} %collective-permute-done.3.refs_4_), channel_id=1, source_target_pairs={{8,0},{0,8},{24,16},{16,24},{9,1},{1,9},{25,17},{17,25},{10,2},{2,... | collective-permute-start | bytes 1769480 | tf_op jit(solution)/shard_map/ppermute | solution.py:747
  77.0 22.2 %collective-permute-start.25 = (bf16[144,2048]{1,0:T(8,128)(2,1)}, bf16[144,2048]{1,0:T(8,128)(2,1)}, u32[]{:S(2)}, u32[]{:S(2)}) collective-permute-start(bf16[144,2048]{1,0:T(8,128)(2,1)} %collective-permute-done.9.refs_10_), channel_id=1, source_target_pairs={{16,0},{24,8},{0,16},{8,24},{17,1},{25,9},{1,17},{9,25},{18,2},{26... | collective-permute-start | bytes 1769480 | tf_op jit(solution)/shard_map/ppermute | solution.py:747
  89.7 16.3 %collective-permute-start.13 = (bf16[144,2048]{1,0:T(8,128)(2,1)S(1)}, bf16[144,2048]{1,0:T(8,128)(2,1)}, u32[]{:S(2)}, u32[]{:S(2)}) collective-permute-start(bf16[144,2048]{1,0:T(8,128)(2,1)S(1)} %collective-permute-done.5.refs_6_), channel_id=1, source_target_pairs={{8,0},{0,8},{24,16},{16,24},{9,1},{1,9},{25,17},{17,25},{10,2},{2,... | collective-permute-start | bytes 1769480 | tf_op jit(solution)/shard_map/ppermute | solution.py:747
  99.7 18.4 %collective-permute-start.27 = (bf16[144,2048]{1,0:T(8,128)(2,1)S(1)}, bf16[144,2048]{1,0:T(8,128)(2,1)}, u32[]{:S(2)}, u32[]{:S(2)}) collective-permute-start(bf16[144,2048]{1,0:T(8,128)(2,1)S(1)} %collective-permute-done.19.refs_20_), channel_id=1, source_target_pairs={{8,0},{0,8},{24,16},{16,24},{9,1},{1,9},{25,17},{17,25},{10,2},{2,... | collective-permute-start | bytes 1769480 | tf_op jit(solution)/shard_map/ppermute | solution.py:747
  100.9 17.1 %collective-permute-start.6 = (bf16[144,2048]{1,0:T(8,128)(2,1)S(1)}, bf16[144,2048]{1,0:T(8,128)(2,1)S(1)}, u32[]{:S(2)}, u32[]{:S(2)}) collective-permute-start(bf16[144,2048]{1,0:T(8,128)(2,1)S(1)} %collective-permute-done.5.refs_6_), channel_id=1, source_target_pairs={{1,0},{0,1},{3,2},{2,3},{5,4},{4,5},{7,6},{6,7},{9,8},{8,9},{11,10... | collective-permute-start | bytes 1769480 | tf_op jit(solution)/shard_map/ppermute | solution.py:747
  100.9 17.6 %collective-permute-start.20 = (bf16[144,2048]{1,0:T(8,128)(2,1)S(1)}, bf16[144,2048]{1,0:T(8,128)(2,1)S(1)}, u32[]{:S(2)}, u32[]{:S(2)}) collective-permute-start(bf16[144,2048]{1,0:T(8,128)(2,1)S(1)} %collective-permute-done.19.refs_20_), channel_id=1, source_target_pairs={{1,0},{0,1},{3,2},{2,3},{5,4},{4,5},{7,6},{6,7},{9,8},{8,9},{11,10... | collective-permute-start | bytes 1769480 | tf_op jit(solution)/shard_map/ppermute | solution.py:747
  240.6 63.6 %all-to-all-start.1 = ((bf16[32,64,3,128]{3,1,2,0:T(8,128)(2,1)}), bf16[32,64,3,128]{3,1,2,0:T(8,128)(2,1)S(1)}, u32[]{:S(2)}, u32[]{:S(2)}) async-start(bf16[32,64,3,128]{3,1,2,0:T(8,128)(2,1)} %copy.88), calls=%async_computation.1 | async-start | bytes 3145728 | tf_op jit(solution)/shard_map/all_to_all | solution.py:881
  243.5 481.3 %reduce-scatter.2.cloned.1.call-start = ((), (), s32[]{:S(2)}) async-start(), calls=%async_computation.5 | async-start | bytes 17301504 | tf_op jit(solution)/shard_map/reduce_scatter | solution.py:1007
  527.3 49.0 %collective-permute-start.63 = (bf16[2,2,4,1,128,1024]{5,4,3,2,1,0:T(8,128)(2,1)}, bf16[2,2,4,1,128,1024]{5,4,3,2,1,0:T(8,128)(2,1)}, u32[]{:S(2)}, u32[]{:S(2)}) collective-permute-start(bf16[2,2,4,1,128,1024]{5,4,3,2,1,0:T(8,128)(2,1)} %slice.323), channel_id=1, source_target_pairs={{1,0},{0,1},{3,2},{2,3},{5,4},{4,5},{7,6},{6,7},{9,8},{8,9},{11,10... | collective-permute-start | bytes 12582920 | tf_op jit(solution)/shard_map/ppermute | solution.py:747
  540.2 46.3 %collective-permute-start.69 = (bf16[2,2,4,1,128,1024]{5,4,3,2,1,0:T(8,128)(2,1)}, bf16[2,2,4,1,128,1024]{5,4,3,2,1,0:T(8,128)(2,1)}, u32[]{:S(2)}, u32[]{:S(2)}) collective-permute-start(bf16[2,2,4,1,128,1024]{5,4,3,2,1,0:T(8,128)(2,1)} %slice.334), channel_id=1, source_target_pairs={{1,0},{0,1},{3,2},{2,3},{5,4},{4,5},{7,6},{6,7},{9,8},{8,9},{11,10... | collective-permute-start | bytes 12582920 | tf_op jit(solution)/shard_map/ppermute | solution.py:747
  556.3 42.0 %all-to-all-start.3 = ((bf16[32,192,128]{2,1,0:T(8,128)(2,1)}), bf16[32,192,128]{2,1,0:T(8,128)(2,1)S(1)}, u32[]{:S(2)}, u32[]{:S(2)}) async-start(bf16[32,192,128]{2,1,0:T(8,128)(2,1)} %add.315), calls=%async_computation.4 | async-start | bytes 3145728 | tf_op jit(solution)/shard_map/all_to_all | solution.py:881
  584.7 64.9 %collective-permute-start.64 = (bf16[1,2,4,1,128,1024]{5,4,3,2,1,0:T(8,128)(2,1)}, bf16[1,2,4,1,128,1024]{5,4,3,2,1,0:T(8,128)(2,1)}, u32[]{:S(2)}, u32[]{:S(2)}) collective-permute-start(bf16[1,2,4,1,128,1024]{5,4,3,2,1,0:T(8,128)(2,1)} %slice.325), channel_id=1, source_target_pairs={{16,0},{24,8},{0,16},{8,24},{17,1},{25,9},{1,17},{9,25},{18,2},{26... | collective-permute-start | bytes 6291464 | tf_op jit(solution)/shard_map/ppermute | solution.py:747
  594.8 62.5 %collective-permute-start.70 = (bf16[2,1,4,1,128,1024]{5,4,3,2,1,0:T(8,128)(2,1)}, bf16[2,1,4,1,128,1024]{5,4,3,2,1,0:T(8,128)(2,1)}, u32[]{:S(2)}, u32[]{:S(2)}) collective-permute-start(bf16[2,1,4,1,128,1024]{5,4,3,2,1,0:T(8,128)(2,1)} %slice.336), channel_id=1, source_target_pairs={{8,0},{0,8},{24,16},{16,24},{9,1},{1,9},{25,17},{17,25},{10,2},{2,... | collective-permute-start | bytes 6291464 | tf_op jit(solution)/shard_map/ppermute | solution.py:747
  598.3 75.0 %all-to-all-start.2 = ((bf16[32,204,128]{2,1,0:T(8,128)(2,1)}), bf16[32,204,128]{2,1,0:T(8,128)(2,1)}, u32[]{:S(2)}, u32[]{:S(2)}) async-start(bf16[32,204,128]{2,1,0:T(8,128)(2,1)} %pad_maximum_fusion.4), calls=%async_computation.3 | async-start | bytes 3407872 | tf_op jit(solution)/shard_map/all_to_all | solution.py:881
  654.1 29.4 %collective-permute-start.65 = (bf16[1,1,4,1,128,1024]{5,4,3,2,1,0:T(8,128)(2,1)}, bf16[1,1,4,1,128,1024]{5,4,3,2,1,0:T(8,128)(2,1)}, u32[]{:S(2)}, u32[]{:S(2)}) collective-permute-start(bf16[1,1,4,1,128,1024]{5,4,3,2,1,0:T(8,128)(2,1)} %slice.327), channel_id=1, source_target_pairs={{8,0},{0,8},{24,16},{16,24},{9,1},{1,9},{25,17},{17,25},{10,2},{2,... | collective-permute-start | bytes 3145736 | tf_op jit(solution)/shard_map/ppermute | solution.py:747
  662.2 24.4 %collective-permute-start.71 = (bf16[1,1,4,1,128,1024]{5,4,3,2,1,0:T(8,128)(2,1)}, bf16[1,1,4,1,128,1024]{5,4,3,2,1,0:T(8,128)(2,1)}, u32[]{:S(2)}, u32[]{:S(2)}) collective-permute-start(bf16[1,1,4,1,128,1024]{5,4,3,2,1,0:T(8,128)(2,1)} %slice.338), channel_id=1, source_target_pairs={{16,0},{24,8},{0,16},{8,24},{17,1},{25,9},{1,17},{9,25},{18,2},{26... | collective-permute-start | bytes 3145736 | tf_op jit(solution)/shard_map/ppermute | solution.py:747
  688.3 13.4 %collective-permute-start.72 = (bf16[1,1,1,1,128,1024]{5,4,3,2,1,0:T(8,128)(2,1)S(1)}, bf16[1,1,1,1,128,1024]{5,4,3,2,1,0:T(8,128)(2,1)S(1)}, u32[]{:S(2)}, u32[]{:S(2)}) collective-permute-start(bf16[1,1,1,1,128,1024]{5,4,3,2,1,0:T(8,128)(2,1)S(1)} %slice.342), channel_id=1, source_target_pairs={{6,0},{7,1},{0,2},{1,3},{2,4},{3,5},{4,6},{5,7},{14,8},{15,9},{8,1... | collective-permute-start | bytes 786440 | tf_op jit(solution)/shard_map/ppermute | solution.py:747
  (112 other events, 1266.7 us)
Sparse Core Ops, SparseCore 0:
  148.5 153.5 all-gather.2
  339.3 191.7 reduce-scatter.1

commit v5 on v4

--- a/solution.py
+++ b/solution.py
@@ -154,7 +154,7 @@
         return tuple(out)
 
     first = tuple(state[s * 8 : s * 8 + 8, :] for s in range(count))
-    last = lax.fori_loop(0, length, one, first, unroll=4)
+    last = lax.fori_loop(0, length, one, first, unroll=8)
     for s in range(count):
         state[s * 8 : s * 8 + 8, :] = last[s]
     end[...] = state[...]
@@ -223,7 +223,7 @@
         return tuple(ref[s * 8 : s * 8 + 8, :] for s in range(count))
 
     c, h, r = lax.fori_loop(
-        0, length, one, (parts(carry), parts(held), parts(rate_grad)), unroll=2
+        0, length, one, (parts(carry), parts(held), parts(rate_grad)), unroll=4
     )
     for s in range(count):
         carry[s * 8 : s * 8 + 8, :] = c[s]

time: 746 us -> 745 us (level)
  no operation moved by 1% of the time
where the time goes in v5:
time: 745 us; the launch traced here: 735 us
  waiting for transfers between devices  269 us (36%)
  Pallas kernels  186 us (25%)
  starting transfers between devices  91.3 us (12%)
  local copies, waits for them, and re-layouts  64.5 us (9%)
  matrix products  58.3 us (8%)
  other arithmetic  47.9 us (6%)
  between operations  18.4 us (2%)
    ppermute x75, waiting for transfers between devices, fetch(): return lax.ppermute(x, self.axis, pairs)  250 us
    ppermute x75, starting transfers between devices, fetch(): return lax.ppermute(x, self.axis, pairs)  79 us
    pallas_call x1, Pallas kernels, scan_back(): pl.pallas_call(functools.partial(back_kernel, groups, length, states, las...  61 us
    dot_general x5, matrix products, dot(): return lax.dot_general(a, b, (dims, ((), ())), preferred_element_type=F32)  58.3 us
    pallas_call x1, Pallas kernels, scan(): pl.pallas_call(functools.partial(scan_kernel, groups, length, states), gr...  37.9 us
    pallas_call x1, Pallas kernels, cot_part(): pl.pallas_call(cot_kernel, grid_spec=pltpu.PrefetchScalarGridSpec(num_sca...  23.3 us
    convert_element_type x6, other arithmetic, reduce_parts(): x = x.astype(BF)  20.5 us
    all_to_all x4, waiting for transfers between devices, exchange(): return lax.all_to_all(x, chan, 0, 0, tiled=True)  18.7 us
  transfers between devices with their start and end apart: 81, of which 53 were waited for; matrix products, arithmetic and copies ran while one was open for 20% of the time, Pallas kernels for 23%

profile of v5, /device:TPU:0, one launch (start us, length us, event | category | flops | bytes accessed | tf_op | source)
XLA Modules:
  0.0 735.3 jit_solution(6842362647884704940)
XLA Ops:
  19.4 8.1 %collective-permute-done.1.refs_2_ = bf16[144,2048]{1,0:T(8,128)(2,1)S(1)} collective-permute-done((bf16[144,2048]{1,0:T(8,128)(2,1)S(1)}, bf16[144,2048]{1,0:T(8,128)(2,1)S(1)}, u32[]{:S(2)}, u32[]{:S(2)}) %collective-permute-start.1) | collective-permute-done | bytes 589856 | tf_op jit(solution)/shard_map/ppermute | solution.py:747
  45.7 7.2 collective-permute-done.9.refs_10_
  52.9 15.7 %collective-permute-done.17.refs_18_ = bf16[144,2048]{1,0:T(8,128)(2,1)S(1)} collective-permute-done((bf16[144,2048]{1,0:T(8,128)(2,1)S(1)}, bf16[144,2048]{1,0:T(8,128)(2,1)S(1)}, u32[]{:S(2)}, u32[]{:S(2)}) %collective-permute-start.17) | collective-permute-done | bytes 589856 | tf_op jit(solution)/shard_map/ppermute | solution.py:747
  78.8 9.0 %collective-permute-done.5.refs_6_ = bf16[144,2048]{1,0:T(8,128)(2,1)S(1)} collective-permute-done((bf16[144,2048]{1,0:T(8,128)(2,1)}, bf16[144,2048]{1,0:T(8,128)(2,1)S(1)}, u32[]{:S(2)}, u32[]{:S(2)}) %collective-permute-start.5) | collective-permute-done | bytes 589856 | tf_op jit(solution)/shard_map/ppermute | solution.py:747
  90.8 8.3 %collective-permute-done.25.refs_26_ = bf16[144,2048]{1,0:T(8,128)(2,1)} collective-permute-done((bf16[144,2048]{1,0:T(8,128)(2,1)}, bf16[144,2048]{1,0:T(8,128)(2,1)}, u32[]{:S(2)}, u32[]{:S(2)}) %collective-permute-start.25) | collective-permute-done | bytes 589856 | tf_op jit(solution)/shard_map/ppermute | solution.py:747
  106.0 6.5 collective-permute-done.21.refs_22_
  119.1 5.4 collective-permute-done.29.refs_30_
  127.0 18.7 %shard_map.265 = (bf16[4,1024,2048]{2,1,0:T(8,128)(2,1)}, f32[4,1024,128]{2,1,0:T(8,128)}, f32[4,1024,3]{2,1,0:T(8,128)}, f32[4,8,128]{2,1,0:T(8,128)}, bf16[2048,384]{1,0:T(8,128)(2,1)}) custom-call(bf16[144,2048]{1,0:T(8,128)(2,1)} %copy-done.23, bf16[144,2048]{1,0:T(8,128)(2,1)} %collective-permute-done.refs_1_, bf16[144,2048]{1,0:T(8,128)(2,1)} %copy-done.40, ...), custom_call_target="tpu_custom_call" | custom-call | flops 6442450944 | bytes 50331648 | tf_op jit(solution)/shard_map/pallas_call | solution.py:435
  152.4 12.3 %shard_map.266 = (f32[4,8,128,128]{3,2,1,0:T(8,128)}, f32[4,8,128,128]{3,2,1,0:T(8,128)}, f32[4,8,160,128]{3,2,1,0:T(8,128)}) custom-call(s32[8]{0:T(128)} %fusion.35.table, s32[4]{0:T(128)} %add_reduce_fusion.starts, f32[4,8,128,128]{3,2,1,0:T(8,128)} %bitcast.156, f32[4,8,128,3]{3,2,1,0:T(8,128)} %bitcast.146, f32[4,128]{1,0:T(4,128)} %convert_bitcast_fusion.2.taps, ...), custom_call_target="tpu_custom_call" | custom-call | tf_op jit(solution)/shard_map/pallas_call | solution.py:461
  196.0 5.7 collective-permute-done.37
  201.8 7.8 %collective-permute-start.39 = (bf16[1,1,1,1,192,128]{5,4,3,2,1,0:T(8,128)(2,1)S(1)}, bf16[1,1,1,1,192,128]{5,4,3,2,1,0:T(8,128)(2,1)S(1)}, u32[]{:S(2)}, u32[]{:S(2)}) collective-permute-start(bf16[1,1,1,1,192,128]{5,4,3,2,1,0:T(8,128)(2,1)S(1)} %maximum_bitcast_fusion), channel_id=1, source_target_pairs={{2,0},{3,1},{4,2},{5,3},{6,4},{7,5},{0,6},{1,7},{10,8},{11,9},{12,... | collective-permute-start | bytes 147464 | tf_op jit(solution)/shard_map/ppermute | solution.py:747
  224.0 8.0 %collective-permute-done.43 = bf16[2,1,4,1,96,128]{5,4,3,2,1,0:T(8,128)(2,1)S(1)} collective-permute-done((bf16[2,1,4,1,96,128]{5,4,3,2,1,0:T(8,128)(2,1)S(1)}, bf16[2,1,4,1,96,128]{5,4,3,2,1,0:T(8,128)(2,1)S(1)}, u32[]{:S(2)}, u32[]{:S(2)}) %collective-permute-start.43) | collective-permute-done | bytes 196640 | tf_op jit(solution)/shard_map/ppermute | solution.py:747
  248.3 37.9 %shard_map.267 = (f32[4,8,128,128]{3,2,1,0:T(8,128)}, f32[4,8,128,128]{3,2,1,0:T(8,128)}, f32[65536,128]{1,0:T(8,128)}, f32[64,128]{1,0:T(8,128)}) custom-call(s32[8]{0:T(128)} %fusion.35.table, s32[4]{0:T(128)} %add_reduce_fusion.starts, f32[4,8,128,128]{3,2,1,0:T(8,128)} %get-tuple-element.45.act, bf16[4,8,192,128]{3,2,1,0:T(8,128)(2,1)} %bitcast.166, ...), custom_call_target="tpu_custom_call" | custom-call | flops 10000000000 | bytes 100000000 | tf_op jit(solution)/shard_map/pallas_call | solution.py:545
  286.3 18.0 %all-to-all-done.1 = bf16[32,64,3,128]{3,1,2,0:T(8,128)(2,1)S(1)} async-done(((bf16[32,64,3,128]{3,1,2,0:T(8,128)(2,1)}), bf16[32,64,3,128]{3,1,2,0:T(8,128)(2,1)S(1)}, u32[]{:S(2)}, u32[]{:S(2)}) %all-to-all-start.1) | async-done | bytes 1572896 | tf_op jit(solution)/shard_map/all_to_all | solution.py:881
  309.4 15.3 %shard_map.268 = (f32[4,1024,128]{2,1,0:T(8,128)}, bf16[4,1024,128]{2,1,0:T(8,128)(2,1)}, bf16[4,1024,384]{2,1,0:T(8,128)(2,1)}) custom-call(s32[4]{0:T(128)} %fusion.33.lots_at, s32[8]{0:T(128)} %fusion.34.spans_at, bf16[4,1024,2048]{2,1,0:T(8,128)(2,1)} %get-tuple-element.40.normed, bf16[2048,384]{1,0:T(8,128)(2,1)} %get-tuple-element.95.weight, ...), custom_call_target="tpu_custom_call" | custom-call | flops 6442450944 | bytes 25165824 | tf_op jit(solution)/shard_map/pallas_call | solution.py:601
  324.8 14.4 %convolution_convert_fusion = bf16[4096,2048]{1,0:T(8,128)(2,1)} fusion(bf16[4096,384]{1,0:T(8,128)(2,1)} %bitcast.201, bf16[384,2048]{1,0:T(8,128)(2,1)S(1)} %bitcast.194), kind=kOutput, calls=%fused_computation | convolution fusion | flops 6450839552 | bytes 21495808 | tf_op jit(solution)/shard_map/dot_general | solution.py:21
  340.5 23.3 %shard_map.269 = (f32[4,1024,128]{2,1,0:T(8,128)}, bf16[4,1024,384]{2,1,0:T(8,128)(2,1)}, f32[384,2048]{1,0:T(8,128)}) custom-call(s32[4]{0:T(128)} %fusion.33.lots_at, s32[8]{0:T(128)} %fusion.34.spans_at, bf16[4,1024,2048]{2,1,0:T(8,128)(2,1)} %bitcast.189, bf16[384,2048]{1,0:T(8,128)(2,1)} %bitcast.193, f32[4,1024,3]{2,1,0:T(8,128)} %get-tuple-element.43.mask, ...), custom_call_target="tpu_custom_call" | custom-call | flops 12884901888 | bytes 25165824 | tf_op jit(solution)/shard_map/pallas_call | solution.py:712
  363.8 61.0 %shard_map.270 = (f32[4,8,128,128]{3,2,1,0:T(8,128)}, f32[4,8,160,128]{3,2,1,0:T(8,128)}, f32[128,128]{1,0:T(8,128)}, f32[64,128]{1,0:T(8,128)}, f32[128,384]{1,...) custom-call(s32[8]{0:T(128)} %fusion.35.table, s32[4]{0:T(128)} %add_reduce_fusion.starts, ...), custom_call_target="tpu_custom_call" | custom-call | flops 10000000000 | bytes 200000000 | tf_op jit(solution)/shard_map/pallas_call | solution.py:650
  431.0 8.7 %collective-permute-done.50 = bf16[2,1,4,1,80,128]{5,4,3,2,1,0:T(8,128)(2,1)S(1)} collective-permute-done((bf16[2,1,4,1,80,128]{5,4,3,2,1,0:T(8,128)(2,1)S(1)}, bf16[2,1,4,1,80,128]{5,4,3,2,1,0:T(8,128)(2,1)S(1)}, u32[]{:S(2)}, u32[]{:S(2)}) %collective-permute-start.50) | collective-permute-done | bytes 163872 | tf_op jit(solution)/shard_map/ppermute | solution.py:747
  440.9 7.9 %collective-permute-done.51 = f32[1,1,4,1,80,128]{5,4,3,2,1,0:T(8,128)S(1)} collective-permute-done((f32[1,1,4,1,80,128]{5,4,3,2,1,0:T(8,128)S(1)}, f32[1,1,4,1,80,128]{5,4,3,2,1,0:T(8,128)S(1)}, u32[]{:S(2)}, u32[]{:S(2)}) %collective-permute-start.51) | collective-permute-done | bytes 163872 | tf_op jit(solution)/shard_map/ppermute | solution.py:747
  453.4 5.2 collective-permute-done.52
  468.8 5.2 collective-permute-done.56
  492.6 17.1 %shard_map.271 = (bf16[4,8,128,384]{3,2,1,0:T(8,128)(2,1)}, f32[8,128]{1,0:T(8,128)}, f32[1,128]{1,0:T(1,128)}, f32[128,480]{1,0:T(8,128)}) custom-call(s32[8]{0:T(128)} %fusion.35.table, s32[4]{0:T(128)} %add_reduce_fusion.starts, f32[4,8,128,128]{3,2,1,0:T(8,128)} %get-tuple-element.54.grad, bf16[4,8,160,128]{3,2,1,0:T(8,128)(2,1)} %bitcast.168, ...), custom_call_target="tpu_custom_call" | custom-call | tf_op jit(solution)/shard_map/pallas_call | solution.py:495
  509.8 9.9 %convolution_convert_fusion.2 = bf16[4096,1024]{1,0:T(8,128)(2,1)S(1)} fusion(bf16[4096,384]{1,0:T(8,128)(2,1)} %bitcast.199, bf16[4096,384]{1,0:T(8,128)(2,1)} %bitcast.190, bf16[2048,768]{1,0:T(8,128)(2,1)S(1)} %copy-done.22), kind=kOutput, calls=%fused_computation.4 | convolution fusion | flops 6459228160 | bytes 16252928 | tf_op jit(solution)/shard_map/dot_general | solution.py:21
  527.0 7.2 convolution_convert_fusion.1
  540.8 12.5 %fusion = bf16[2048,384]{1,0:T(8,128)(2,1)S(1)} fusion(bf16[4,1024,2048]{2,1,0:T(8,128)(2,1)} %get-tuple-element.40.normed, bf16[4,1024,384]{2,1,0:T(8,128)(2,1)S(1)} %copy-done.60, bf16[]{:T(256)} %bitcast.54), kind=kOutput, calls=%fused_computation.12 | convolution fusion | flops 6444023808 | bytes 21495810 | tf_op jit(solution)/shard_map/dot_general | solution.py:21
  558.1 14.2 %convolution_convert_fusion.3 = bf16[2048,384]{1,0:T(8,128)(2,1)} fusion(bf16[4096,2048]{1,0:T(8,128)(2,1)} %bitcast.197, bf16[4096,384]{1,0:T(8,128)(2,1)} %bitcast.191), kind=kOutput, calls=%fused_computation.11 | convolution fusion | flops 6443237376 | bytes 21495808 | tf_op jit(solution)/shard_map/dot_general | solution.py:21
  575.0 5.6 add_convert_fusion.1
  585.2 5.6 add_convert_fusion
  600.8 47.5 %collective-permute-done.64 = bf16[1,2,4,1,128,1024]{5,4,3,2,1,0:T(8,128)(2,1)} collective-permute-done((bf16[1,2,4,1,128,1024]{5,4,3,2,1,0:T(8,128)(2,1)}, bf16[1,2,4,1,128,1024]{5,4,3,2,1,0:T(8,128)(2,1)}, u32[]{:S(2)}, u32[]{:S(2)}) %collective-permute-start.64) | collective-permute-done | bytes 2097184 | tf_op jit(solution)/shard_map/ppermute | solution.py:747
  700.4 5.8 collective-permute-done.67
  706.4 5.5 collective-permute-done.73
  (399 shorter events, 276.2 us)
Async XLA Ops:
  9.8 17.7 %collective-permute-start.1 = (bf16[144,2048]{1,0:T(8,128)(2,1)S(1)}, bf16[144,2048]{1,0:T(8,128)(2,1)S(1)}, u32[]{:S(2)}, u32[]{:S(2)}) collective-permute-start(bf16[144,2048]{1,0:T(8,128)(2,1)S(1)} %fusion.11.refs_0_), channel_id=1, source_target_pairs={{2,0},{3,1},{4,2},{5,3},{6,4},{7,5},{0,6},{1,7},{10,8},{11,9},{12,... | collective-permute-start | bytes 1769480 | tf_op jit(solution)/shard_map/ppermute | solution.py:747
  14.9 22.5 %collective-permute-start.15 = (bf16[144,2048]{1,0:T(8,128)(2,1)S(1)}, bf16[144,2048]{1,0:T(8,128)(2,1)}, u32[]{:S(2)}, u32[]{:S(2)}) collective-permute-start(bf16[144,2048]{1,0:T(8,128)(2,1)S(1)} %fusion.11.refs_0_), channel_id=1, source_target_pairs={{16,0},{24,8},{0,16},{8,24},{17,1},{25,9},{1,17},{9,25},{18,2},{26... | collective-permute-start | bytes 1769480 | tf_op jit(solution)/shard_map/ppermute | solution.py:747
  16.4 22.7 %collective-permute-start.7 = (bf16[144,2048]{1,0:T(8,128)(2,1)S(1)}, bf16[144,2048]{1,0:T(8,128)(2,1)}, u32[]{:S(2)}, u32[]{:S(2)}) collective-permute-start(bf16[144,2048]{1,0:T(8,128)(2,1)S(1)} %fusion.11.refs_0_), channel_id=1, source_target_pairs={{8,0},{0,8},{24,16},{16,24},{9,1},{1,9},{25,17},{17,25},{10,2},{2,... | collective-permute-start | bytes 1769480 | tf_op jit(solution)/shard_map/ppermute | solution.py:747
  17.9 21.2 %collective-permute-start = (bf16[144,2048]{1,0:T(8,128)(2,1)S(1)}, bf16[144,2048]{1,0:T(8,128)(2,1)}, u32[]{:S(2)}, u32[]{:S(2)}) collective-permute-start(bf16[144,2048]{1,0:T(8,128)(2,1)S(1)} %fusion.11.refs_0_), channel_id=1, source_target_pairs={{1,0},{0,1},{3,2},{2,3},{5,4},{4,5},{7,6},{6,7},{9,8},{8,9},{11,10... | collective-permute-start | bytes 1769480 | tf_op jit(solution)/shard_map/ppermute | solution.py:747
  27.5 18.1 %collective-permute-start.3 = (bf16[144,2048]{1,0:T(8,128)(2,1)S(1)}, bf16[144,2048]{1,0:T(8,128)(2,1)}, u32[]{:S(2)}, u32[]{:S(2)}) collective-permute-start(bf16[144,2048]{1,0:T(8,128)(2,1)S(1)} %collective-permute-done.1.refs_2_), channel_id=1, source_target_pairs={{2,0},{3,1},{4,2},{5,3},{6,4},{7,5},{0,6},{1,7},{10,8},{11,9},{12,... | collective-permute-start | bytes 1769480 | tf_op jit(solution)/shard_map/ppermute | solution.py:747
  31.8 21.1 %collective-permute-start.9 = (bf16[144,2048]{1,0:T(8,128)(2,1)S(1)}, bf16[144,2048]{1,0:T(8,128)(2,1)}, u32[]{:S(2)}, u32[]{:S(2)}) collective-permute-start(bf16[144,2048]{1,0:T(8,128)(2,1)S(1)} %collective-permute-done.1.refs_2_), channel_id=1, source_target_pairs={{8,0},{0,8},{24,16},{16,24},{9,1},{1,9},{25,17},{17,25},{10,2},{2,... | collective-permute-start | bytes 1769480 | tf_op jit(solution)/shard_map/ppermute | solution.py:747
  34.6 90.0 %all-to-all-start = ((bf16[32,205,128]{2,1,0:T(8,128)(2,1)}), bf16[32,205,128]{2,1,0:T(8,128)(2,1)S(1)}, u32[]{:S(2)}, u32[]{:S(2)}) async-start(bf16[32,205,128]{2,1,0:T(8,128)(2,1)} %pad_maximum_fusion.3), calls=%async_computation | async-start | bytes 3407872 | tf_op jit(solution)/shard_map/all_to_all | solution.py:881
  37.3 303.2 %all-gather.3.cloned.1.call-start = ((), (), s32[]{:S(2)}) async-start(), calls=%async_computation.6 | async-start | bytes 17301504 | tf_op jit(solution)/shard_map/all_gather | solution.py:974
  37.4 31.2 %collective-permute-start.17 = (bf16[144,2048]{1,0:T(8,128)(2,1)S(1)}, bf16[144,2048]{1,0:T(8,128)(2,1)S(1)}, u32[]{:S(2)}, u32[]{:S(2)}) collective-permute-start(bf16[144,2048]{1,0:T(8,128)(2,1)S(1)} %collective-permute-done.1.refs_2_), channel_id=1, source_target_pairs={{16,0},{24,8},{0,16},{8,24},{17,1},{25,9},{1,17},{9,25},{18,2},{26... | collective-permute-start | bytes 1769480 | tf_op jit(solution)/shard_map/ppermute | solution.py:747
  39.1 31.3 %collective-permute-start.2 = (bf16[144,2048]{1,0:T(8,128)(2,1)S(1)}, bf16[144,2048]{1,0:T(8,128)(2,1)S(1)}, u32[]{:S(2)}, u32[]{:S(2)}) collective-permute-start(bf16[144,2048]{1,0:T(8,128)(2,1)S(1)} %collective-permute-done.1.refs_2_), channel_id=1, source_target_pairs={{1,0},{0,1},{3,2},{2,3},{5,4},{4,5},{7,6},{6,7},{9,8},{8,9},{11,10... | collective-permute-start | bytes 1769480 | tf_op jit(solution)/shard_map/ppermute | solution.py:747
  39.1 35.8 %collective-permute-start.23 = (bf16[144,2048]{1,0:T(8,128)(2,1)}, bf16[144,2048]{1,0:T(8,128)(2,1)S(1)}, u32[]{:S(2)}, u32[]{:S(2)}) collective-permute-start(bf16[144,2048]{1,0:T(8,128)(2,1)} %collective-permute-done.15.refs_16_), channel_id=1, source_target_pairs={{8,0},{0,8},{24,16},{16,24},{9,1},{1,9},{25,17},{17,25},{10,2},{2,... | collective-permute-start | bytes 1769480 | tf_op jit(solution)/shard_map/ppermute | solution.py:747
  45.7 31.3 %collective-permute-start.16 = (bf16[144,2048]{1,0:T(8,128)(2,1)}, bf16[144,2048]{1,0:T(8,128)(2,1)S(1)}, u32[]{:S(2)}, u32[]{:S(2)}) collective-permute-start(bf16[144,2048]{1,0:T(8,128)(2,1)} %collective-permute-done.15.refs_16_), channel_id=1, source_target_pairs={{1,0},{0,1},{3,2},{2,3},{5,4},{4,5},{7,6},{6,7},{9,8},{8,9},{11,10... | collective-permute-start | bytes 1769480 | tf_op jit(solution)/shard_map/ppermute | solution.py:747
  52.9 24.1 %collective-permute-start.8 = (bf16[144,2048]{1,0:T(8,128)(2,1)}, bf16[144,2048]{1,0:T(8,128)(2,1)S(1)}, u32[]{:S(2)}, u32[]{:S(2)}) collective-permute-start(bf16[144,2048]{1,0:T(8,128)(2,1)} %collective-permute-done.7.refs_8_), channel_id=1, source_target_pairs={{1,0},{0,1},{3,2},{2,3},{5,4},{4,5},{7,6},{6,7},{9,8},{8,9},{11,10... | collective-permute-start | bytes 1769480 | tf_op jit(solution)/shard_map/ppermute | solution.py:747
  68.6 19.2 %collective-permute-start.5 = (bf16[144,2048]{1,0:T(8,128)(2,1)}, bf16[144,2048]{1,0:T(8,128)(2,1)S(1)}, u32[]{:S(2)}, u32[]{:S(2)}) collective-permute-start(bf16[144,2048]{1,0:T(8,128)(2,1)} %collective-permute-done.3.refs_4_), channel_id=1, source_target_pairs={{2,0},{3,1},{4,2},{5,3},{6,4},{7,5},{0,6},{1,7},{10,8},{11,9},{12,... | collective-permute-start | bytes 1769480 | tf_op jit(solution)/shard_map/ppermute | solution.py:747
  70.5 18.8 %collective-permute-start.19 = (bf16[144,2048]{1,0:T(8,128)(2,1)}, bf16[144,2048]{1,0:T(8,128)(2,1)S(1)}, u32[]{:S(2)}, u32[]{:S(2)}) collective-permute-start(bf16[144,2048]{1,0:T(8,128)(2,1)} %collective-permute-done.3.refs_4_), channel_id=1, source_target_pairs={{16,0},{24,8},{0,16},{8,24},{17,1},{25,9},{1,17},{9,25},{18,2},{26... | collective-permute-start | bytes 1769480 | tf_op jit(solution)/shard_map/ppermute | solution.py:747
  74.9 14.7 %collective-permute-start.11 = (bf16[144,2048]{1,0:T(8,128)(2,1)}, bf16[144,2048]{1,0:T(8,128)(2,1)S(1)}, u32[]{:S(2)}, u32[]{:S(2)}) collective-permute-start(bf16[144,2048]{1,0:T(8,128)(2,1)} %collective-permute-done.3.refs_4_), channel_id=1, source_target_pairs={{8,0},{0,8},{24,16},{16,24},{9,1},{1,9},{25,17},{17,25},{10,2},{2,... | collective-permute-start | bytes 1769480 | tf_op jit(solution)/shard_map/ppermute | solution.py:747
  77.0 22.2 %collective-permute-start.25 = (bf16[144,2048]{1,0:T(8,128)(2,1)}, bf16[144,2048]{1,0:T(8,128)(2,1)}, u32[]{:S(2)}, u32[]{:S(2)}) collective-permute-start(bf16[144,2048]{1,0:T(8,128)(2,1)} %collective-permute-done.9.refs_10_), channel_id=1, source_target_pairs={{16,0},{24,8},{0,16},{8,24},{17,1},{25,9},{1,17},{9,25},{18,2},{26... | collective-permute-start | bytes 1769480 | tf_op jit(solution)/shard_map/ppermute | solution.py:747
  89.7 16.3 %collective-permute-start.13 = (bf16[144,2048]{1,0:T(8,128)(2,1)S(1)}, bf16[144,2048]{1,0:T(8,128)(2,1)}, u32[]{:S(2)}, u32[]{:S(2)}) collective-permute-start(bf16[144,2048]{1,0:T(8,128)(2,1)S(1)} %collective-permute-done.5.refs_6_), channel_id=1, source_target_pairs={{8,0},{0,8},{24,16},{16,24},{9,1},{1,9},{25,17},{17,25},{10,2},{2,... | collective-permute-start | bytes 1769480 | tf_op jit(solution)/shard_map/ppermute | solution.py:747
  99.7 18.4 %collective-permute-start.27 = (bf16[144,2048]{1,0:T(8,128)(2,1)S(1)}, bf16[144,2048]{1,0:T(8,128)(2,1)}, u32[]{:S(2)}, u32[]{:S(2)}) collective-permute-start(bf16[144,2048]{1,0:T(8,128)(2,1)S(1)} %collective-permute-done.19.refs_20_), channel_id=1, source_target_pairs={{8,0},{0,8},{24,16},{16,24},{9,1},{1,9},{25,17},{17,25},{10,2},{2,... | collective-permute-start | bytes 1769480 | tf_op jit(solution)/shard_map/ppermute | solution.py:747
  100.9 17.1 %collective-permute-start.6 = (bf16[144,2048]{1,0:T(8,128)(2,1)S(1)}, bf16[144,2048]{1,0:T(8,128)(2,1)S(1)}, u32[]{:S(2)}, u32[]{:S(2)}) collective-permute-start(bf16[144,2048]{1,0:T(8,128)(2,1)S(1)} %collective-permute-done.5.refs_6_), channel_id=1, source_target_pairs={{1,0},{0,1},{3,2},{2,3},{5,4},{4,5},{7,6},{6,7},{9,8},{8,9},{11,10... | collective-permute-start | bytes 1769480 | tf_op jit(solution)/shard_map/ppermute | solution.py:747
  100.9 17.6 %collective-permute-start.20 = (bf16[144,2048]{1,0:T(8,128)(2,1)S(1)}, bf16[144,2048]{1,0:T(8,128)(2,1)S(1)}, u32[]{:S(2)}, u32[]{:S(2)}) collective-permute-start(bf16[144,2048]{1,0:T(8,128)(2,1)S(1)} %collective-permute-done.19.refs_20_), channel_id=1, source_target_pairs={{1,0},{0,1},{3,2},{2,3},{5,4},{4,5},{7,6},{6,7},{9,8},{8,9},{11,10... | collective-permute-start | bytes 1769480 | tf_op jit(solution)/shard_map/ppermute | solution.py:747
  240.6 63.6 %all-to-all-start.1 = ((bf16[32,64,3,128]{3,1,2,0:T(8,128)(2,1)}), bf16[32,64,3,128]{3,1,2,0:T(8,128)(2,1)S(1)}, u32[]{:S(2)}, u32[]{:S(2)}) async-start(bf16[32,64,3,128]{3,1,2,0:T(8,128)(2,1)} %copy.88), calls=%async_computation.1 | async-start | bytes 3145728 | tf_op jit(solution)/shard_map/all_to_all | solution.py:881
  243.5 479.9 %reduce-scatter.2.cloned.1.call-start = ((), (), s32[]{:S(2)}) async-start(), calls=%async_computation.5 | async-start | bytes 17301504 | tf_op jit(solution)/shard_map/reduce_scatter | solution.py:1007
  526.0 49.0 %collective-permute-start.63 = (bf16[2,2,4,1,128,1024]{5,4,3,2,1,0:T(8,128)(2,1)}, bf16[2,2,4,1,128,1024]{5,4,3,2,1,0:T(8,128)(2,1)}, u32[]{:S(2)}, u32[]{:S(2)}) collective-permute-start(bf16[2,2,4,1,128,1024]{5,4,3,2,1,0:T(8,128)(2,1)} %slice.323), channel_id=1, source_target_pairs={{1,0},{0,1},{3,2},{2,3},{5,4},{4,5},{7,6},{6,7},{9,8},{8,9},{11,10... | collective-permute-start | bytes 12582920 | tf_op jit(solution)/shard_map/ppermute | solution.py:747
  538.8 46.3 %collective-permute-start.69 = (bf16[2,2,4,1,128,1024]{5,4,3,2,1,0:T(8,128)(2,1)}, bf16[2,2,4,1,128,1024]{5,4,3,2,1,0:T(8,128)(2,1)}, u32[]{:S(2)}, u32[]{:S(2)}) collective-permute-start(bf16[2,2,4,1,128,1024]{5,4,3,2,1,0:T(8,128)(2,1)} %slice.334), channel_id=1, source_target_pairs={{1,0},{0,1},{3,2},{2,3},{5,4},{4,5},{7,6},{6,7},{9,8},{8,9},{11,10... | collective-permute-start | bytes 12582920 | tf_op jit(solution)/shard_map/ppermute | solution.py:747
  555.0 42.0 %all-to-all-start.3 = ((bf16[32,192,128]{2,1,0:T(8,128)(2,1)}), bf16[32,192,128]{2,1,0:T(8,128)(2,1)S(1)}, u32[]{:S(2)}, u32[]{:S(2)}) async-start(bf16[32,192,128]{2,1,0:T(8,128)(2,1)} %add.315), calls=%async_computation.4 | async-start | bytes 3145728 | tf_op jit(solution)/shard_map/all_to_all | solution.py:881
  583.4 65.0 %collective-permute-start.64 = (bf16[1,2,4,1,128,1024]{5,4,3,2,1,0:T(8,128)(2,1)}, bf16[1,2,4,1,128,1024]{5,4,3,2,1,0:T(8,128)(2,1)}, u32[]{:S(2)}, u32[]{:S(2)}) collective-permute-start(bf16[1,2,4,1,128,1024]{5,4,3,2,1,0:T(8,128)(2,1)} %slice.325), channel_id=1, source_target_pairs={{16,0},{24,8},{0,16},{8,24},{17,1},{25,9},{1,17},{9,25},{18,2},{26... | collective-permute-start | bytes 6291464 | tf_op jit(solution)/shard_map/ppermute | solution.py:747
  593.4 62.5 %collective-permute-start.70 = (bf16[2,1,4,1,128,1024]{5,4,3,2,1,0:T(8,128)(2,1)}, bf16[2,1,4,1,128,1024]{5,4,3,2,1,0:T(8,128)(2,1)}, u32[]{:S(2)}, u32[]{:S(2)}) collective-permute-start(bf16[2,1,4,1,128,1024]{5,4,3,2,1,0:T(8,128)(2,1)} %slice.336), channel_id=1, source_target_pairs={{8,0},{0,8},{24,16},{16,24},{9,1},{1,9},{25,17},{17,25},{10,2},{2,... | collective-permute-start | bytes 6291464 | tf_op jit(solution)/shard_map/ppermute | solution.py:747
  597.0 75.0 %all-to-all-start.2 = ((bf16[32,204,128]{2,1,0:T(8,128)(2,1)}), bf16[32,204,128]{2,1,0:T(8,128)(2,1)}, u32[]{:S(2)}, u32[]{:S(2)}) async-start(bf16[32,204,128]{2,1,0:T(8,128)(2,1)} %pad_maximum_fusion.4), calls=%async_computation.3 | async-start | bytes 3407872 | tf_op jit(solution)/shard_map/all_to_all | solution.py:881
  652.8 29.4 %collective-permute-start.65 = (bf16[1,1,4,1,128,1024]{5,4,3,2,1,0:T(8,128)(2,1)}, bf16[1,1,4,1,128,1024]{5,4,3,2,1,0:T(8,128)(2,1)}, u32[]{:S(2)}, u32[]{:S(2)}) collective-permute-start(bf16[1,1,4,1,128,1024]{5,4,3,2,1,0:T(8,128)(2,1)} %slice.327), channel_id=1, source_target_pairs={{8,0},{0,8},{24,16},{16,24},{9,1},{1,9},{25,17},{17,25},{10,2},{2,... | collective-permute-start | bytes 3145736 | tf_op jit(solution)/shard_map/ppermute | solution.py:747
  660.9 24.3 %collective-permute-start.71 = (bf16[1,1,4,1,128,1024]{5,4,3,2,1,0:T(8,128)(2,1)}, bf16[1,1,4,1,128,1024]{5,4,3,2,1,0:T(8,128)(2,1)}, u32[]{:S(2)}, u32[]{:S(2)}) collective-permute-start(bf16[1,1,4,1,128,1024]{5,4,3,2,1,0:T(8,128)(2,1)} %slice.338), channel_id=1, source_target_pairs={{16,0},{24,8},{0,16},{8,24},{17,1},{25,9},{1,17},{9,25},{18,2},{26... | collective-permute-start | bytes 3145736 | tf_op jit(solution)/shard_map/ppermute | solution.py:747
  686.9 13.4 %collective-permute-start.72 = (bf16[1,1,1,1,128,1024]{5,4,3,2,1,0:T(8,128)(2,1)S(1)}, bf16[1,1,1,1,128,1024]{5,4,3,2,1,0:T(8,128)(2,1)S(1)}, u32[]{:S(2)}, u32[]{:S(2)}) collective-permute-start(bf16[1,1,1,1,128,1024]{5,4,3,2,1,0:T(8,128)(2,1)S(1)} %slice.342), channel_id=1, source_target_pairs={{6,0},{7,1},{0,2},{1,3},{2,4},{3,5},{4,6},{5,7},{14,8},{15,9},{8,1... | collective-permute-start | bytes 786440 | tf_op jit(solution)/shard_map/ppermute | solution.py:747
  (112 other events, 1266.7 us)
Sparse Core Ops, SparseCore 0:
  148.5 153.5 all-gather.2
  339.3 191.8 reduce-scatter.1

commit v6 on v5

--- a/solution.py
+++ b/solution.py
@@ -1032,7 +1032,8 @@
     grad_decay = jnp.moveaxis(rate_grad, 0, 1).reshape(states, lanes).T * rate
     picked_grad = reduce_small(dims, picked_grad.reshape(sizes + (-1, 128))).astype(BF)
     picked_grad = gather_small(dims, picked_grad).reshape(groups, blocks, -1, 128)
-    grad_gate_cols = exchange(after(gate_sent, picked_grad))
+    gate_sent, picked_grad = fence(gate_sent, picked_grad)
+    grad_gate_cols = exchange(gate_sent)
     x_grad, tap_grad, base_grad, grad_xproj = conv_back(
         table, begins, act_grad, picked_grad, pre_act, act, conv_in.reshape(grouped), masks, taps,
         xproj, [],

time: 745 us -> 740 us (level)
    unnamed x128 -> x130, local copies, waits for them, and re-layouts: 15.9 us -> 15.5 us
  transfers between devices with their start and end apart: 81 -> 81, of which waited for: 53 -> 51; matrix products, arithmetic and copies ran while one was open for 20% -> 20% of each run, Pallas kernels for 23% -> 23%
where the time goes in v6:
time: 740 us; the launch traced here: 731 us
  waiting for transfers between devices  267 us (36%)
  Pallas kernels  186 us (25%)
  starting transfers between devices  91.8 us (12%)
  local copies, waits for them, and re-layouts  63 us (9%)
  matrix products  58.5 us (8%)
  other arithmetic  48.1 us (6%)
  between operations  17.8 us (2%)
    ppermute x75, waiting for transfers between devices, fetch(): return lax.ppermute(x, self.axis, pairs)  248 us
    ppermute x75, starting transfers between devices, fetch(): return lax.ppermute(x, self.axis, pairs)  79.6 us
    pallas_call x1, Pallas kernels, scan_back(): pl.pallas_call(functools.partial(back_kernel, groups, length, states, las...  61.1 us
    dot_general x5, matrix products, dot(): return lax.dot_general(a, b, (dims, ((), ())), preferred_element_type=F32)  58.5 us
    pallas_call x1, Pallas kernels, scan(): pl.pallas_call(functools.partial(scan_kernel, groups, length, states), gr...  37.9 us
    pallas_call x1, Pallas kernels, cot_part(): pl.pallas_call(cot_kernel, grid_spec=pltpu.PrefetchScalarGridSpec(num_sca...  23.3 us
    convert_element_type x6, other arithmetic, reduce_parts(): x = x.astype(BF)  20.6 us
    all_to_all x4, waiting for transfers between devices, exchange(): return lax.all_to_all(x, chan, 0, 0, tiled=True)  18.7 us
  transfers between devices with their start and end apart: 81, of which 51 were waited for; matrix products, arithmetic and copies ran while one was open for 20% of the time, Pallas kernels for 23%

profile of v6, /device:TPU:0, one launch (start us, length us, event | category | flops | bytes accessed | tf_op | source)
XLA Modules:
  0.0 731.3 jit_solution(13781031523655092132)
XLA Ops:
  19.4 8.1 %collective-permute-done.1.refs_2_ = bf16[144,2048]{1,0:T(8,128)(2,1)S(1)} collective-permute-done((bf16[144,2048]{1,0:T(8,128)(2,1)S(1)}, bf16[144,2048]{1,0:T(8,128)(2,1)S(1)}, u32[]{:S(2)}, u32[]{:S(2)}) %collective-permute-start.1) | collective-permute-done | bytes 589856 | tf_op jit(solution)/shard_map/ppermute | solution.py:747
  45.7 7.2 collective-permute-done.9.refs_10_
  52.9 15.7 %collective-permute-done.17.refs_18_ = bf16[144,2048]{1,0:T(8,128)(2,1)S(1)} collective-permute-done((bf16[144,2048]{1,0:T(8,128)(2,1)S(1)}, bf16[144,2048]{1,0:T(8,128)(2,1)S(1)}, u32[]{:S(2)}, u32[]{:S(2)}) %collective-permute-start.17) | collective-permute-done | bytes 589856 | tf_op jit(solution)/shard_map/ppermute | solution.py:747
  78.8 9.0 %collective-permute-done.5.refs_6_ = bf16[144,2048]{1,0:T(8,128)(2,1)S(1)} collective-permute-done((bf16[144,2048]{1,0:T(8,128)(2,1)}, bf16[144,2048]{1,0:T(8,128)(2,1)S(1)}, u32[]{:S(2)}, u32[]{:S(2)}) %collective-permute-start.5) | collective-permute-done | bytes 589856 | tf_op jit(solution)/shard_map/ppermute | solution.py:747
  90.8 8.3 %collective-permute-done.25.refs_26_ = bf16[144,2048]{1,0:T(8,128)(2,1)} collective-permute-done((bf16[144,2048]{1,0:T(8,128)(2,1)}, bf16[144,2048]{1,0:T(8,128)(2,1)}, u32[]{:S(2)}, u32[]{:S(2)}) %collective-permute-start.25) | collective-permute-done | bytes 589856 | tf_op jit(solution)/shard_map/ppermute | solution.py:747
  106.0 6.5 collective-permute-done.21.refs_22_
  119.1 5.4 collective-permute-done.29.refs_30_
  127.0 18.7 %shard_map.265 = (bf16[4,1024,2048]{2,1,0:T(8,128)(2,1)}, f32[4,1024,128]{2,1,0:T(8,128)}, f32[4,1024,3]{2,1,0:T(8,128)}, f32[4,8,128]{2,1,0:T(8,128)}, bf16[2048,384]{1,0:T(8,128)(2,1)}) custom-call(bf16[144,2048]{1,0:T(8,128)(2,1)} %copy-done.23, bf16[144,2048]{1,0:T(8,128)(2,1)} %collective-permute-done.refs_1_, bf16[144,2048]{1,0:T(8,128)(2,1)} %copy-done.40, ...), custom_call_target="tpu_custom_call" | custom-call | flops 6442450944 | bytes 50331648 | tf_op jit(solution)/shard_map/pallas_call | solution.py:435
  152.3 12.3 %shard_map.266 = (f32[4,8,128,128]{3,2,1,0:T(8,128)}, f32[4,8,128,128]{3,2,1,0:T(8,128)}, f32[4,8,160,128]{3,2,1,0:T(8,128)}) custom-call(s32[8]{0:T(128)} %fusion.34.table, s32[4]{0:T(128)} %add_reduce_fusion.starts, f32[4,8,128,128]{3,2,1,0:T(8,128)} %bitcast.154, f32[4,8,128,3]{3,2,1,0:T(8,128)} %bitcast.143, f32[4,128]{1,0:T(4,128)} %convert_bitcast_fusion.2.taps, ...), custom_call_target="tpu_custom_call" | custom-call | tf_op jit(solution)/shard_map/pallas_call | solution.py:461
  195.9 5.7 collective-permute-done.37
  201.7 7.7 %collective-permute-start.39 = (bf16[1,1,1,1,192,128]{5,4,3,2,1,0:T(8,128)(2,1)S(1)}, bf16[1,1,1,1,192,128]{5,4,3,2,1,0:T(8,128)(2,1)S(1)}, u32[]{:S(2)}, u32[]{:S(2)}) collective-permute-start(bf16[1,1,1,1,192,128]{5,4,3,2,1,0:T(8,128)(2,1)S(1)} %maximum_bitcast_fusion), channel_id=1, source_target_pairs={{2,0},{3,1},{4,2},{5,3},{6,4},{7,5},{0,6},{1,7},{10,8},{11,9},{12,... | collective-permute-start | bytes 147464 | tf_op jit(solution)/shard_map/ppermute | solution.py:747
  224.1 7.7 %collective-permute-done.43 = bf16[2,1,4,1,96,128]{5,4,3,2,1,0:T(8,128)(2,1)S(1)} collective-permute-done((bf16[2,1,4,1,96,128]{5,4,3,2,1,0:T(8,128)(2,1)S(1)}, bf16[2,1,4,1,96,128]{5,4,3,2,1,0:T(8,128)(2,1)S(1)}, u32[]{:S(2)}, u32[]{:S(2)}) %collective-permute-start.43) | collective-permute-done | bytes 196640 | tf_op jit(solution)/shard_map/ppermute | solution.py:747
  248.4 37.9 %shard_map.267 = (f32[4,8,128,128]{3,2,1,0:T(8,128)}, f32[4,8,128,128]{3,2,1,0:T(8,128)}, f32[65536,128]{1,0:T(8,128)}, f32[64,128]{1,0:T(8,128)}) custom-call(s32[8]{0:T(128)} %fusion.34.table, s32[4]{0:T(128)} %add_reduce_fusion.starts, f32[4,8,128,128]{3,2,1,0:T(8,128)} %get-tuple-element.47.act, bf16[4,8,192,128]{3,2,1,0:T(8,128)(2,1)} %bitcast.164, ...), custom_call_target="tpu_custom_call" | custom-call | flops 10000000000 | bytes 100000000 | tf_op jit(solution)/shard_map/pallas_call | solution.py:545
  286.3 18.0 %all-to-all-done.1 = bf16[32,64,3,128]{3,1,2,0:T(8,128)(2,1)S(1)} async-done(((bf16[32,64,3,128]{3,1,2,0:T(8,128)(2,1)}), bf16[32,64,3,128]{3,1,2,0:T(8,128)(2,1)S(1)}, u32[]{:S(2)}, u32[]{:S(2)}) %all-to-all-start.1) | async-done | bytes 1572896 | tf_op jit(solution)/shard_map/all_to_all | solution.py:881
  309.4 15.3 %shard_map.268 = (f32[4,1024,128]{2,1,0:T(8,128)}, bf16[4,1024,128]{2,1,0:T(8,128)(2,1)}, bf16[4,1024,384]{2,1,0:T(8,128)(2,1)}) custom-call(s32[4]{0:T(128)} %fusion.32.lots_at, s32[8]{0:T(128)} %fusion.33.spans_at, bf16[4,1024,2048]{2,1,0:T(8,128)(2,1)} %get-tuple-element.42.normed, bf16[2048,384]{1,0:T(8,128)(2,1)} %get-tuple-element.99.weight, ...), custom_call_target="tpu_custom_call" | custom-call | flops 6442450944 | bytes 25165824 | tf_op jit(solution)/shard_map/pallas_call | solution.py:601
  324.7 14.4 %convolution_convert_fusion = bf16[4096,2048]{1,0:T(8,128)(2,1)} fusion(bf16[4096,384]{1,0:T(8,128)(2,1)} %bitcast.197, bf16[384,2048]{1,0:T(8,128)(2,1)S(1)} %bitcast.190), kind=kOutput, calls=%fused_computation | convolution fusion | flops 6450839552 | bytes 21495808 | tf_op jit(solution)/shard_map/dot_general | solution.py:21
  340.5 23.3 %shard_map.269 = (f32[4,1024,128]{2,1,0:T(8,128)}, bf16[4,1024,384]{2,1,0:T(8,128)(2,1)}, f32[384,2048]{1,0:T(8,128)}) custom-call(s32[4]{0:T(128)} %fusion.32.lots_at, s32[8]{0:T(128)} %fusion.33.spans_at, bf16[4,1024,2048]{2,1,0:T(8,128)(2,1)} %bitcast.185, bf16[384,2048]{1,0:T(8,128)(2,1)} %bitcast.189, f32[4,1024,3]{2,1,0:T(8,128)} %get-tuple-element.45.mask, ...), custom_call_target="tpu_custom_call" | custom-call | flops 12884901888 | bytes 25165824 | tf_op jit(solution)/shard_map/pallas_call | solution.py:712
  363.7 61.1 %shard_map.270 = (f32[4,8,128,128]{3,2,1,0:T(8,128)}, f32[4,8,160,128]{3,2,1,0:T(8,128)}, f32[128,128]{1,0:T(8,128)}, f32[64,128]{1,0:T(8,128)}, f32[128,384]{1,...) custom-call(s32[8]{0:T(128)} %fusion.34.table, s32[4]{0:T(128)} %add_reduce_fusion.starts, ...), custom_call_target="tpu_custom_call" | custom-call | flops 10000000000 | bytes 200000000 | tf_op jit(solution)/shard_map/pallas_call | solution.py:650
  431.0 8.6 %collective-permute-done.50 = bf16[2,1,4,1,80,128]{5,4,3,2,1,0:T(8,128)(2,1)S(1)} collective-permute-done((bf16[2,1,4,1,80,128]{5,4,3,2,1,0:T(8,128)(2,1)S(1)}, bf16[2,1,4,1,80,128]{5,4,3,2,1,0:T(8,128)(2,1)S(1)}, u32[]{:S(2)}, u32[]{:S(2)}) %collective-permute-start.50) | collective-permute-done | bytes 163872 | tf_op jit(solution)/shard_map/ppermute | solution.py:747
  440.9 7.7 %collective-permute-done.51 = f32[1,1,4,1,80,128]{5,4,3,2,1,0:T(8,128)S(1)} collective-permute-done((f32[1,1,4,1,80,128]{5,4,3,2,1,0:T(8,128)S(1)}, f32[1,1,4,1,80,128]{5,4,3,2,1,0:T(8,128)S(1)}, u32[]{:S(2)}, u32[]{:S(2)}) %collective-permute-start.51) | collective-permute-done | bytes 163872 | tf_op jit(solution)/shard_map/ppermute | solution.py:747
  453.4 5.2 collective-permute-done.52
  468.8 5.2 collective-permute-done.56
  489.0 12.8 %bitcast_convert_fusion = bf16[2048,384]{1,0:T(8,128)(2,1)S(1)} fusion(bf16[4,1024,2048]{2,1,0:T(8,128)(2,1)} %get-tuple-element.42.normed, bf16[4,1024,384]{2,1,0:T(8,128)(2,1)S(1)} %copy-done.60), kind=kOutput, calls=%fused_computation.10 | convolution fusion | flops 6443237376 | bytes 21495808 | tf_op jit(solution)/shard_map/dot_general | solution.py:21
  504.6 17.0 %shard_map.272 = (bf16[4,8,128,384]{3,2,1,0:T(8,128)(2,1)}, f32[8,128]{1,0:T(8,128)}, f32[1,128]{1,0:T(1,128)}, f32[128,480]{1,0:T(8,128)}) custom-call(s32[8]{0:T(128)} %fusion.34.table, s32[4]{0:T(128)} %add_reduce_fusion.starts, f32[4,8,128,128]{3,2,1,0:T(8,128)} %get-tuple-element.56.grad, bf16[4,8,160,128]{3,2,1,0:T(8,128)(2,1)} %get-tuple-element.59.sel_grad, ...), custom_call_target="tpu_custom_call" | custom-call | tf_op jit(solution)/shard_map/pallas_call | solution.py:495
  521.7 9.9 %convolution_convert_fusion.2 = bf16[4096,1024]{1,0:T(8,128)(2,1)S(1)} fusion(bf16[4096,384]{1,0:T(8,128)(2,1)} %bitcast.195, bf16[4096,384]{1,0:T(8,128)(2,1)} %bitcast.186, bf16[2048,768]{1,0:T(8,128)(2,1)S(1)} %copy-done.22), kind=kOutput, calls=%fused_computation.4 | convolution fusion | flops 6459228160 | bytes 16252928 | tf_op jit(solution)/shard_map/dot_general | solution.py:21
  538.9 7.2 convolution_convert_fusion.1
  554.1 14.2 %convolution_convert_fusion.3 = bf16[2048,384]{1,0:T(8,128)(2,1)} fusion(bf16[4096,2048]{1,0:T(8,128)(2,1)} %bitcast.193, bf16[4096,384]{1,0:T(8,128)(2,1)} %bitcast.187), kind=kOutput, calls=%fused_computation.11 | convolution fusion | flops 6443237376 | bytes 21495808 | tf_op jit(solution)/shard_map/dot_general | solution.py:21
  570.9 5.6 add_convert_fusion.1
  581.1 5.6 add_convert_fusion
  596.8 47.5 %collective-permute-done.64 = bf16[1,2,4,1,128,1024]{5,4,3,2,1,0:T(8,128)(2,1)} collective-permute-done((bf16[1,2,4,1,128,1024]{5,4,3,2,1,0:T(8,128)(2,1)}, bf16[1,2,4,1,128,1024]{5,4,3,2,1,0:T(8,128)(2,1)}, u32[]{:S(2)}, u32[]{:S(2)}) %collective-permute-start.64) | collective-permute-done | bytes 2097184 | tf_op jit(solution)/shard_map/ppermute | solution.py:747
  696.5 5.7 collective-permute-done.67
  702.4 5.5 collective-permute-done.73
  (401 shorter events, 273.5 us)
Async XLA Ops:
  9.8 17.7 %collective-permute-start.1 = (bf16[144,2048]{1,0:T(8,128)(2,1)S(1)}, bf16[144,2048]{1,0:T(8,128)(2,1)S(1)}, u32[]{:S(2)}, u32[]{:S(2)}) collective-permute-start(bf16[144,2048]{1,0:T(8,128)(2,1)S(1)} %fusion.10.refs_0_), channel_id=1, source_target_pairs={{2,0},{3,1},{4,2},{5,3},{6,4},{7,5},{0,6},{1,7},{10,8},{11,9},{12,... | collective-permute-start | bytes 1769480 | tf_op jit(solution)/shard_map/ppermute | solution.py:747
  14.9 22.5 %collective-permute-start.15 = (bf16[144,2048]{1,0:T(8,128)(2,1)S(1)}, bf16[144,2048]{1,0:T(8,128)(2,1)}, u32[]{:S(2)}, u32[]{:S(2)}) collective-permute-start(bf16[144,2048]{1,0:T(8,128)(2,1)S(1)} %fusion.10.refs_0_), channel_id=1, source_target_pairs={{16,0},{24,8},{0,16},{8,24},{17,1},{25,9},{1,17},{9,25},{18,2},{26... | collective-permute-start | bytes 1769480 | tf_op jit(solution)/shard_map/ppermute | solution.py:747
  16.4 22.7 %collective-permute-start.7 = (bf16[144,2048]{1,0:T(8,128)(2,1)S(1)}, bf16[144,2048]{1,0:T(8,128)(2,1)}, u32[]{:S(2)}, u32[]{:S(2)}) collective-permute-start(bf16[144,2048]{1,0:T(8,128)(2,1)S(1)} %fusion.10.refs_0_), channel_id=1, source_target_pairs={{8,0},{0,8},{24,16},{16,24},{9,1},{1,9},{25,17},{17,25},{10,2},{2,... | collective-permute-start | bytes 1769480 | tf_op jit(solution)/shard_map/ppermute | solution.py:747
  17.9 21.2 %collective-permute-start = (bf16[144,2048]{1,0:T(8,128)(2,1)S(1)}, bf16[144,2048]{1,0:T(8,128)(2,1)}, u32[]{:S(2)}, u32[]{:S(2)}) collective-permute-start(bf16[144,2048]{1,0:T(8,128)(2,1)S(1)} %fusion.10.refs_0_), channel_id=1, source_target_pairs={{1,0},{0,1},{3,2},{2,3},{5,4},{4,5},{7,6},{6,7},{9,8},{8,9},{11,10... | collective-permute-start | bytes 1769480 | tf_op jit(solution)/shard_map/ppermute | solution.py:747
  27.5 18.1 %collective-permute-start.3 = (bf16[144,2048]{1,0:T(8,128)(2,1)S(1)}, bf16[144,2048]{1,0:T(8,128)(2,1)}, u32[]{:S(2)}, u32[]{:S(2)}) collective-permute-start(bf16[144,2048]{1,0:T(8,128)(2,1)S(1)} %collective-permute-done.1.refs_2_), channel_id=1, source_target_pairs={{2,0},{3,1},{4,2},{5,3},{6,4},{7,5},{0,6},{1,7},{10,8},{11,9},{12,... | collective-permute-start | bytes 1769480 | tf_op jit(solution)/shard_map/ppermute | solution.py:747
  31.8 21.1 %collective-permute-start.9 = (bf16[144,2048]{1,0:T(8,128)(2,1)S(1)}, bf16[144,2048]{1,0:T(8,128)(2,1)}, u32[]{:S(2)}, u32[]{:S(2)}) collective-permute-start(bf16[144,2048]{1,0:T(8,128)(2,1)S(1)} %collective-permute-done.1.refs_2_), channel_id=1, source_target_pairs={{8,0},{0,8},{24,16},{16,24},{9,1},{1,9},{25,17},{17,25},{10,2},{2,... | collective-permute-start | bytes 1769480 | tf_op jit(solution)/shard_map/ppermute | solution.py:747
  34.6 90.0 %all-to-all-start = ((bf16[32,205,128]{2,1,0:T(8,128)(2,1)}), bf16[32,205,128]{2,1,0:T(8,128)(2,1)S(1)}, u32[]{:S(2)}, u32[]{:S(2)}) async-start(bf16[32,205,128]{2,1,0:T(8,128)(2,1)} %pad_maximum_fusion.3), calls=%async_computation | async-start | bytes 3407872 | tf_op jit(solution)/shard_map/all_to_all | solution.py:881
  37.3 303.1 %all-gather.3.cloned.1.call-start = ((), (), s32[]{:S(2)}) async-start(), calls=%async_computation.6 | async-start | bytes 17301504 | tf_op jit(solution)/shard_map/all_gather | solution.py:974
  37.4 31.2 %collective-permute-start.17 = (bf16[144,2048]{1,0:T(8,128)(2,1)S(1)}, bf16[144,2048]{1,0:T(8,128)(2,1)S(1)}, u32[]{:S(2)}, u32[]{:S(2)}) collective-permute-start(bf16[144,2048]{1,0:T(8,128)(2,1)S(1)} %collective-permute-done.1.refs_2_), channel_id=1, source_target_pairs={{16,0},{24,8},{0,16},{8,24},{17,1},{25,9},{1,17},{9,25},{18,2},{26... | collective-permute-start | bytes 1769480 | tf_op jit(solution)/shard_map/ppermute | solution.py:747
  39.1 31.3 %collective-permute-start.2 = (bf16[144,2048]{1,0:T(8,128)(2,1)S(1)}, bf16[144,2048]{1,0:T(8,128)(2,1)S(1)}, u32[]{:S(2)}, u32[]{:S(2)}) collective-permute-start(bf16[144,2048]{1,0:T(8,128)(2,1)S(1)} %collective-permute-done.1.refs_2_), channel_id=1, source_target_pairs={{1,0},{0,1},{3,2},{2,3},{5,4},{4,5},{7,6},{6,7},{9,8},{8,9},{11,10... | collective-permute-start | bytes 1769480 | tf_op jit(solution)/shard_map/ppermute | solution.py:747
  39.1 35.8 %collective-permute-start.23 = (bf16[144,2048]{1,0:T(8,128)(2,1)}, bf16[144,2048]{1,0:T(8,128)(2,1)S(1)}, u32[]{:S(2)}, u32[]{:S(2)}) collective-permute-start(bf16[144,2048]{1,0:T(8,128)(2,1)} %collective-permute-done.15.refs_16_), channel_id=1, source_target_pairs={{8,0},{0,8},{24,16},{16,24},{9,1},{1,9},{25,17},{17,25},{10,2},{2,... | collective-permute-start | bytes 1769480 | tf_op jit(solution)/shard_map/ppermute | solution.py:747
  45.7 31.3 %collective-permute-start.16 = (bf16[144,2048]{1,0:T(8,128)(2,1)}, bf16[144,2048]{1,0:T(8,128)(2,1)S(1)}, u32[]{:S(2)}, u32[]{:S(2)}) collective-permute-start(bf16[144,2048]{1,0:T(8,128)(2,1)} %collective-permute-done.15.refs_16_), channel_id=1, source_target_pairs={{1,0},{0,1},{3,2},{2,3},{5,4},{4,5},{7,6},{6,7},{9,8},{8,9},{11,10... | collective-permute-start | bytes 1769480 | tf_op jit(solution)/shard_map/ppermute | solution.py:747
  52.9 24.1 %collective-permute-start.8 = (bf16[144,2048]{1,0:T(8,128)(2,1)}, bf16[144,2048]{1,0:T(8,128)(2,1)S(1)}, u32[]{:S(2)}, u32[]{:S(2)}) collective-permute-start(bf16[144,2048]{1,0:T(8,128)(2,1)} %collective-permute-done.7.refs_8_), channel_id=1, source_target_pairs={{1,0},{0,1},{3,2},{2,3},{5,4},{4,5},{7,6},{6,7},{9,8},{8,9},{11,10... | collective-permute-start | bytes 1769480 | tf_op jit(solution)/shard_map/ppermute | solution.py:747
  68.6 19.2 %collective-permute-start.5 = (bf16[144,2048]{1,0:T(8,128)(2,1)}, bf16[144,2048]{1,0:T(8,128)(2,1)S(1)}, u32[]{:S(2)}, u32[]{:S(2)}) collective-permute-start(bf16[144,2048]{1,0:T(8,128)(2,1)} %collective-permute-done.3.refs_4_), channel_id=1, source_target_pairs={{2,0},{3,1},{4,2},{5,3},{6,4},{7,5},{0,6},{1,7},{10,8},{11,9},{12,... | collective-permute-start | bytes 1769480 | tf_op jit(solution)/shard_map/ppermute | solution.py:747
  70.5 18.8 %collective-permute-start.19 = (bf16[144,2048]{1,0:T(8,128)(2,1)}, bf16[144,2048]{1,0:T(8,128)(2,1)S(1)}, u32[]{:S(2)}, u32[]{:S(2)}) collective-permute-start(bf16[144,2048]{1,0:T(8,128)(2,1)} %collective-permute-done.3.refs_4_), channel_id=1, source_target_pairs={{16,0},{24,8},{0,16},{8,24},{17,1},{25,9},{1,17},{9,25},{18,2},{26... | collective-permute-start | bytes 1769480 | tf_op jit(solution)/shard_map/ppermute | solution.py:747
  74.9 14.7 %collective-permute-start.11 = (bf16[144,2048]{1,0:T(8,128)(2,1)}, bf16[144,2048]{1,0:T(8,128)(2,1)S(1)}, u32[]{:S(2)}, u32[]{:S(2)}) collective-permute-start(bf16[144,2048]{1,0:T(8,128)(2,1)} %collective-permute-done.3.refs_4_), channel_id=1, source_target_pairs={{8,0},{0,8},{24,16},{16,24},{9,1},{1,9},{25,17},{17,25},{10,2},{2,... | collective-permute-start | bytes 1769480 | tf_op jit(solution)/shard_map/ppermute | solution.py:747
  77.0 22.2 %collective-permute-start.25 = (bf16[144,2048]{1,0:T(8,128)(2,1)}, bf16[144,2048]{1,0:T(8,128)(2,1)}, u32[]{:S(2)}, u32[]{:S(2)}) collective-permute-start(bf16[144,2048]{1,0:T(8,128)(2,1)} %collective-permute-done.9.refs_10_), channel_id=1, source_target_pairs={{16,0},{24,8},{0,16},{8,24},{17,1},{25,9},{1,17},{9,25},{18,2},{26... | collective-permute-start | bytes 1769480 | tf_op jit(solution)/shard_map/ppermute | solution.py:747
  89.7 16.3 %collective-permute-start.13 = (bf16[144,2048]{1,0:T(8,128)(2,1)S(1)}, bf16[144,2048]{1,0:T(8,128)(2,1)}, u32[]{:S(2)}, u32[]{:S(2)}) collective-permute-start(bf16[144,2048]{1,0:T(8,128)(2,1)S(1)} %collective-permute-done.5.refs_6_), channel_id=1, source_target_pairs={{8,0},{0,8},{24,16},{16,24},{9,1},{1,9},{25,17},{17,25},{10,2},{2,... | collective-permute-start | bytes 1769480 | tf_op jit(solution)/shard_map/ppermute | solution.py:747
  99.7 18.4 %collective-permute-start.27 = (bf16[144,2048]{1,0:T(8,128)(2,1)S(1)}, bf16[144,2048]{1,0:T(8,128)(2,1)}, u32[]{:S(2)}, u32[]{:S(2)}) collective-permute-start(bf16[144,2048]{1,0:T(8,128)(2,1)S(1)} %collective-permute-done.19.refs_20_), channel_id=1, source_target_pairs={{8,0},{0,8},{24,16},{16,24},{9,1},{1,9},{25,17},{17,25},{10,2},{2,... | collective-permute-start | bytes 1769480 | tf_op jit(solution)/shard_map/ppermute | solution.py:747
  100.9 17.1 %collective-permute-start.6 = (bf16[144,2048]{1,0:T(8,128)(2,1)S(1)}, bf16[144,2048]{1,0:T(8,128)(2,1)S(1)}, u32[]{:S(2)}, u32[]{:S(2)}) collective-permute-start(bf16[144,2048]{1,0:T(8,128)(2,1)S(1)} %collective-permute-done.5.refs_6_), channel_id=1, source_target_pairs={{1,0},{0,1},{3,2},{2,3},{5,4},{4,5},{7,6},{6,7},{9,8},{8,9},{11,10... | collective-permute-start | bytes 1769480 | tf_op jit(solution)/shard_map/ppermute | solution.py:747
  100.9 17.6 %collective-permute-start.20 = (bf16[144,2048]{1,0:T(8,128)(2,1)S(1)}, bf16[144,2048]{1,0:T(8,128)(2,1)S(1)}, u32[]{:S(2)}, u32[]{:S(2)}) collective-permute-start(bf16[144,2048]{1,0:T(8,128)(2,1)S(1)} %collective-permute-done.19.refs_20_), channel_id=1, source_target_pairs={{1,0},{0,1},{3,2},{2,3},{5,4},{4,5},{7,6},{6,7},{9,8},{8,9},{11,10... | collective-permute-start | bytes 1769480 | tf_op jit(solution)/shard_map/ppermute | solution.py:747
  240.6 63.7 %all-to-all-start.1 = ((bf16[32,64,3,128]{3,1,2,0:T(8,128)(2,1)}), bf16[32,64,3,128]{3,1,2,0:T(8,128)(2,1)S(1)}, u32[]{:S(2)}, u32[]{:S(2)}) async-start(bf16[32,64,3,128]{3,1,2,0:T(8,128)(2,1)} %copy.90), calls=%async_computation.1 | async-start | bytes 3145728 | tf_op jit(solution)/shard_map/all_to_all | solution.py:881
  243.4 476.0 %reduce-scatter.2.cloned.1.call-start = ((), (), s32[]{:S(2)}) async-start(), calls=%async_computation.5 | async-start | bytes 17301504 | tf_op jit(solution)/shard_map/reduce_scatter | solution.py:1007
  488.9 14.5 %collective-permute-start.62 = (bf16[2,2,4,1,160,128]{5,4,3,2,1,0:T(8,128)(2,1)S(1)}, bf16[2,2,4,1,160,128]{5,4,3,2,1,0:T(8,128)(2,1)S(1)}, u32[]{:S(2)}, u32[]{:S(2)}) collective-permute-start(bf16[2,2,4,1,160,128]{5,4,3,2,1,0:T(8,128)(2,1)S(1)} %maximum_maximum_fusion.1), channel_id=1, source_target_pairs={{1,0},{0,1},{3,2},{2,3},{5,4},{4,5},{7,6},{6,7},{9,8},{8,9},{11,10... | collective-permute-start | bytes 1966088 | tf_op jit(solution)/shard_map/ppermute | solution.py:747
  537.9 33.1 %collective-permute-start.63 = (bf16[2,2,4,1,128,1024]{5,4,3,2,1,0:T(8,128)(2,1)}, bf16[2,2,4,1,128,1024]{5,4,3,2,1,0:T(8,128)(2,1)}, u32[]{:S(2)}, u32[]{:S(2)}) collective-permute-start(bf16[2,2,4,1,128,1024]{5,4,3,2,1,0:T(8,128)(2,1)} %slice.319), channel_id=1, source_target_pairs={{1,0},{0,1},{3,2},{2,3},{5,4},{4,5},{7,6},{6,7},{9,8},{8,9},{11,10... | collective-permute-start | bytes 12582920 | tf_op jit(solution)/shard_map/ppermute | solution.py:747
  550.7 30.4 %collective-permute-start.69 = (bf16[2,2,4,1,128,1024]{5,4,3,2,1,0:T(8,128)(2,1)}, bf16[2,2,4,1,128,1024]{5,4,3,2,1,0:T(8,128)(2,1)}, u32[]{:S(2)}, u32[]{:S(2)}) collective-permute-start(bf16[2,2,4,1,128,1024]{5,4,3,2,1,0:T(8,128)(2,1)} %slice.330), channel_id=1, source_target_pairs={{1,0},{0,1},{3,2},{2,3},{5,4},{4,5},{7,6},{6,7},{9,8},{8,9},{11,10... | collective-permute-start | bytes 12582920 | tf_op jit(solution)/shard_map/ppermute | solution.py:747
  551.1 41.9 %all-to-all-start.3 = ((bf16[32,192,128]{2,1,0:T(8,128)(2,1)}), bf16[32,192,128]{2,1,0:T(8,128)(2,1)S(1)}, u32[]{:S(2)}, u32[]{:S(2)}) async-start(bf16[32,192,128]{2,1,0:T(8,128)(2,1)} %get-tuple-element.64), calls=%async_computation.4 | async-start | bytes 3145728 | tf_op jit(solution)/shard_map/all_to_all | solution.py:881
  579.3 65.0 %collective-permute-start.64 = (bf16[1,2,4,1,128,1024]{5,4,3,2,1,0:T(8,128)(2,1)}, bf16[1,2,4,1,128,1024]{5,4,3,2,1,0:T(8,128)(2,1)}, u32[]{:S(2)}, u32[]{:S(2)}) collective-permute-start(bf16[1,2,4,1,128,1024]{5,4,3,2,1,0:T(8,128)(2,1)} %slice.321), channel_id=1, source_target_pairs={{16,0},{24,8},{0,16},{8,24},{17,1},{25,9},{1,17},{9,25},{18,2},{26... | collective-permute-start | bytes 6291464 | tf_op jit(solution)/shard_map/ppermute | solution.py:747
  589.4 62.5 %collective-permute-start.70 = (bf16[2,1,4,1,128,1024]{5,4,3,2,1,0:T(8,128)(2,1)}, bf16[2,1,4,1,128,1024]{5,4,3,2,1,0:T(8,128)(2,1)}, u32[]{:S(2)}, u32[]{:S(2)}) collective-permute-start(bf16[2,1,4,1,128,1024]{5,4,3,2,1,0:T(8,128)(2,1)} %slice.332), channel_id=1, source_target_pairs={{8,0},{0,8},{24,16},{16,24},{9,1},{1,9},{25,17},{17,25},{10,2},{2,... | collective-permute-start | bytes 6291464 | tf_op jit(solution)/shard_map/ppermute | solution.py:747
  592.9 75.0 %all-to-all-start.2 = ((bf16[32,204,128]{2,1,0:T(8,128)(2,1)}), bf16[32,204,128]{2,1,0:T(8,128)(2,1)}, u32[]{:S(2)}, u32[]{:S(2)}) async-start(bf16[32,204,128]{2,1,0:T(8,128)(2,1)} %pad_maximum_fusion.4), calls=%async_computation.3 | async-start | bytes 3407872 | tf_op jit(solution)/shard_map/all_to_all | solution.py:881
  648.7 29.4 %collective-permute-start.65 = (bf16[1,1,4,1,128,1024]{5,4,3,2,1,0:T(8,128)(2,1)}, bf16[1,1,4,1,128,1024]{5,4,3,2,1,0:T(8,128)(2,1)}, u32[]{:S(2)}, u32[]{:S(2)}) collective-permute-start(bf16[1,1,4,1,128,1024]{5,4,3,2,1,0:T(8,128)(2,1)} %slice.323), channel_id=1, source_target_pairs={{8,0},{0,8},{24,16},{16,24},{9,1},{1,9},{25,17},{17,25},{10,2},{2,... | collective-permute-start | bytes 3145736 | tf_op jit(solution)/shard_map/ppermute | solution.py:747
  656.9 24.3 %collective-permute-start.71 = (bf16[1,1,4,1,128,1024]{5,4,3,2,1,0:T(8,128)(2,1)}, bf16[1,1,4,1,128,1024]{5,4,3,2,1,0:T(8,128)(2,1)}, u32[]{:S(2)}, u32[]{:S(2)}) collective-permute-start(bf16[1,1,4,1,128,1024]{5,4,3,2,1,0:T(8,128)(2,1)} %slice.334), channel_id=1, source_target_pairs={{16,0},{24,8},{0,16},{8,24},{17,1},{25,9},{1,17},{9,25},{18,2},{26... | collective-permute-start | bytes 3145736 | tf_op jit(solution)/shard_map/ppermute | solution.py:747
  (113 other events, 1318.2 us)
Sparse Core Ops, SparseCore 0:
  148.5 153.5 all-gather.2
  339.2 191.7 reduce-scatter.1
